TPU v7x, 512 devices: a whole 4x8x8 slice. The times are simulated.
512 devices in a mesh: pipe: 16 (over z, core), head: 32 (over y, x).
Axes of the slice: x: 4, y: 8, z: 8, core: 2. Of those that a mesh axis runs over, the one named last changes fastest.
Arguments:
- query: bfloat16 [4096, 4096], P(('pipe', 'head')), may hold values from -12 to 12
- key: bfloat16 [4096, 4096], P(('pipe', 'head')), may hold values from -6 to 6
- value: bfloat16 [4096, 4096], P(('pipe', 'head')), may hold values from -24 to 24
- stale_key: bfloat16 [2, 4096, 4096], P(None, 'pipe', 'head'), may hold values from -6 to 6
- stale_value: bfloat16 [2, 4096, 4096], P(None, 'pipe', 'head'), may hold values from -24 to 24
- patch_lengths: int32 [4], replicated, may hold values from 1 to 1536, 4096 in all
- stale_step: int32 [4], replicated, may hold values from 0 to 1
Outputs:
- attended: bfloat16 [4096, 4096], P(('pipe', 'head'))
All inputs are finite; a program needn't handle non-finite values.
Results may differ from a plain program's by a relative error of at most 0.0085.
Values may be sent and summed in bfloat16 or wider, within the bound.
No kernel may reach another device: no remote copies, remote signals or barrier semaphores. Data moves between devices by JAX's collectives and lax.ppermute only.
A program may use at most 64 MiB of HBM per device.

v0:
```python
import math

import jax
import jax.numpy as jnp
from jax import lax
from jax.sharding import PartitionSpec as P

masked_score = -1e30


def patch_index(positions, patch_lengths):
    bounds = jnp.cumsum(patch_lengths)
    return jnp.sum((positions[:, None] >= bounds[None, :]).astype(jnp.int32), axis=1)


def version_index(key_patch, stale_step):
    slots = jnp.arange(stale_step.shape[0], dtype=jnp.int32)
    picked = jnp.where(key_patch[:, None] == slots[None, :], stale_step[None, :], 0)
    return jnp.sum(picked, axis=1)


def absorb(carry, queries, keys_block, values_block, allowed):
    peak, total, summed = carry
    scale = 1.0 / math.sqrt(queries.shape[1])
    scores = jnp.dot(queries, keys_block.T, preferred_element_type=jnp.float32) * scale
    if allowed is not None:
        scores = jnp.where(allowed, scores, masked_score)
    new_peak = jnp.maximum(peak, jnp.max(scores, axis=1))
    weights = jnp.exp(scores - new_peak[:, None])
    if allowed is not None:
        weights = jnp.where(allowed, weights, 0.0)
    factor = jnp.exp(peak - new_peak)
    total = total * factor + jnp.sum(weights, axis=1)
    summed = summed * factor[:, None] + jnp.dot(
        weights.astype(jnp.bfloat16), values_block, preferred_element_type=jnp.float32
    )
    return (new_peak, total, summed)


def absorb_mixed(carry, queries, query_patch, fresh_k, fresh_v, cached_k, cached_v, key_patch):

    def only_current(state):
        return absorb(state, queries, fresh_k, fresh_v, None)

    def only_cached(state):
        return absorb(state, queries, cached_k, cached_v, None)

    def straddle(state):
        state = absorb(state, queries, fresh_k, fresh_v, key_patch[None, :] <= query_patch[:, None])
        return absorb(state, queries, cached_k, cached_v, key_patch[None, :] > query_patch[:, None])

    all_current = jnp.max(key_patch) <= jnp.min(query_patch)
    all_cached = jnp.min(key_patch) > jnp.max(query_patch)
    branch = jnp.where(all_current, 0, jnp.where(all_cached, 1, 2)).astype(jnp.int32)
    return lax.switch(branch, (only_current, only_cached, straddle), carry)


def empty_carry(count, width):
    return (
        jnp.full((count,), masked_score, jnp.float32),
        jnp.zeros((count,), jnp.float32),
        jnp.zeros((count, width), jnp.float32),
    )


def on_device(query, key, value, stale_key, stale_value, patch_lengths, stale_step):
    local_q, local_k, local_v = (
        lax.all_to_all(query, "head", split_axis=1, concat_axis=0, tiled=True),
        lax.all_to_all(key, "head", split_axis=1, concat_axis=0, tiled=True),
        lax.all_to_all(value, "head", split_axis=1, concat_axis=0, tiled=True),
    )
    rows, width = local_q.shape
    offsets = jnp.arange(rows, dtype=jnp.int32)
    span_start = lax.axis_index("pipe") * rows
    own_patch = patch_index(span_start + offsets, patch_lengths)
    older = (version_index(own_patch, stale_step) == 1)[:, None]
    cached_k = jnp.where(older, stale_key[1], stale_key[0])
    cached_v = jnp.where(older, stale_value[1], stale_value[0])
    pieces = (
        lax.all_gather(local_k, "pipe", axis=0, tiled=True),
        lax.all_gather(local_v, "pipe", axis=0, tiled=True),
        lax.all_gather(cached_k, "pipe", axis=0, tiled=True),
        lax.all_gather(cached_v, "pipe", axis=0, tiled=True),
    )
    piece_patch = patch_index(jnp.arange(pieces[0].shape[0], dtype=jnp.int32), patch_lengths)
    peak, total, summed = absorb_mixed(
        empty_carry(rows, width),
        local_q,
        own_patch,
        pieces[0],
        pieces[1],
        pieces[2],
        pieces[3],
        piece_patch,
    )
    output = (summed / total[:, None]).astype(jnp.bfloat16)
    return lax.all_to_all(output, "head", split_axis=0, concat_axis=1, tiled=True)


def solution(mesh):
    return jax.shard_map(
        on_device,
        mesh=mesh,
        in_specs=(
            P(("pipe", "head"), None),
            P(("pipe", "head"), None),
            P(("pipe", "head"), None),
            P(None, "pipe", "head"),
            P(None, "pipe", "head"),
            P(),
            P(),
        ),
        out_specs=P(("pipe", "head"), None),
        check_vma=False,
    )
```

profile of v0, /device:TPU:1, one launch (start us, length us, event | category | flops | bytes accessed | tf_op | source)
XLA Modules:
  0.0 217.1 jit_solution(14783723956120732913)
XLA Ops:
  6.5 0.8 reduce-window.8
  7.5 0.7 select_reduce_fusion
  8.2 1.7 bitcast_select_fusion
  10.0 0.7 all-gather.11.cloned.1.call-update
  10.7 19.4 %all_to_all.76 = bf16[8,32,128]{2,0,1:T(8,128)(2,1)} all-to-all(bf16[8,32,128]{2,0,1:T(8,128)(2,1)} %bitcast.45), channel_id=1, replica_groups=mesh['pipe'=16,'head'=32] {'head'}, dimensions={1} | all-to-all | bytes 131072 | tf_op jit(solution)/shard_map/all_to_all | solution.py:69
  30.2 13.4 %all_to_all.77 = bf16[8,32,128]{2,0,1:T(8,128)(2,1)} all-to-all(bf16[8,32,128]{2,0,1:T(8,128)(2,1)} %bitcast.46), channel_id=1, replica_groups=mesh['pipe'=16,'head'=32] {'head'}, dimensions={1} | all-to-all | bytes 131072 | tf_op jit(solution)/shard_map/all_to_all | solution.py:70
  43.7 3.9 %all-to-all-start = ((bf16[8,32,128]{2,0,1:T(8,128)(2,1)}), bf16[8,32,128]{2,0,1:T(8,128)(2,1)S(1)}, u32[]{:S(2)}, u32[]{:S(2)}) async-start(bf16[8,32,128]{2,0,1:T(8,128)(2,1)} %bitcast.47), calls=%async_computation | async-start | bytes 131072 | tf_op jit(solution)/shard_map/all_to_all | solution.py:68
  47.5 0.1 convert_reduce_fusion
  47.7 0.7 fusion.42
  48.4 0.7 fusion.41
  51.6 4.8 %all-to-all-done = bf16[8,32,128]{2,0,1:T(8,128)(2,1)S(1)} async-done(((bf16[8,32,128]{2,0,1:T(8,128)(2,1)}), bf16[8,32,128]{2,0,1:T(8,128)(2,1)S(1)}, u32[]{:S(2)}, u32[]{:S(2)}) %all-to-all-start) | async-done | bytes 65568 | tf_op jit(solution)/shard_map/all_to_all | solution.py:68
  56.4 1.6 all-gather.9.cloned.1.call-done
  58.0 42.2 %all-gather.11.cloned.1.call-done = bf16[4096,128]{1,0:T(8,128)(2,1)} async-done(((bf16[256,128]{1,0:T(8,128)(2,1)}), bf16[4096,128]{1,0:T(8,128)(2,1)}) %all-gather.11.cloned.1.call-update) | async-done | bytes 1048592 | tf_op jit(solution)/shard_map/all_gather | solution.py:83
  100.1 42.2 %all-gather.5.cloned.1.call-done = bf16[4096,128]{1,0:T(8,128)(2,1)} async-done(((bf16[256,128]{1,0:T(8,128)(2,1)}), bf16[4096,128]{1,0:T(8,128)(2,1)}) %all-gather.5.cloned.1.call-update) | async-done | bytes 1048592 | tf_op jit(solution)/shard_map/all_gather | solution.py:80
  142.4 42.1 %all-gather.7.cloned.1.call-done = bf16[4096,128]{1,0:T(8,128)(2,1)} async-done(((bf16[256,128]{1,0:T(8,128)(2,1)}), bf16[4096,128]{1,0:T(8,128)(2,1)}) %all-gather.7.cloned.1.call-update) | async-done | bytes 1048592 | tf_op jit(solution)/shard_map/all_gather | solution.py:81
  184.5 7.4 %conditional.1 = (f32[256]{0:T(256)S(1)}, f32[256,128]{1,0:T(8,128)S(1)}) conditional(s32[]{:T(128)} %clamp.3, (bf16[256,128]{1,0:T(8,128)(2,1)S(1)}, bf16[4096,128]{1,0:T(8,128)(2,1)}, bf16[4096,128]{1,0:T(8,128)(2,1)}) %tuple.44, (bf16[256,128]{1,0:T(8,128)(2,1)S(1)}, bf16[4096,128]{1,0:T(8,128)(2,1)}, ...), branch_computations={%region_8.11_spmd, %region_11.14_spmd, %region_14.19_spmd} | conditional | flops 1099008000 | bytes 42575972 | solution.py:55
  184.5 2.2 %fusion.45 = (f32[256]{0:T(256)S(1)}, f32[256,4096]{1,0:T(8,128)S(1)}) fusion(bf16[256,128]{1,0:T(8,128)(2,1)S(1)} %get-tuple-element.39, bf16[4096,128]{1,0:T(8,128)(2,1)} %get-tuple-element.40, s32[256]{0:T(256)S(1)} %get-tuple-element.38, s32[4096]{0:T(1024)S(1)} %get-tuple-element.37), kind=kOutput, calls=%fused_computation.57 | convolution fusion | flops 272629504 | bytes 5326848 | tf_op jit(solution)/shard_map/cond/branch_2_fun/dot_general | solution.py:25
  186.7 0.9 fusion.46
  187.6 2.0 fusion.21
  189.6 1.0 fusion.31
  190.7 0.2 copy-done.1
  190.8 1.0 fusion.34
  192.0 17.9 %all_to_all.78 = bf16[32,8,128]{2,1,0:T(8,128)(2,1)S(1)} all-to-all(bf16[32,8,128]{2,1,0:T(8,128)(2,1)S(1)} %fusion.40), channel_id=1, replica_groups=mesh['pipe'=16,'head'=32] {'head'}, dimensions={0} | all-to-all | bytes 131072 | tf_op jit(solution)/shard_map/all_to_all | solution.py:97
  209.9 0.6 copy.15
  (18 shorter events, 0.4 us)
Async XLA Ops:
  6.5 51.4 %all-gather.9.cloned.1.call-start = ((), (), s32[]{:S(2)}) async-start(), calls=%async_computation.6 | async-start | bytes 1114112 | tf_op jit(solution)/shard_map/all_gather | solution.py:82
  9.9 90.2 %all-gather.11.cloned.1.call-start = ((), (), s32[]{:S(2)}) async-start(), calls=%async_computation.7 | async-start | bytes 1114112 | tf_op jit(solution)/shard_map/all_gather | solution.py:83
  10.7 131.7 %all-gather.5.cloned.1.call-start = ((), (), s32[]{:S(2)}) async-start(), calls=%async_computation.4 | async-start | bytes 1114112 | tf_op jit(solution)/shard_map/all_gather | solution.py:80
  30.2 154.3 %all-gather.7.cloned.1.call-start = ((), (), s32[]{:S(2)}) async-start(), calls=%async_computation.5 | async-start | bytes 1114112 | tf_op jit(solution)/shard_map/all_gather | solution.py:81
  43.7 12.8 %all-to-all-start = ((bf16[8,32,128]{2,0,1:T(8,128)(2,1)}), bf16[8,32,128]{2,0,1:T(8,128)(2,1)S(1)}, u32[]{:S(2)}, u32[]{:S(2)}) async-start(bf16[8,32,128]{2,0,1:T(8,128)(2,1)} %bitcast.47), calls=%async_computation | async-start | bytes 131072 | tf_op jit(solution)/shard_map/all_to_all | solution.py:68
  184.5 2.2 %copy-start.4 = (bf16[4096,128]{1,0:T(8,128)(2,1)S(1)}, bf16[4096,128]{1,0:T(8,128)(2,1)}, u32[]{:S(2)}) copy-start(bf16[4096,128]{1,0:T(8,128)(2,1)} %get-tuple-element.41) | copy-start | bytes 3145732 | tf_op jit(solution)/shard_map/cond
  187.6 2.1 copy-start.3
  189.6 1.2 copy-start.1
Sparse Core Ops, SparseCore 0:
  10.0 47.8 all-gather.8
  60.1 39.9 all-gather.10
  102.3 40.0 all-gather.4
  144.3 40.0 all-gather.6
where the time goes:
time: 218 us; the launch traced here: 217 us
  waiting for transfers between devices  134 us (61%)
  blocking collectives  50.8 us (23%)
  between operations  15.7 us (7%)
  other arithmetic  7.04 us (3%)
  matrix products  5.15 us (2%)
  starting transfers between devices  3.99 us (2%)
    all_gather x1, waiting for transfers between devices, on_device(): lax.all_gather(local_k, 'pipe', axis=0, tiled=True)  42.2 us
    all_gather x1, waiting for transfers between devices, on_device(): lax.all_gather(cached_v, 'pipe', axis=0, tiled=True)  42.2 us
    all_gather x1, waiting for transfers between devices, on_device(): lax.all_gather(local_v, 'pipe', axis=0, tiled=True)  42.1 us
    all_to_all x1, blocking collectives, on_device(): lax.all_to_all(key, 'head', split_axis=1, concat_axis=0, tiled=True)  19.4 us
    all_to_all x1, blocking collectives, on_device(): lax.all_to_all(output, 'head', split_axis=0, concat_axis=1, tiled=True)  17.9 us
    all_to_all x1, blocking collectives, on_device(): lax.all_to_all(value, 'head', split_axis=1, concat_axis=0, tiled=True)  13.4 us
    all_to_all x1, waiting for transfers between devices, on_device(): lax.all_to_all(query, 'head', split_axis=1, concat_axis=0, tiled=True)  4.83 us
  transfers between devices with their start and end apart: 5, of which 5 were waited for; matrix products, arithmetic and copies ran while one was open for 1% of the time, Pallas kernels for 0%

commit v1 on v0

v1 whole, which is shorter than its diff:
```python
import functools
import math

import jax
import jax.numpy as jnp
from jax import lax
from jax.experimental import pallas as pl
from jax.experimental.pallas import tpu as pltpu
from jax.sharding import Mesh, PartitionSpec as P

width = 128
span = 256
patches = 4
log2_scale = math.log2(math.e) / math.sqrt(width)

quad, pair, core, head = "za", "zb", "core", ("y", "x")
pipe = (quad, pair, core)
everywhere = pipe + head

whole_vmem = pl.BlockSpec(memory_space=pltpu.VMEM)
whole_smem = pl.BlockSpec(memory_space=pltpu.SMEM)


def patch_ends(lengths):
    ends, last = [], 0
    for m in range(patches):
        last = last + lengths[m]
        ends.append(last)
    return ends


def pick_stale(lengths, steps, keys, values, out, *, first):
    ends = patch_ends(lengths)
    position = first() + lax.broadcasted_iota(jnp.int32, (span, width), 0)
    step = jnp.full((span, width), steps[0], jnp.int32)
    for m in range(1, patches):
        step = jnp.where(position >= ends[m - 1], steps[m], step)
    older = step == 1
    for at, cache in enumerate((keys, values)):
        older_rows, newer_rows = cache[1].astype(jnp.float32), cache[0].astype(jnp.float32)
        out[:, at * width : (at + 1) * width] = jnp.where(older, older_rows, newer_rows).astype(jnp.bfloat16)


def attend(lengths, queries, own, other, stale_own, stale_core, stale_pair, stale_both, out, *, place):
    za, zb, c = place()
    ends = patch_ends(lengths)
    chip = 2 * span
    lane = lax.broadcasted_iota(jnp.int32, (span, width), 1)

    own_first = za * 1024 + zb * chip
    other_first = za * 1024 + (1 - zb) * chip
    own_rows = pl.ds(pl.multiple_of(c * span, span), span)
    away_rows = pl.ds(pl.multiple_of((1 - c) * span, span), span)
    groups = (
        (own, own_rows, stale_own, own_first + c * span),
        (own, away_rows, stale_core, own_first + (1 - c) * span),
        (other, own_rows, stale_pair, other_first + c * span),
        (other, away_rows, stale_both, other_first + (1 - c) * span),
    )
    key_offset = lax.broadcasted_iota(jnp.int32, (span, span), 1)
    row_offset = lax.broadcasted_iota(jnp.int32, (span, 1), 0)

    for at in range(4):
        rows = pl.ds(at * span, span)
        q = queries[rows, :]
        position = at * 1024 + zb * chip + c * span + row_offset
        reach = jnp.full((span, 1), ends[patches - 1], jnp.int32)
        for m in range(patches - 2, -1, -1):
            reach = jnp.where(position < ends[m], ends[m], reach)
        scores, fresh_at = [], []
        for fresh, where_rows, stale, first in groups:
            fresh_scores = lax.dot_general(
                q, fresh[where_rows, width : 2 * width], (((1,), (1,)), ((), ())), preferred_element_type=jnp.float32
            )
            stale_scores = lax.dot_general(
                q, stale[:, :width], (((1,), (1,)), ((), ())), preferred_element_type=jnp.float32
            )
            is_fresh = key_offset < reach - first
            fresh_at.append(is_fresh)
            scores.append(jnp.where(is_fresh, fresh_scores, stale_scores))
        peak = functools.reduce(jnp.maximum, scores)
        peak = jnp.max(peak, axis=1, keepdims=True) * log2_scale
        peak = peak.astype(jnp.bfloat16).astype(jnp.float32)
        weights = [jnp.exp2(s * log2_scale - peak) for s in scores]
        total = jnp.sum(functools.reduce(jnp.add, weights), axis=1, keepdims=True)
        summed = jnp.zeros((span, width), jnp.float32)
        for w, is_fresh, (fresh, where_rows, stale, first) in zip(weights, fresh_at, groups):
            summed += jnp.dot(
                jnp.where(is_fresh, w, 0.0).astype(jnp.bfloat16),
                fresh[where_rows, 2 * width : 3 * width],
                preferred_element_type=jnp.float32,
            )
            summed += jnp.dot(
                jnp.where(is_fresh, 0.0, w).astype(jnp.bfloat16),
                stale[:, width:],
                preferred_element_type=jnp.float32,
            )
        high = total.astype(jnp.bfloat16).astype(jnp.float32)
        stats = jnp.where(lane == 0, peak, jnp.where(lane == 1, high, total - high))
        out[rows, :width] = (summed / total).astype(jnp.bfloat16)
        out[rows, width:] = stats.astype(jnp.bfloat16)


def combine(parts, out):
    heads = out.shape[1] // width
    blocks = parts[...].astype(jnp.float32).reshape(4, heads, 8, 2 * width)
    outputs = blocks[..., :width]
    peaks = blocks[..., width : width + 1]
    totals = blocks[..., width + 1 : width + 2] + blocks[..., width + 2 : width + 3]
    shares = totals * jnp.exp2(peaks - jnp.max(peaks, axis=0, keepdims=True))
    shares = shares / jnp.sum(shares, axis=0, keepdims=True)
    joined = jnp.sum(outputs * shares, axis=0)
    for h in range(heads):
        out[:, h * width : (h + 1) * width] = joined[h].astype(jnp.bfloat16)


def on_device(query, key, value, stale_key, stale_value, patch_lengths, stale_step):
    def place():
        return lax.axis_index(quad), lax.axis_index(pair), lax.axis_index(core)

    za, zb, c = place()
    spot = jnp.stack([za, zb, c]).astype(jnp.int32)

    def by_head(x):
        return jnp.transpose(x.reshape(8, 32, width), (1, 0, 2))

    with jax.named_scope("tokens_to_heads"):
        mine = jnp.concatenate([by_head(query), by_head(key), by_head(value)], axis=2)
        mine = jnp.broadcast_to(mine[None], (2, 32, 8, 3 * width)).reshape(64, 8, 3 * width)
        own = lax.all_to_all(mine, (core,) + head, split_axis=0, concat_axis=0, tiled=True)
        own = own.reshape(2 * span, 3 * width)

    def select(lengths, steps, spot_ref, keys, values, out):
        first = lambda: spot_ref[0] * 1024 + spot_ref[1] * 512 + spot_ref[2] * 256
        pick_stale(lengths, steps, keys, values, out, first=first)

    with jax.named_scope("stale"):
        stale_own = pl.pallas_call(
            select,
            out_shape=jax.ShapeDtypeStruct((span, 2 * width), jnp.bfloat16),
            in_specs=[whole_smem] * 3 + [whole_vmem] * 2,
            out_specs=whole_vmem,
            name="pick_stale",
        )(patch_lengths, stale_step, spot, stale_key, stale_value)
        stale_core = lax.ppermute(stale_own, core, [(0, 1), (1, 0)])
        stale_pair = lax.ppermute(stale_own, pair, [(0, 1), (1, 0)])
        stale_both = lax.ppermute(stale_own, (pair, core), [(i, 3 - i) for i in range(4)])

    with jax.named_scope("swap"):
        other = lax.ppermute(own, pair, [(0, 1), (1, 0)])

    with jax.named_scope("gather_queries"):
        local_q = lax.dynamic_slice(own, (c * span, 0), (span, width))
        queries = lax.all_gather(local_q, quad, axis=0, tiled=True)

    def attend_here(lengths, spot_ref, *refs):
        attend(lengths, *refs, place=lambda: (spot_ref[0], spot_ref[1], spot_ref[2]))

    with jax.named_scope("attend"):
        parts = pl.pallas_call(
            attend_here,
            out_shape=jax.ShapeDtypeStruct((4 * span, 2 * width), jnp.bfloat16),
            in_specs=[whole_smem] * 2 + [whole_vmem] * 7,
            out_specs=whole_vmem,
            compiler_params=pltpu.CompilerParams(vmem_limit_bytes=40 * 1024 * 1024),
            cost_estimate=pl.CostEstimate(flops=2 * 2 * 1024 * 2048 * 128, bytes_accessed=3 << 20, transcendentals=1 << 20),
            name="attend",
        )(patch_lengths, spot, queries, own, other, stale_own, stale_core, stale_pair, stale_both)

    with jax.named_scope("heads_to_tokens"):
        parts = lax.all_to_all(
            parts.reshape(128, 8, 2 * width), (quad,) + head, split_axis=0, concat_axis=0, tiled=True
        )
        return pl.pallas_call(
            combine,
            out_shape=jax.ShapeDtypeStruct((8, 32 * width), jnp.bfloat16),
            in_specs=[whole_vmem],
            out_specs=whole_vmem,
            name="combine",
        )(parts.reshape(1024, 2 * width))


def solution(mesh):
    fine = Mesh(mesh.devices.reshape(4, 2, 2, 8, 4), (quad, pair, core) + head)
    rows = P(everywhere, None)
    cache = P(None, pipe, head)
    return jax.shard_map(
        on_device,
        mesh=fine,
        in_specs=(rows, rows, rows, cache, cache, P(), P()),
        out_specs=rows,
        check_vma=False,
    )
```

time: 218 us -> 96.5 us (0.44)
  the two profiles are of different devices: /device:TPU:1 before, /device:TPU:16 now
where the time goes in v1:
time: 96.5 us; the launch traced here: 96.1 us
  blocking collectives  74.5 us (77%)
  starting transfers between devices  11.9 us (12%)
  Pallas kernels  7.95 us (8%)
  other arithmetic  1.55 us (2%)
    all_to_all x1, blocking collectives, on_device(): lax.all_to_all(parts.reshape(128, 8, 2 * width), (quad,) + head, split_ax...  27.4 us
    all_to_all x1, blocking collectives, on_device(): lax.all_to_all(mine, (core,) + head, split_axis=0, concat_axis=0, tiled=T...  24.5 us
    all_gather x1, blocking collectives, on_device(): queries = lax.all_gather(local_q, quad, axis=0, tiled=True)  22.6 us
    ppermute x1, starting transfers between devices, on_device(): other = lax.ppermute(own, pair, [(0, 1), (1, 0)])  4.27 us
    pallas_call x1, Pallas kernels, on_device(): pl.pallas_call(attend_here, out_shape=jax.ShapeDtypeStruct((4 * span, 2 *...  4.07 us
    ppermute x1, starting transfers between devices, on_device(): stale_pair = lax.ppermute(stale_own, pair, [(0, 1), (1, 0)])  3.64 us
    pallas_call x1, Pallas kernels, on_device(): pl.pallas_call(combine, out_shape=jax.ShapeDtypeStruct((8, 32 * width), j...  2.18 us
    ppermute x1, starting transfers between devices, on_device(): lax.ppermute(stale_own, (pair, core), [(i, 3 - i) for i in range(4)])  2.08 us
  transfers between devices with their start and end apart: 4, of which 0 were waited for; matrix products, arithmetic and copies ran while one was open for 1% of the time, Pallas kernels for 2%

profile of v1, /device:TPU:16, one launch (start us, length us, event | category | flops | bytes accessed | tf_op | source)
XLA Modules:
  0.0 96.1 jit_solution(3620742529606250141)
XLA Ops:
  0.0 0.9 pad_maximum_fusion
  1.0 24.5 %all_to_all.10 = bf16[64,8,384]{2,1,0:T(8,128)(2,1)S(1)} all-to-all(bf16[64,8,384]{2,1,0:T(8,128)(2,1)S(1)} %bitcast.21), channel_id=1, replica_groups=mesh['za'=4,'zb'=2,'core'=2,'y'=8,'x'=4] {'core','y','x'}, dimensions={0} | all-to-all | bytes 786432 | tf_op jit(solution)/shard_map/tokens_to_heads/all_to_all | solution.py:130
  25.4 4.3 %collective-permute-start = (bf16[512,384]{1,0:T(8,128)(2,1)S(1)}, bf16[512,384]{1,0:T(8,128)(2,1)S(1)}, u32[]{:S(2)}, u32[]{:S(2)}) collective-permute-start(bf16[512,384]{1,0:T(8,128)(2,1)S(1)} %bitcast.16), channel_id=1, source_target_pairs={{0,64},{64,0},{1,65},{65,1},{2,66},{66,2},{3,67},{67,3},{4,68},{68... | collective-permute-start | bytes 1179656 | tf_op jit(solution)/shard_map/swap/ppermute | solution.py:150
  29.7 0.6 pad_add_fusion.spot_ref
  30.3 1.7 %pick_stale.1.refs_3_ = bf16[256,256]{1,0:T(8,128)(2,1)} custom-call(s32[4]{0:T(128)} %lengths.3, s32[4]{0:T(128)} %steps.1, s32[3]{0:T(128)} %pad_add_fusion.spot_ref, bf16[2,256,128]{2,1,0:T(8,128)(2,1)} %keys.1, bf16[2,256,128]{2,1,0:T(8,128)(2,1)} %values.1), custom_call_target="tpu_custom_call" | custom-call | tf_op jit(solution)/shard_map/stale/pick_stale/pallas_call | solution.py:138
  32.1 2.1 %collective-permute-start.3 = (bf16[256,256]{1,0:T(8,128)(2,1)}, bf16[256,256]{1,0:T(8,128)(2,1)S(1)}, u32[]{:S(2)}, u32[]{:S(2)}) collective-permute-start(bf16[256,256]{1,0:T(8,128)(2,1)} %pick_stale.1.refs_3_), channel_id=1, source_target_pairs={{0,96},{32,64},{64,32},{96,0},{1,97},{33,65},{65,33},{97,1},{2,98}... | collective-permute-start | bytes 393224 | tf_op jit(solution)/shard_map/stale/ppermute | solution.py:147
  34.1 3.6 %collective-permute-start.2 = (bf16[256,256]{1,0:T(8,128)(2,1)}, bf16[256,256]{1,0:T(8,128)(2,1)S(1)}, u32[]{:S(2)}, u32[]{:S(2)}) collective-permute-start(bf16[256,256]{1,0:T(8,128)(2,1)} %pick_stale.1.refs_3_), channel_id=1, source_target_pairs={{0,64},{64,0},{1,65},{65,1},{2,66},{66,2},{3,67},{67,3},{4,68},{68... | collective-permute-start | bytes 393224 | tf_op jit(solution)/shard_map/stale/ppermute | solution.py:146
  37.8 1.9 %collective-permute-start.1 = (bf16[256,256]{1,0:T(8,128)(2,1)}, bf16[256,256]{1,0:T(8,128)(2,1)S(1)}, u32[]{:S(2)}, u32[]{:S(2)}) collective-permute-start(bf16[256,256]{1,0:T(8,128)(2,1)} %pick_stale.1.refs_3_), channel_id=1, source_target_pairs={{0,32},{32,0},{1,33},{33,1},{2,34},{34,2},{3,35},{35,3},{4,36},{36... | collective-permute-start | bytes 393224 | tf_op jit(solution)/shard_map/stale/ppermute | solution.py:145
  39.7 0.0 copy-start
  39.8 0.0 copy-start.1
  39.8 0.0 copy-start.2
  39.8 22.6 %all_gather.3.refs_0_ = bf16[1024,128]{1,0:T(8,128)(2,1)S(1)} all-gather(bf16[256,128]{1,0:T(8,128)(2,1)S(1)} %constant_dynamic-slice_fusion), channel_id=1, replica_groups=mesh['za'=4,'zb'=2,'core'=2,'y'=8,'x'=4] {'za'}, dimensions={0}, use_global_device_ids=true | all-gather | bytes 327680 | tf_op jit(solution)/shard_map/gather_queries/all_gather | solution.py:154
  62.4 0.0 collective-permute-done.3.refs_6_
  62.4 0.0 collective-permute-done.2.refs_5_
  62.4 0.0 collective-permute-done.1.refs_4_
  62.4 0.0 collective-permute-done.refs_2_
  62.4 0.0 copy-done
  62.4 0.0 copy-done.1
  62.4 0.0 copy-done.2
  62.4 4.1 %attend.1 = bf16[1024,256]{1,0:T(8,128)(2,1)S(1)} custom-call(s32[4]{0:T(128)S(1)} %copy-done.2, s32[3]{0:T(128)S(1)} %copy-done.1, bf16[1024,128]{1,0:T(8,128)(2,1)S(1)} %all_gather.3.refs_0_, bf16[512,384]{1,0:T(8,128)(2,1)S(1)} %bitcast.18, bf16[512,384]{1,0:T(8,128)(2,1)S(1)} %collective-permute-done.refs_2_, bf16[256,256]{1,0:T(8,128)(2,1)S(1)} %copy-done, ...), custom_call_target="tpu_custom_call" | custom-call | flops 1073741824 | bytes 3145728 | tf_op jit(solution)/shard_map/attend/attend/pallas_call | solution.py:160
  66.5 27.4 %all_to_all.11 = bf16[128,8,256]{2,1,0:T(8,128)(2,1)} all-to-all(bf16[128,8,256]{2,1,0:T(8,128)(2,1)S(1)} %bitcast.19), channel_id=1, replica_groups=mesh['za'=4,'zb'=2,'core'=2,'y'=8,'x'=4] {'za','y','x'}, dimensions={0} | all-to-all | bytes 1048576 | tf_op jit(solution)/shard_map/heads_to_tokens/all_to_all | solution.py:171
  93.9 2.2 %combine.1 = bf16[8,4096]{1,0:T(8,128)(2,1)} custom-call(bf16[1024,256]{1,0:T(8,128)(2,1)} %bitcast.20), custom_call_target="tpu_custom_call" | custom-call | tf_op jit(solution)/shard_map/heads_to_tokens/combine/pallas_call | solution.py:174
  (2 shorter events, 0.0 us)
Async XLA Ops:
  25.4 36.9 %collective-permute-start = (bf16[512,384]{1,0:T(8,128)(2,1)S(1)}, bf16[512,384]{1,0:T(8,128)(2,1)S(1)}, u32[]{:S(2)}, u32[]{:S(2)}) collective-permute-start(bf16[512,384]{1,0:T(8,128)(2,1)S(1)} %bitcast.16), channel_id=1, source_target_pairs={{0,64},{64,0},{1,65},{65,1},{2,66},{66,2},{3,67},{67,3},{4,68},{68... | collective-permute-start | bytes 1179656 | tf_op jit(solution)/shard_map/swap/ppermute | solution.py:150
  32.1 30.3 %collective-permute-start.3 = (bf16[256,256]{1,0:T(8,128)(2,1)}, bf16[256,256]{1,0:T(8,128)(2,1)S(1)}, u32[]{:S(2)}, u32[]{:S(2)}) collective-permute-start(bf16[256,256]{1,0:T(8,128)(2,1)} %pick_stale.1.refs_3_), channel_id=1, source_target_pairs={{0,96},{32,64},{64,32},{96,0},{1,97},{33,65},{65,33},{97,1},{2,98}... | collective-permute-start | bytes 393224 | tf_op jit(solution)/shard_map/stale/ppermute | solution.py:147
  34.1 28.2 %collective-permute-start.2 = (bf16[256,256]{1,0:T(8,128)(2,1)}, bf16[256,256]{1,0:T(8,128)(2,1)S(1)}, u32[]{:S(2)}, u32[]{:S(2)}) collective-permute-start(bf16[256,256]{1,0:T(8,128)(2,1)} %pick_stale.1.refs_3_), channel_id=1, source_target_pairs={{0,64},{64,0},{1,65},{65,1},{2,66},{66,2},{3,67},{67,3},{4,68},{68... | collective-permute-start | bytes 393224 | tf_op jit(solution)/shard_map/stale/ppermute | solution.py:146
  37.8 24.6 %collective-permute-start.1 = (bf16[256,256]{1,0:T(8,128)(2,1)}, bf16[256,256]{1,0:T(8,128)(2,1)S(1)}, u32[]{:S(2)}, u32[]{:S(2)}) collective-permute-start(bf16[256,256]{1,0:T(8,128)(2,1)} %pick_stale.1.refs_3_), channel_id=1, source_target_pairs={{0,32},{32,0},{1,33},{33,1},{2,34},{34,2},{3,35},{35,3},{4,36},{36... | collective-permute-start | bytes 393224 | tf_op jit(solution)/shard_map/stale/ppermute | solution.py:145
  39.7 22.6 %copy-start = (bf16[256,256]{1,0:T(8,128)(2,1)S(1)}, bf16[256,256]{1,0:T(8,128)(2,1)}, u32[]{:S(2)}) copy-start(bf16[256,256]{1,0:T(8,128)(2,1)} %pick_stale.1.refs_3_) | copy-start | bytes 393220
  39.8 22.6 %copy-start.1 = (s32[3]{0:T(128)S(1)}, s32[3]{0:T(128)}, u32[]{:S(2)}) copy-start(s32[3]{0:T(128)} %pad_add_fusion.spot_ref) | copy-start | bytes 40
  39.8 22.6 %copy-start.2 = (s32[4]{0:T(128)S(1)}, s32[4]{0:T(128)}, u32[]{:S(2)}) copy-start(s32[4]{0:T(128)} %lengths.3) | copy-start | bytes 52

commit v2 on v1

v2 whole, which is shorter than its diff:
```python
import functools
import math

import jax
import jax.numpy as jnp
from jax import lax
from jax.experimental import pallas as pl
from jax.experimental.pallas import tpu as pltpu
from jax.sharding import Mesh, PartitionSpec as P

width = 128
span = 256
patches = 4
log2_scale = math.log2(math.e) / math.sqrt(width)

quad, pair, core, head = "za", "zb", "core", ("y", "x")
pipe = (quad, pair, core)
everywhere = pipe + head

whole_vmem = pl.BlockSpec(memory_space=pltpu.VMEM)
whole_smem = pl.BlockSpec(memory_space=pltpu.SMEM)


def patch_ends(lengths):
    ends, last = [], 0
    for m in range(patches):
        last = last + lengths[m]
        ends.append(last)
    return ends


def pick_stale(lengths, steps, keys, values, out, *, first):
    ends = patch_ends(lengths)
    position = first + lax.broadcasted_iota(jnp.int32, (span, width), 0)
    step = jnp.full((span, width), steps[0], jnp.int32)
    for m in range(1, patches):
        step = jnp.where(position >= ends[m - 1], steps[m], step)
    older = step == 1
    for at, cache in enumerate((keys, values)):
        older_rows, newer_rows = cache[1].astype(jnp.float32), cache[0].astype(jnp.float32)
        out[:, at * width : (at + 1) * width] = jnp.where(older, older_rows, newer_rows).astype(jnp.bfloat16)


def attend(lengths, own, away, same_core, other_core, stale, out, *, place):
    za, zb, c = place()
    ends = patch_ends(lengths)
    lane = lax.broadcasted_iota(jnp.int32, (span, width), 1)
    key_offset = lax.broadcasted_iota(jnp.int32, (span, span), 1)
    row_offset = lax.broadcasted_iota(jnp.int32, (span, 1), 0)

    for queries, pair_at in ((own, zb), (away, 1 - zb)):
        q = queries[...]
        position = za * 1024 + pair_at * 512 + c * span + row_offset
        reach = jnp.full((span, 1), ends[patches - 1], jnp.int32)
        for m in range(patches - 2, -1, -1):
            reach = jnp.where(position < ends[m], ends[m], reach)
        scores, fresh_at, values = [], [], []
        for at in range(4):
            for fresh, core_at in ((same_core, c), (other_core, 1 - c)):
                first = pl.multiple_of(at * 1024 + zb * 512 + core_at * span, span)
                rows, stale_rows = pl.ds(at * span, span), pl.ds(first, span)
                fresh_scores = lax.dot_general(
                    q, fresh[rows, :width], (((1,), (1,)), ((), ())), preferred_element_type=jnp.float32
                )
                stale_scores = lax.dot_general(
                    q, stale[stale_rows, :width], (((1,), (1,)), ((), ())), preferred_element_type=jnp.float32
                )
                is_fresh = key_offset < reach - first
                fresh_at.append(is_fresh)
                scores.append(jnp.where(is_fresh, fresh_scores, stale_scores))
                values.append((fresh, rows, stale_rows))
        peak = functools.reduce(jnp.maximum, scores)
        peak = jnp.max(peak, axis=1, keepdims=True) * log2_scale
        peak = peak.astype(jnp.bfloat16).astype(jnp.float32)
        weights = [jnp.exp2(s * log2_scale - peak) for s in scores]
        total = jnp.sum(functools.reduce(jnp.add, weights), axis=1, keepdims=True)
        summed = jnp.zeros((span, width), jnp.float32)
        for w, is_fresh, (fresh, rows, stale_rows) in zip(weights, fresh_at, values):
            summed += jnp.dot(
                jnp.where(is_fresh, w, 0.0).astype(jnp.bfloat16), fresh[rows, width:], preferred_element_type=jnp.float32
            )
            summed += jnp.dot(
                jnp.where(is_fresh, 0.0, w).astype(jnp.bfloat16),
                stale[stale_rows, width:],
                preferred_element_type=jnp.float32,
            )
        high = total.astype(jnp.bfloat16).astype(jnp.float32)
        stats = jnp.where(lane == 0, peak, jnp.where(lane == 1, high, total - high))
        out_rows = pl.ds(pl.multiple_of(pair_at * span, span), span)
        out[out_rows, :width] = (summed / total).astype(jnp.bfloat16)
        out[out_rows, width:] = stats.astype(jnp.bfloat16)


def combine(parts, out):
    heads = out.shape[1] // width
    blocks = parts[...].astype(jnp.float32).reshape(2, heads, 8, 2 * width)
    outputs = blocks[..., :width]
    peaks = blocks[..., width : width + 1]
    totals = blocks[..., width + 1 : width + 2] + blocks[..., width + 2 : width + 3]
    shares = totals * jnp.exp2(peaks - jnp.max(peaks, axis=0, keepdims=True))
    shares = shares / jnp.sum(shares, axis=0, keepdims=True)
    joined = jnp.sum(outputs * shares, axis=0)
    for h in range(heads):
        out[:, h * width : (h + 1) * width] = joined[h].astype(jnp.bfloat16)


def on_device(query, key, value, stale_key, stale_value, patch_lengths, stale_step):
    def place():
        return lax.axis_index(quad), lax.axis_index(pair), lax.axis_index(core)

    def select(lengths, steps, keys, values, out):
        za, zb, c = place()
        pick_stale(lengths, steps, keys, values, out, first=za * 1024 + zb * 512 + c * span)

    with jax.named_scope("stale"):
        stale_own = pl.pallas_call(
            select,
            out_shape=jax.ShapeDtypeStruct((span, 2 * width), jnp.bfloat16),
            in_specs=[whole_smem] * 2 + [whole_vmem] * 2,
            out_specs=whole_vmem,
            name="pick_stale",
        )(patch_lengths, stale_step, stale_key, stale_value)
        stale = lax.all_gather(stale_own, pipe, axis=0, tiled=True)

    def by_head(x):
        return jnp.transpose(x.reshape(8, 32, width), (1, 0, 2))

    with jax.named_scope("tokens_to_heads"):
        mine = jnp.concatenate([by_head(query), by_head(key), by_head(value)], axis=2)
        mine = lax.all_to_all(mine, head, split_axis=0, concat_axis=0, tiled=True)
        mine = mine.reshape(span, 3 * width)
        own_q, own_kv = mine[:, :width], mine[:, width:]

    with jax.named_scope("swap_queries"):
        away_q = lax.ppermute(own_q, pair, [(0, 1), (1, 0)])

    with jax.named_scope("gather_keys"):
        same_core = lax.all_gather(own_kv, quad, axis=0, tiled=True)
        other_core = lax.ppermute(same_core, core, [(0, 1), (1, 0)])

    with jax.named_scope("attend"):
        parts = pl.pallas_call(
            functools.partial(attend, place=place),
            out_shape=jax.ShapeDtypeStruct((2 * span, 2 * width), jnp.bfloat16),
            in_specs=[whole_smem] + [whole_vmem] * 5,
            out_specs=whole_vmem,
            compiler_params=pltpu.CompilerParams(vmem_limit_bytes=40 * 1024 * 1024),
            cost_estimate=pl.CostEstimate(flops=2 * 2 * 512 * 4096 * 128, bytes_accessed=4 << 20, transcendentals=1 << 20),
            name="attend",
        )(patch_lengths, own_q, away_q, same_core, other_core, stale)

    with jax.named_scope("heads_to_tokens"):
        parts = lax.all_to_all(parts.reshape(64, 8, 2 * width), (pair,) + head, split_axis=0, concat_axis=0, tiled=True)
        return pl.pallas_call(
            combine,
            out_shape=jax.ShapeDtypeStruct((8, 32 * width), jnp.bfloat16),
            in_specs=[whole_vmem],
            out_specs=whole_vmem,
            name="combine",
        )(parts.reshape(512, 2 * width))


def solution(mesh):
    fine = Mesh(mesh.devices.reshape(4, 2, 2, 8, 4), (quad, pair, core) + head)
    rows = P(everywhere, None)
    cache = P(None, pipe, head)
    return jax.shard_map(
        on_device,
        mesh=fine,
        in_specs=(rows, rows, rows, cache, cache, P(), P()),
        out_specs=rows,
        check_vma=False,
    )
```

time: 96.5 us -> 97.8 us (1.013)
  the two profiles are of different devices: /device:TPU:16 before, /device:TPU:8 now
where the time goes in v2:
time: 97.8 us; the launch traced here: 97.5 us
  blocking collectives  65.7 us (67%)
  between operations  13.4 us (14%)
  Pallas kernels  7.46 us (8%)
  starting transfers between devices  5.38 us (6%)
  waiting for transfers between devices  2.93 us (3%)
  local copies, waits for them, and re-layouts  1.6 us (2%)
    all_gather x1, blocking collectives, on_device(): same_core = lax.all_gather(own_kv, quad, axis=0, tiled=True)  24.2 us
    all_to_all x1, blocking collectives, on_device(): mine = lax.all_to_all(mine, head, split_axis=0, concat_axis=0, tiled=True)  20.8 us
    all_to_all x1, blocking collectives, on_device(): lax.all_to_all(parts.reshape(64, 8, 2 * width), (pair,) + head, split_axi...  20.7 us
    pallas_call x1, Pallas kernels, on_device(): pl.pallas_call(functools.partial(attend, place=place), out_shape=jax.Shap...  3.86 us
    ppermute x1, starting transfers between devices, on_device(): away_q = lax.ppermute(own_q, pair, [(0, 1), (1, 0)])  3.47 us
    ppermute x1, waiting for transfers between devices, on_device(): away_q = lax.ppermute(own_q, pair, [(0, 1), (1, 0)])  2.91 us
  transfers between devices with their start and end apart: 3, of which 1 were waited for; matrix products, arithmetic and copies ran while one was open for 1% of the time, Pallas kernels for 0%

profile of v2, /device:TPU:8, one launch (start us, length us, event | category | flops | bytes accessed | tf_op | source)
XLA Modules:
  0.0 97.5 jit_solution(11630632484074325366)
XLA Ops:
  6.5 0.0 copy-start
  6.5 0.0 all-gather.2.cloned.1.call-start
  6.5 1.7 %pick_stale.1 = bf16[256,256]{1,0:T(8,128)(2,1)} custom-call(s32[4]{0:T(128)} %lengths.3, s32[4]{0:T(128)} %steps.1, bf16[2,256,128]{2,1,0:T(8,128)(2,1)} %keys.1, bf16[2,256,128]{2,1,0:T(8,128)(2,1)} %values.1), custom_call_target="tpu_custom_call" | custom-call | tf_op jit(solution)/shard_map/stale/pick_stale/pallas_call | solution.py:116
  8.3 0.0 all-gather.2.cloned.1.call-update
  8.3 0.9 pad_maximum_fusion
  9.2 20.8 %all_to_all.10 = bf16[32,8,384]{2,1,0:T(8,128)(2,1)S(1)} all-to-all(bf16[32,8,384]{2,1,0:T(8,128)(2,1)S(1)} %pad_maximum_fusion), channel_id=1, replica_groups=mesh['za'=4,'zb'=2,'core'=2,'y'=8,'x'=4] {'y','x'}, dimensions={0} | all-to-all | bytes 393216 | tf_op jit(solution)/shard_map/tokens_to_heads/all_to_all | solution.py:130
  30.1 24.2 %all_gather.6.same_core = bf16[1024,256]{1,0:T(8,128)(2,1)S(1)} all-gather(bf16[256,256]{1,0:T(8,128)(2,1)S(1)} %slice.9), channel_id=1, replica_groups=mesh['za'=4,'zb'=2,'core'=2,'y'=8,'x'=4] {'za'}, dimensions={0}, use_global_device_ids=true | all-gather | bytes 655360 | tf_op jit(solution)/shard_map/gather_keys/all_gather | solution.py:138
  54.2 1.9 %collective-permute-start.1 = (bf16[1024,256]{1,0:T(8,128)(2,1)S(1)}, bf16[1024,256]{1,0:T(8,128)(2,1)S(1)}, u32[]{:S(2)}, u32[]{:S(2)}) collective-permute-start(bf16[1024,256]{1,0:T(8,128)(2,1)S(1)} %all_gather.6.same_core), channel_id=1, source_target_pairs={{0,32},{32,0},{1,33},{33,1},{2,34},{34,2},{3,35},{35,3},{4,36},{36... | collective-permute-start | bytes 1572872 | tf_op jit(solution)/shard_map/gather_keys/ppermute | solution.py:139
  56.2 3.5 %collective-permute-start = (bf16[256,128]{1,0:T(8,128)(2,1)S(1)}, bf16[256,128]{1,0:T(8,128)(2,1)S(1)}, u32[]{:S(2)}, u32[]{:S(2)}) collective-permute-start(bf16[256,128]{1,0:T(8,128)(2,1)S(1)} %slice.8.own), channel_id=1, source_target_pairs={{0,64},{64,0},{1,65},{65,1},{2,66},{66,2},{3,67},{67,3},{4,68},{68... | collective-permute-start | bytes 196616 | tf_op jit(solution)/shard_map/swap_queries/ppermute | solution.py:135
  59.6 2.9 %collective-permute-done.away = bf16[256,128]{1,0:T(8,128)(2,1)S(1)} collective-permute-done((bf16[256,128]{1,0:T(8,128)(2,1)S(1)}, bf16[256,128]{1,0:T(8,128)(2,1)S(1)}, u32[]{:S(2)}, u32[]{:S(2)}) %collective-permute-start) | collective-permute-done | bytes 65568 | tf_op jit(solution)/shard_map/swap_queries/ppermute | solution.py:135
  62.6 0.0 collective-permute-done.1.other_core
  62.6 0.0 all-gather.2.cloned.1.call-done.stale
  62.6 0.0 copy-done
  62.6 0.0 copy-start.1
  62.6 1.6 %copy-done.1 = bf16[4096,256]{1,0:T(8,128)(2,1)S(1)} copy-done((bf16[4096,256]{1,0:T(8,128)(2,1)S(1)}, bf16[4096,256]{1,0:T(8,128)(2,1)}, u32[]{:S(2)}) %copy-start.1) | copy-done | bytes 2097176
  64.2 3.9 %attend.1 = bf16[512,256]{1,0:T(8,128)(2,1)S(1)} custom-call(s32[4]{0:T(128)S(1)} %copy-done, bf16[256,128]{1,0:T(8,128)(2,1)S(1)} %slice.8.own, bf16[256,128]{1,0:T(8,128)(2,1)S(1)} %collective-permute-done.away, bf16[1024,256]{1,0:T(8,128)(2,1)S(1)} %all_gather.6.same_core, bf16[1024,256]{1,0:T(8,128)(2,1)S(1)} %collective-permute-done.1.other_core, ...), custom_call_target="tpu_custom_call" | custom-call | flops 1073741824 | bytes 4194304 | tf_op jit(solution)/shard_map/attend/attend/pallas_call | solution.py:142
  68.0 20.7 %all_to_all.11 = bf16[64,8,256]{2,1,0:T(8,128)(2,1)} all-to-all(bf16[64,8,256]{2,1,0:T(8,128)(2,1)S(1)} %bitcast.12), channel_id=1, replica_groups=mesh['za'=4,'zb'=2,'core'=2,'y'=8,'x'=4] {'zb','y','x'}, dimensions={0} | all-to-all | bytes 524288 | tf_op jit(solution)/shard_map/heads_to_tokens/all_to_all | solution.py:153
  88.8 1.9 %combine.1 = bf16[8,4096]{1,0:T(8,128)(2,1)} custom-call(bf16[512,256]{1,0:T(8,128)(2,1)} %bitcast.13), custom_call_target="tpu_custom_call" | custom-call | tf_op jit(solution)/shard_map/heads_to_tokens/combine/pallas_call | solution.py:154
  (2 shorter events, 0.0 us)
Async XLA Ops:
  6.5 56.0 %copy-start = (s32[4]{0:T(128)S(1)}, s32[4]{0:T(128)}, u32[]{:S(2)}) copy-start(s32[4]{0:T(128)} %lengths.3) | copy-start | bytes 52
  6.5 56.0 %all-gather.2.cloned.1.call-start = ((), (), s32[]{:S(2)}) async-start(), calls=%async_computation.2 | async-start | bytes 2228224 | tf_op jit(solution)/shard_map/stale/all_gather | solution.py:123
  54.2 8.3 %collective-permute-start.1 = (bf16[1024,256]{1,0:T(8,128)(2,1)S(1)}, bf16[1024,256]{1,0:T(8,128)(2,1)S(1)}, u32[]{:S(2)}, u32[]{:S(2)}) collective-permute-start(bf16[1024,256]{1,0:T(8,128)(2,1)S(1)} %all_gather.6.same_core), channel_id=1, source_target_pairs={{0,32},{32,0},{1,33},{33,1},{2,34},{34,2},{3,35},{35,3},{4,36},{36... | collective-permute-start | bytes 1572872 | tf_op jit(solution)/shard_map/gather_keys/ppermute | solution.py:139
  56.2 6.4 %collective-permute-start = (bf16[256,128]{1,0:T(8,128)(2,1)S(1)}, bf16[256,128]{1,0:T(8,128)(2,1)S(1)}, u32[]{:S(2)}, u32[]{:S(2)}) collective-permute-start(bf16[256,128]{1,0:T(8,128)(2,1)S(1)} %slice.8.own), channel_id=1, source_target_pairs={{0,64},{64,0},{1,65},{65,1},{2,66},{66,2},{3,67},{67,3},{4,68},{68... | collective-permute-start | bytes 196616 | tf_op jit(solution)/shard_map/swap_queries/ppermute | solution.py:135
  62.6 1.6 %copy-start.1 = (bf16[4096,256]{1,0:T(8,128)(2,1)S(1)}, bf16[4096,256]{1,0:T(8,128)(2,1)}, u32[]{:S(2)}) copy-start(bf16[4096,256]{1,0:T(8,128)(2,1)} %all-gather.2.cloned.1.call-done.stale) | copy-start | bytes 6291460
Sparse Core Ops, SparseCore 0:
  9.5 49.1 all-gather.1

commit v3 on v2

--- a/solution.py
+++ b/solution.py
@@ -41,7 +41,7 @@
         out[:, at * width : (at + 1) * width] = jnp.where(older, older_rows, newer_rows).astype(jnp.bfloat16)
 
 
-def attend(lengths, own, away, same_core, other_core, stale, out, *, place):
+def attend(lengths, own, away, same_core, other_core, stale_same, stale_other, out, *, place):
     za, zb, c = place()
     ends = patch_ends(lengths)
     lane = lax.broadcasted_iota(jnp.int32, (span, width), 1)
@@ -55,10 +55,12 @@
         for m in range(patches - 2, -1, -1):
             reach = jnp.where(position < ends[m], ends[m], reach)
         scores, fresh_at, values = [], [], []
-        for at in range(4):
-            for fresh, core_at in ((same_core, c), (other_core, 1 - c)):
-                first = pl.multiple_of(at * 1024 + zb * 512 + core_at * span, span)
-                rows, stale_rows = pl.ds(at * span, span), pl.ds(first, span)
+        for ahead in range(4):
+            at = lax.rem(za + ahead, 4)
+            rows = pl.ds(pl.multiple_of(at * span, span), span)
+            stale_rows = pl.ds(ahead * span, span)
+            for fresh, stale, core_at in ((same_core, stale_same, c), (other_core, stale_other, 1 - c)):
+                first = at * 1024 + zb * 512 + core_at * span
                 fresh_scores = lax.dot_general(
                     q, fresh[rows, :width], (((1,), (1,)), ((), ())), preferred_element_type=jnp.float32
                 )
@@ -68,14 +70,14 @@
                 is_fresh = key_offset < reach - first
                 fresh_at.append(is_fresh)
                 scores.append(jnp.where(is_fresh, fresh_scores, stale_scores))
-                values.append((fresh, rows, stale_rows))
+                values.append((fresh, rows, stale, stale_rows))
         peak = functools.reduce(jnp.maximum, scores)
         peak = jnp.max(peak, axis=1, keepdims=True) * log2_scale
         peak = peak.astype(jnp.bfloat16).astype(jnp.float32)
         weights = [jnp.exp2(s * log2_scale - peak) for s in scores]
         total = jnp.sum(functools.reduce(jnp.add, weights), axis=1, keepdims=True)
         summed = jnp.zeros((span, width), jnp.float32)
-        for w, is_fresh, (fresh, rows, stale_rows) in zip(weights, fresh_at, values):
+        for w, is_fresh, (fresh, rows, stale, stale_rows) in zip(weights, fresh_at, values):
             summed += jnp.dot(
                 jnp.where(is_fresh, w, 0.0).astype(jnp.bfloat16), fresh[rows, width:], preferred_element_type=jnp.float32
             )
@@ -112,6 +114,16 @@
         za, zb, c = place()
         pick_stale(lengths, steps, keys, values, out, first=za * 1024 + zb * 512 + c * span)
 
+    swap = [(0, 1), (1, 0)]
+
+    def by_head(x):
+        return jnp.transpose(x.reshape(8, 32, width), (1, 0, 2))
+
+    with jax.named_scope("tokens_to_heads"):
+        mine = jnp.concatenate([by_head(query), by_head(key), by_head(value)], axis=2)
+        mine = lax.all_to_all(mine, head, split_axis=0, concat_axis=0, tiled=True)
+        mine = mine.reshape(span, 3 * width)
+
     with jax.named_scope("stale"):
         stale_own = pl.pallas_call(
             select,
@@ -120,34 +132,37 @@
             out_specs=whole_vmem,
             name="pick_stale",
         )(patch_lengths, stale_step, stale_key, stale_value)
-        stale = lax.all_gather(stale_own, pipe, axis=0, tiled=True)
+        stale_ahead = [
+            lax.ppermute(stale_own, quad, [(i, i - ahead) for i in range(ahead, 4)]) for ahead in (1, 2, 3)
+        ]
 
-    def by_head(x):
-        return jnp.transpose(x.reshape(8, 32, width), (1, 0, 2))
+    mine, *stale_ahead = lax.optimization_barrier((mine, *stale_ahead))
+    own_q, own_kv = mine[:, :width], mine[:, width:]
 
-    with jax.named_scope("tokens_to_heads"):
-        mine = jnp.concatenate([by_head(query), by_head(key), by_head(value)], axis=2)
-        mine = lax.all_to_all(mine, head, split_axis=0, concat_axis=0, tiled=True)
-        mine = mine.reshape(span, 3 * width)
-        own_q, own_kv = mine[:, :width], mine[:, width:]
+    with jax.named_scope("stale"):
+        stale_same = jnp.concatenate([stale_own, *stale_ahead], axis=0)
+        stale_other = lax.ppermute(stale_same, core, swap)
 
     with jax.named_scope("swap_queries"):
-        away_q = lax.ppermute(own_q, pair, [(0, 1), (1, 0)])
+        away_q = lax.ppermute(own_q, pair, swap)
 
     with jax.named_scope("gather_keys"):
-        same_core = lax.all_gather(own_kv, quad, axis=0, tiled=True)
-        other_core = lax.ppermute(same_core, core, [(0, 1), (1, 0)])
+        same_core = jnp.broadcast_to(own_kv[None], (4, span, 2 * width))
+        same_core = lax.all_to_all(same_core, quad, split_axis=0, concat_axis=0, tiled=True)
+        same_core, stale_other, away_q = lax.optimization_barrier((same_core, stale_other, away_q))
+        same_core = same_core.reshape(4 * span, 2 * width)
+        other_core = lax.ppermute(same_core, core, swap)
 
     with jax.named_scope("attend"):
         parts = pl.pallas_call(
             functools.partial(attend, place=place),
             out_shape=jax.ShapeDtypeStruct((2 * span, 2 * width), jnp.bfloat16),
-            in_specs=[whole_smem] + [whole_vmem] * 5,
+            in_specs=[whole_smem] + [whole_vmem] * 6,
             out_specs=whole_vmem,
             compiler_params=pltpu.CompilerParams(vmem_limit_bytes=40 * 1024 * 1024),
             cost_estimate=pl.CostEstimate(flops=2 * 2 * 512 * 4096 * 128, bytes_accessed=4 << 20, transcendentals=1 << 20),
             name="attend",
-        )(patch_lengths, own_q, away_q, same_core, other_core, stale)
+        )(patch_lengths, own_q, away_q, same_core, other_core, stale_same, stale_other)
 
     with jax.named_scope("heads_to_tokens"):
         parts = lax.all_to_all(parts.reshape(64, 8, 2 * width), (pair,) + head, split_axis=0, concat_axis=0, tiled=True)

time: 97.8 us -> 91.4 us (0.935)
  blocking collectives: 65.7 us -> 24.6 us
  starting transfers between devices: 5.38 us -> 29.6 us
  waiting for transfers between devices: 2.93 us -> 26.7 us
  between operations: 13.4 us -> 0.1 us
    all_gather x1 -> x0, blocking collectives: 24.2 us -> none  [on_device(): same_core = lax.all_gather(own_kv, quad, axis=0, tiled=True)]
    ppermute x2 -> x6, waiting for transfers between devices: 2.91 us -> 24.6 us  [the longest x3 13.3 us: on_device(): lax.ppermute(stale_own, quad, [(i, i - ahead) for i in range(ahead, 4)])]
    all_to_all x1 -> x0, blocking collectives: 20.8 us -> none  [on_device(): mine = lax.all_to_all(mine, head, split_axis=0, concat_axis=0, tiled=True)]
    all_to_all x0 -> x2, starting transfers between devices: none -> 18.2 us  [the longest x1 10.2 us: on_device(): mine = lax.all_to_all(mine, head, split_axis=0, concat_axis=0, tiled=True)]
    ppermute x2 -> x6, starting transfers between devices: 5.38 us -> 11.4 us  [the longest x3 3.86 us: on_device(): lax.ppermute(stale_own, quad, [(i, i - ahead) for i in range(ahead, 4)])]
    all_to_all x1, blocking collectives: 20.7 us -> 24.6 us  [on_device(): lax.all_to_all(parts.reshape(64, 8, 2 * width), (pair,) + head, split_axi...]
    all_to_all x0 -> x2, waiting for transfers between devices: none -> 2.1 us  [the longest x1 2.09 us: on_device(): lax.all_to_all(same_core, quad, split_axis=0, concat_axis=0, tiled=True)]
    unnamed x4, local copies, waits for them, and re-layouts: 1.59 us -> 0.01 us
  transfers between devices with their start and end apart: 3 -> 8, of which waited for: 1 -> 4; matrix products, arithmetic and copies ran while one was open for 1% -> 0% of each run, Pallas kernels for 0% -> 2%
where the time goes in v3:
time: 91.4 us; the launch traced here: 90.9 us
  starting transfers between devices  29.6 us (32%)
  waiting for transfers between devices  26.7 us (29%)
  blocking collectives  24.6 us (27%)
  Pallas kernels  7.39 us (8%)
  other arithmetic  1.64 us (2%)
    all_to_all x1, blocking collectives, on_device(): lax.all_to_all(parts.reshape(64, 8, 2 * width), (pair,) + head, split_axi...  24.6 us
    ppermute x3, waiting for transfers between devices, on_device(): lax.ppermute(stale_own, quad, [(i, i - ahead) for i in range(ahead, 4)])  13.3 us
    all_to_all x1, starting transfers between devices, on_device(): mine = lax.all_to_all(mine, head, split_axis=0, concat_axis=0, tiled=True)  10.2 us
    ppermute x1, waiting for transfers between devices, on_device(): away_q = lax.ppermute(own_q, pair, swap)  9.48 us
    all_to_all x1, starting transfers between devices, on_device(): lax.all_to_all(same_core, quad, split_axis=0, concat_axis=0, tiled=True)  8.01 us
    ppermute x3, starting transfers between devices, on_device(): lax.ppermute(stale_own, quad, [(i, i - ahead) for i in range(ahead, 4)])  3.86 us
    pallas_call x1, Pallas kernels, on_device(): pl.pallas_call(functools.partial(attend, place=place), out_shape=jax.Shap...  3.81 us
    ppermute x1, starting transfers between devices, on_device(): away_q = lax.ppermute(own_q, pair, swap)  3.7 us
  transfers between devices with their start and end apart: 8, of which 4 were waited for; matrix products, arithmetic and copies ran while one was open for 0% of the time, Pallas kernels for 2%

profile of v3, /device:TPU:8, one launch (start us, length us, event | category | flops | bytes accessed | tf_op | source)
XLA Modules:
  0.0 90.9 jit_solution(1162697715409726313)
XLA Ops:
  0.0 1.6 %pad_maximum_fusion.1 = bf16[32,8,384]{2,1,0:T(8,128)(2,1)} fusion(bf16[32,8,128]{2,1,0:T(8,128)(2,1)} %bitcast.19, bf16[32,8,128]{2,1,0:T(8,128)(2,1)} %bitcast.20, bf16[32,8,128]{2,1,0:T(8,128)(2,1)} %bitcast.21), kind=kLoop, calls=%fused_computation.1 | loop fusion | flops 589824 | bytes 393216 | tf_op jit(solution)/shard_map/tokens_to_heads/concatenate | solution.py:123
  1.6 10.2 %all-to-all-start = ((bf16[32,8,384]{2,1,0:T(8,128)(2,1)}), bf16[32,8,384]{2,1,0:T(8,128)(2,1)S(1)}, u32[]{:S(2)}, u32[]{:S(2)}) async-start(bf16[32,8,384]{2,1,0:T(8,128)(2,1)} %pad_maximum_fusion.1), calls=%async_computation | async-start | bytes 393216 | tf_op jit(solution)/shard_map/tokens_to_heads/all_to_all | solution.py:124
  11.8 1.7 %pick_stale.1 = bf16[256,256]{1,0:T(8,128)(2,1)} custom-call(s32[4]{0:T(128)} %lengths.3, s32[4]{0:T(128)} %steps.1, bf16[2,256,128]{2,1,0:T(8,128)(2,1)} %keys.1, bf16[2,256,128]{2,1,0:T(8,128)(2,1)} %values.1), custom_call_target="tpu_custom_call" | custom-call | tf_op jit(solution)/shard_map/stale/pick_stale/pallas_call | solution.py:128
  13.5 1.3 %collective-permute-start.2 = (bf16[256,256]{1,0:T(8,128)(2,1)}, bf16[256,256]{1,0:T(8,128)(2,1)S(1)}, u32[]{:S(2)}, u32[]{:S(2)}) collective-permute-start(bf16[256,256]{1,0:T(8,128)(2,1)} %pick_stale.1), channel_id=1, source_target_pairs={{384,0},{385,1},{386,2},{387,3},{388,4},{389,5},{390,6},{391,7},{3... | collective-permute-start | bytes 393224 | tf_op jit(solution)/shard_map/stale/ppermute | solution.py:136
  14.8 1.3 %collective-permute-start.1 = (bf16[256,256]{1,0:T(8,128)(2,1)}, bf16[256,256]{1,0:T(8,128)(2,1)S(1)}, u32[]{:S(2)}, u32[]{:S(2)}) collective-permute-start(bf16[256,256]{1,0:T(8,128)(2,1)} %pick_stale.1), channel_id=1, source_target_pairs={{256,0},{384,128},{257,1},{385,129},{258,2},{386,130},{259,3},{387... | collective-permute-start | bytes 393224 | tf_op jit(solution)/shard_map/stale/ppermute | solution.py:136
  16.1 1.3 %collective-permute-start = (bf16[256,256]{1,0:T(8,128)(2,1)}, bf16[256,256]{1,0:T(8,128)(2,1)S(1)}, u32[]{:S(2)}, u32[]{:S(2)}) collective-permute-start(bf16[256,256]{1,0:T(8,128)(2,1)} %pick_stale.1), channel_id=1, source_target_pairs={{128,0},{256,128},{384,256},{129,1},{257,129},{385,257},{130,2},{2... | collective-permute-start | bytes 393224 | tf_op jit(solution)/shard_map/stale/ppermute | solution.py:136
  17.4 13.3 %collective-permute-done.2 = bf16[256,256]{1,0:T(8,128)(2,1)S(1)} collective-permute-done((bf16[256,256]{1,0:T(8,128)(2,1)}, bf16[256,256]{1,0:T(8,128)(2,1)S(1)}, u32[]{:S(2)}, u32[]{:S(2)}) %collective-permute-start.2) | collective-permute-done | bytes 131104 | tf_op jit(solution)/shard_map/stale/ppermute | solution.py:136
  30.6 0.0 collective-permute-done.1
  30.7 0.0 collective-permute-done
  30.7 0.0 all-to-all-done
  30.7 0.8 broadcast_in_dim.2
  31.5 8.0 %all-to-all-start.1 = ((bf16[4,256,256]{2,1,0:T(8,128)(2,1)}), bf16[4,256,256]{2,1,0:T(8,128)(2,1)S(1)}, u32[]{:S(2)}, u32[]{:S(2)}) async-start(bf16[4,256,256]{2,1,0:T(8,128)(2,1)} %broadcast_in_dim.2), calls=%async_computation.1 | async-start | bytes 1048576 | tf_op jit(solution)/shard_map/gather_keys/all_to_all | solution.py:151
  39.5 0.0 copy-done.1
  39.6 1.9 %collective-permute-start.3 = (bf16[1024,256]{1,0:T(8,128)(2,1)S(1)}, bf16[1024,256]{1,0:T(8,128)(2,1)S(1)}, u32[]{:S(2)}, u32[]{:S(2)}) collective-permute-start(bf16[1024,256]{1,0:T(8,128)(2,1)S(1)} %pad_maximum_fusion.stale_same), channel_id=1, source_target_pairs={{0,32},{32,0},{1,33},{33,1},{2,34},{34,2},{3,35},{35,3},{4,36},{36... | collective-permute-start | bytes 1572872 | tf_op jit(solution)/shard_map/stale/ppermute | solution.py:144
  41.5 0.0 copy-start
  41.5 3.7 %collective-permute-start.4 = (bf16[256,128]{1,0:T(8,128)(2,1)S(1)}, bf16[256,128]{1,0:T(8,128)(2,1)S(1)}, u32[]{:S(2)}, u32[]{:S(2)}) collective-permute-start(bf16[256,128]{1,0:T(8,128)(2,1)S(1)} %slice.6.own), channel_id=1, source_target_pairs={{0,64},{64,0},{1,65},{65,1},{2,66},{66,2},{3,67},{67,3},{4,68},{68... | collective-permute-start | bytes 196616 | tf_op jit(solution)/shard_map/swap_queries/ppermute | solution.py:147
  45.2 9.5 %collective-permute-done.4.away = bf16[256,128]{1,0:T(8,128)(2,1)S(1)} collective-permute-done((bf16[256,128]{1,0:T(8,128)(2,1)S(1)}, bf16[256,128]{1,0:T(8,128)(2,1)S(1)}, u32[]{:S(2)}, u32[]{:S(2)}) %collective-permute-start.4) | collective-permute-done | bytes 65568 | tf_op jit(solution)/shard_map/swap_queries/ppermute | solution.py:147
  54.7 0.0 collective-permute-done.3.stale_other
  54.7 2.1 %all-to-all-done.1 = bf16[4,256,256]{2,1,0:T(8,128)(2,1)S(1)} async-done(((bf16[4,256,256]{2,1,0:T(8,128)(2,1)}), bf16[4,256,256]{2,1,0:T(8,128)(2,1)S(1)}, u32[]{:S(2)}, u32[]{:S(2)}) %all-to-all-start.1) | async-done | bytes 524320 | tf_op jit(solution)/shard_map/gather_keys/all_to_all | solution.py:151
  56.8 1.9 %collective-permute-start.5 = (bf16[1024,256]{1,0:T(8,128)(2,1)S(1)}, bf16[1024,256]{1,0:T(8,128)(2,1)S(1)}, u32[]{:S(2)}, u32[]{:S(2)}) collective-permute-start(bf16[1024,256]{1,0:T(8,128)(2,1)S(1)} %bitcast.13), channel_id=1, source_target_pairs={{0,32},{32,0},{1,33},{33,1},{2,34},{34,2},{3,35},{35,3},{4,36},{36... | collective-permute-start | bytes 1572872 | tf_op jit(solution)/shard_map/gather_keys/ppermute | solution.py:154
  58.7 1.9 %collective-permute-done.5.other_core = bf16[1024,256]{1,0:T(8,128)(2,1)S(1)} collective-permute-done((bf16[1024,256]{1,0:T(8,128)(2,1)S(1)}, bf16[1024,256]{1,0:T(8,128)(2,1)S(1)}, u32[]{:S(2)}, u32[]{:S(2)}) %collective-permute-start.5) | collective-permute-done | bytes 524320 | tf_op jit(solution)/shard_map/gather_keys/ppermute | solution.py:154
  60.6 3.8 %attend.1 = bf16[512,256]{1,0:T(8,128)(2,1)S(1)} custom-call(s32[4]{0:T(128)S(1)} %copy-done, bf16[256,128]{1,0:T(8,128)(2,1)S(1)} %slice.6.own, bf16[256,128]{1,0:T(8,128)(2,1)S(1)} %collective-permute-done.4.away, bf16[1024,256]{1,0:T(8,128)(2,1)S(1)} %bitcast.14, bf16[1024,256]{1,0:T(8,128)(2,1)S(1)} %collective-permute-done.5.other_core, ...), custom_call_target="tpu_custom_call" | custom-call | flops 1073741824 | bytes 4194304 | tf_op jit(solution)/shard_map/attend/attend/pallas_call | solution.py:157
  64.4 24.6 %all_to_all.15 = bf16[64,8,256]{2,1,0:T(8,128)(2,1)} all-to-all(bf16[64,8,256]{2,1,0:T(8,128)(2,1)S(1)} %bitcast.15), channel_id=1, replica_groups=mesh['za'=4,'zb'=2,'core'=2,'y'=8,'x'=4] {'zb','y','x'}, dimensions={0} | all-to-all | bytes 524288 | tf_op jit(solution)/shard_map/heads_to_tokens/all_to_all | solution.py:168
  89.0 1.9 %combine.1 = bf16[8,4096]{1,0:T(8,128)(2,1)} custom-call(bf16[512,256]{1,0:T(8,128)(2,1)} %bitcast.16), custom_call_target="tpu_custom_call" | custom-call | tf_op jit(solution)/shard_map/heads_to_tokens/combine/pallas_call | solution.py:169
  (5 shorter events, 0.1 us)
Async XLA Ops:
  1.6 29.0 %all-to-all-start = ((bf16[32,8,384]{2,1,0:T(8,128)(2,1)}), bf16[32,8,384]{2,1,0:T(8,128)(2,1)S(1)}, u32[]{:S(2)}, u32[]{:S(2)}) async-start(bf16[32,8,384]{2,1,0:T(8,128)(2,1)} %pad_maximum_fusion.1), calls=%async_computation | async-start | bytes 393216 | tf_op jit(solution)/shard_map/tokens_to_heads/all_to_all | solution.py:124
  13.5 17.2 %collective-permute-start.2 = (bf16[256,256]{1,0:T(8,128)(2,1)}, bf16[256,256]{1,0:T(8,128)(2,1)S(1)}, u32[]{:S(2)}, u32[]{:S(2)}) collective-permute-start(bf16[256,256]{1,0:T(8,128)(2,1)} %pick_stale.1), channel_id=1, source_target_pairs={{384,0},{385,1},{386,2},{387,3},{388,4},{389,5},{390,6},{391,7},{3... | collective-permute-start | bytes 393224 | tf_op jit(solution)/shard_map/stale/ppermute | solution.py:136
  14.8 15.9 %collective-permute-start.1 = (bf16[256,256]{1,0:T(8,128)(2,1)}, bf16[256,256]{1,0:T(8,128)(2,1)S(1)}, u32[]{:S(2)}, u32[]{:S(2)}) collective-permute-start(bf16[256,256]{1,0:T(8,128)(2,1)} %pick_stale.1), channel_id=1, source_target_pairs={{256,0},{384,128},{257,1},{385,129},{258,2},{386,130},{259,3},{387... | collective-permute-start | bytes 393224 | tf_op jit(solution)/shard_map/stale/ppermute | solution.py:136
  16.1 14.6 %collective-permute-start = (bf16[256,256]{1,0:T(8,128)(2,1)}, bf16[256,256]{1,0:T(8,128)(2,1)S(1)}, u32[]{:S(2)}, u32[]{:S(2)}) collective-permute-start(bf16[256,256]{1,0:T(8,128)(2,1)} %pick_stale.1), channel_id=1, source_target_pairs={{128,0},{256,128},{384,256},{129,1},{257,129},{385,257},{130,2},{2... | collective-permute-start | bytes 393224 | tf_op jit(solution)/shard_map/stale/ppermute | solution.py:136
  31.5 8.0 %copy-start.1 = (bf16[256,256]{1,0:T(8,128)(2,1)S(1)}, bf16[256,256]{1,0:T(8,128)(2,1)}, u32[]{:S(2)}) copy-start(bf16[256,256]{1,0:T(8,128)(2,1)} %pick_stale.1) | copy-start | bytes 393220
  31.5 25.3 %all-to-all-start.1 = ((bf16[4,256,256]{2,1,0:T(8,128)(2,1)}), bf16[4,256,256]{2,1,0:T(8,128)(2,1)S(1)}, u32[]{:S(2)}, u32[]{:S(2)}) async-start(bf16[4,256,256]{2,1,0:T(8,128)(2,1)} %broadcast_in_dim.2), calls=%async_computation.1 | async-start | bytes 1048576 | tf_op jit(solution)/shard_map/gather_keys/all_to_all | solution.py:151
  39.6 15.1 %collective-permute-start.3 = (bf16[1024,256]{1,0:T(8,128)(2,1)S(1)}, bf16[1024,256]{1,0:T(8,128)(2,1)S(1)}, u32[]{:S(2)}, u32[]{:S(2)}) collective-permute-start(bf16[1024,256]{1,0:T(8,128)(2,1)S(1)} %pad_maximum_fusion.stale_same), channel_id=1, source_target_pairs={{0,32},{32,0},{1,33},{33,1},{2,34},{34,2},{3,35},{35,3},{4,36},{36... | collective-permute-start | bytes 1572872 | tf_op jit(solution)/shard_map/stale/ppermute | solution.py:144
  41.5 19.1 %copy-start = (s32[4]{0:T(128)S(1)}, s32[4]{0:T(128)}, u32[]{:S(2)}) copy-start(s32[4]{0:T(128)} %lengths.3) | copy-start | bytes 52
  41.5 13.2 %collective-permute-start.4 = (bf16[256,128]{1,0:T(8,128)(2,1)S(1)}, bf16[256,128]{1,0:T(8,128)(2,1)S(1)}, u32[]{:S(2)}, u32[]{:S(2)}) collective-permute-start(bf16[256,128]{1,0:T(8,128)(2,1)S(1)} %slice.6.own), channel_id=1, source_target_pairs={{0,64},{64,0},{1,65},{65,1},{2,66},{66,2},{3,67},{67,3},{4,68},{68... | collective-permute-start | bytes 196616 | tf_op jit(solution)/shard_map/swap_queries/ppermute | solution.py:147
  56.8 3.8 %collective-permute-start.5 = (bf16[1024,256]{1,0:T(8,128)(2,1)S(1)}, bf16[1024,256]{1,0:T(8,128)(2,1)S(1)}, u32[]{:S(2)}, u32[]{:S(2)}) collective-permute-start(bf16[1024,256]{1,0:T(8,128)(2,1)S(1)} %bitcast.13), channel_id=1, source_target_pairs={{0,32},{32,0},{1,33},{33,1},{2,34},{34,2},{3,35},{35,3},{4,36},{36... | collective-permute-start | bytes 1572872 | tf_op jit(solution)/shard_map/gather_keys/ppermute | solution.py:154

commit v4 on v3

v4 whole, which is shorter than its diff:
```python
import functools
import math

import jax
import jax.numpy as jnp
from jax import lax
from jax.experimental import pallas as pl
from jax.experimental.pallas import tpu as pltpu
from jax.sharding import Mesh, PartitionSpec as P

width = 128
span = 256
patches = 4
log2_scale = math.log2(math.e) / math.sqrt(width)

quad, pair, core, head = "za", "zb", "core", ("y", "x")
pipe = (quad, pair, core)
everywhere = pipe + head

whole_vmem = pl.BlockSpec(memory_space=pltpu.VMEM)
whole_smem = pl.BlockSpec(memory_space=pltpu.SMEM)


def patch_ends(lengths):
    ends, last = [], 0
    for m in range(patches):
        last = last + lengths[m]
        ends.append(last)
    return ends


def pick_stale(lengths, steps, keys, values, out, *, first):
    ends = patch_ends(lengths)
    position = first + lax.broadcasted_iota(jnp.int32, (span, width), 0)
    step = jnp.full((span, width), steps[0], jnp.int32)
    for m in range(1, patches):
        step = jnp.where(position >= ends[m - 1], steps[m], step)
    older = step == 1
    for at, cache in enumerate((keys, values)):
        older_rows, newer_rows = cache[1].astype(jnp.float32), cache[0].astype(jnp.float32)
        out[:, at * width : (at + 1) * width] = jnp.where(older, older_rows, newer_rows).astype(jnp.bfloat16)


def attend(lengths, queries, own, *refs, place):
    fresh_refs, stale_refs, out = refs[:3], refs[3:7], refs[7]
    za, zb, c = place()
    ends = patch_ends(lengths)
    lane = lax.broadcasted_iota(jnp.int32, (span, width), 1)
    key_offset = lax.broadcasted_iota(jnp.int32, (span, span), 1)
    row_offset = lax.broadcasted_iota(jnp.int32, (span, 1), 0)

    blocks = []
    for at, (pair_at, core_at) in enumerate(((zb, c), (zb, 1 - c), (1 - zb, c), (1 - zb, 1 - c))):
        if at == 0:
            keys, values = own[:, width : 2 * width], own[:, 2 * width :]
        else:
            keys, values = fresh_refs[at - 1][:, :width], fresh_refs[at - 1][:, width:]
        stale_keys, stale_values = stale_refs[at][:, :width], stale_refs[at][:, width:]
        blocks.append((keys, values, stale_keys, stale_values, za * 1024 + pair_at * 512 + core_at * span))

    for at in range(4):
        rows = pl.ds(at * span, span)
        q = queries[rows, :]
        position = at * 1024 + zb * 512 + c * span + row_offset
        reach = jnp.full((span, 1), ends[patches - 1], jnp.int32)
        for m in range(patches - 2, -1, -1):
            reach = jnp.where(position < ends[m], ends[m], reach)
        scores, fresh_at = [], []
        for keys, _, stale_keys, _, first in blocks:
            fresh_scores = lax.dot_general(q, keys, (((1,), (1,)), ((), ())), preferred_element_type=jnp.float32)
            stale_scores = lax.dot_general(q, stale_keys, (((1,), (1,)), ((), ())), preferred_element_type=jnp.float32)
            is_fresh = key_offset < reach - first
            fresh_at.append(is_fresh)
            scores.append(jnp.where(is_fresh, fresh_scores, stale_scores))
        peak = functools.reduce(jnp.maximum, scores)
        peak = jnp.max(peak, axis=1, keepdims=True) * log2_scale
        peak = peak.astype(jnp.bfloat16).astype(jnp.float32)
        weights = [jnp.exp2(s * log2_scale - peak) for s in scores]
        total = jnp.sum(functools.reduce(jnp.add, weights), axis=1, keepdims=True)
        summed = jnp.zeros((span, width), jnp.float32)
        for w, is_fresh, (_, values, _, stale_values, _) in zip(weights, fresh_at, blocks):
            summed += jnp.dot(
                jnp.where(is_fresh, w, 0.0).astype(jnp.bfloat16), values, preferred_element_type=jnp.float32
            )
            summed += jnp.dot(
                jnp.where(is_fresh, 0.0, w).astype(jnp.bfloat16), stale_values, preferred_element_type=jnp.float32
            )
        high = total.astype(jnp.bfloat16).astype(jnp.float32)
        stats = jnp.where(lane == 0, peak, jnp.where(lane == 1, high, total - high))
        out[rows, :width] = (summed / total).astype(jnp.bfloat16)
        out[rows, width:] = stats.astype(jnp.bfloat16)


def combine(parts, out):
    heads = out.shape[1] // width
    blocks = parts[...].astype(jnp.float32).reshape(4, heads, 8, 2 * width)
    outputs = blocks[..., :width]
    peaks = blocks[..., width : width + 1]
    totals = blocks[..., width + 1 : width + 2] + blocks[..., width + 2 : width + 3]
    shares = totals * jnp.exp2(peaks - jnp.max(peaks, axis=0, keepdims=True))
    shares = shares / jnp.sum(shares, axis=0, keepdims=True)
    joined = jnp.sum(outputs * shares, axis=0)
    for h in range(heads):
        out[:, h * width : (h + 1) * width] = joined[h].astype(jnp.bfloat16)


def on_device(query, key, value, stale_key, stale_value, patch_lengths, stale_step):
    def place():
        return lax.axis_index(quad), lax.axis_index(pair), lax.axis_index(core)

    def select(lengths, steps, keys, values, out):
        za, zb, c = place()
        pick_stale(lengths, steps, keys, values, out, first=za * 1024 + zb * 512 + c * span)

    swap = [(0, 1), (1, 0)]

    def from_neighbours(x):
        return (
            lax.ppermute(x, core, swap),
            lax.ppermute(x, pair, swap),
            lax.ppermute(x, (pair, core), [(i, 3 - i) for i in range(4)]),
        )

    def by_head(x):
        return jnp.transpose(x.reshape(8, 32, width), (1, 0, 2))

    with jax.named_scope("tokens_to_heads"):
        mine = jnp.concatenate([by_head(query), by_head(key), by_head(value)], axis=2)
        mine = lax.all_to_all(mine, head, split_axis=0, concat_axis=0, tiled=True)
        mine = mine.reshape(span, 3 * width)

    with jax.named_scope("stale"):
        stale_own = pl.pallas_call(
            select,
            out_shape=jax.ShapeDtypeStruct((span, 2 * width), jnp.bfloat16),
            in_specs=[whole_smem] * 2 + [whole_vmem] * 2,
            out_specs=whole_vmem,
            name="pick_stale",
        )(patch_lengths, stale_step, stale_key, stale_value)
        stale = from_neighbours(stale_own)

    mine, *stale = lax.optimization_barrier((mine, *stale))

    with jax.named_scope("gather_queries"):
        queries = jnp.broadcast_to(mine[None, :, :width], (4, span, width))
        queries = lax.all_to_all(queries, quad, split_axis=0, concat_axis=0, tiled=True)
        queries = queries.reshape(4 * span, width)

    with jax.named_scope("neighbour_keys"):
        fresh = from_neighbours(mine[:, width:])

    with jax.named_scope("attend"):
        parts = pl.pallas_call(
            functools.partial(attend, place=place),
            out_shape=jax.ShapeDtypeStruct((4 * span, 2 * width), jnp.bfloat16),
            in_specs=[whole_smem] + [whole_vmem] * 9,
            out_specs=whole_vmem,
            compiler_params=pltpu.CompilerParams(vmem_limit_bytes=40 * 1024 * 1024),
            cost_estimate=pl.CostEstimate(flops=2 * 2 * 512 * 4096 * 128, bytes_accessed=4 << 20, transcendentals=1 << 20),
            name="attend",
        )(patch_lengths, queries, mine, *fresh, stale_own, *stale)

    with jax.named_scope("heads_to_tokens"):
        parts = lax.all_to_all(parts.reshape(128, 8, 2 * width), (quad,) + head, split_axis=0, concat_axis=0, tiled=True)
        return pl.pallas_call(
            combine,
            out_shape=jax.ShapeDtypeStruct((8, 32 * width), jnp.bfloat16),
            in_specs=[whole_vmem],
            out_specs=whole_vmem,
            name="combine",
        )(parts.reshape(1024, 2 * width))


def solution(mesh):
    fine = Mesh(mesh.devices.reshape(4, 2, 2, 8, 4), (quad, pair, core) + head)
    rows = P(everywhere, None)
    cache = P(None, pipe, head)
    return jax.shard_map(
        on_device,
        mesh=fine,
        in_specs=(rows, rows, rows, cache, cache, P(), P()),
        out_specs=rows,
        check_vma=False,
    )
```

time: 91.4 us -> 92.1 us (level)
  the two profiles are of different devices: /device:TPU:8 before, /device:TPU:16 now
where the time goes in v4:
time: 92.1 us; the launch traced here: 91.6 us
  blocking collectives  37.3 us (40%)
  starting transfers between devices  35.4 us (38%)
  waiting for transfers between devices  8.39 us (9%)
  Pallas kernels  8.02 us (9%)
  other arithmetic  1.61 us (2%)
    all_to_all x1, blocking collectives, on_device(): lax.all_to_all(parts.reshape(128, 8, 2 * width), (quad,) + head, split_ax...  37.3 us
    all_to_all x1, starting transfers between devices, on_device(): mine = lax.all_to_all(mine, head, split_axis=0, concat_axis=0, tiled=True)  10.1 us
    all_to_all x1, starting transfers between devices, on_device(): lax.all_to_all(queries, quad, split_axis=0, concat_axis=0, tiled=True)  9.4 us
    ppermute x2, waiting for transfers between devices, from_neighbours(): lax.ppermute(x, pair, swap)  6.13 us
    ppermute x2, starting transfers between devices, from_neighbours(): lax.ppermute(x, pair, swap)  6.12 us
    ppermute x2, starting transfers between devices, from_neighbours(): lax.ppermute(x, (pair, core), [(i, 3 - i) for i in range(4)])  5.48 us
    ppermute x2, starting transfers between devices, from_neighbours(): lax.ppermute(x, core, swap)  4.33 us
    pallas_call x1, Pallas kernels, on_device(): pl.pallas_call(functools.partial(attend, place=place), out_shape=jax.Shap...  4.12 us
  transfers between devices with their start and end apart: 8, of which 3 were waited for; matrix products, arithmetic and copies ran while one was open for 0% of the time, Pallas kernels for 2%

profile of v4, /device:TPU:16, one launch (start us, length us, event | category | flops | bytes accessed | tf_op | source)
XLA Modules:
  0.0 91.6 jit_solution(15096683088426152102)
XLA Ops:
  0.0 1.6 %pad_maximum_fusion = bf16[32,8,384]{2,1,0:T(8,128)(2,1)} fusion(bf16[32,8,128]{2,1,0:T(8,128)(2,1)} %bitcast.19, bf16[32,8,128]{2,1,0:T(8,128)(2,1)} %bitcast.20, bf16[32,8,128]{2,1,0:T(8,128)(2,1)} %bitcast.21), kind=kLoop, calls=%fused_computation | loop fusion | flops 589824 | bytes 393216 | tf_op jit(solution)/shard_map/tokens_to_heads/concatenate | solution.py:128
  1.6 10.1 %all-to-all-start = ((bf16[32,8,384]{2,1,0:T(8,128)(2,1)}), bf16[32,8,384]{2,1,0:T(8,128)(2,1)S(1)}, u32[]{:S(2)}, u32[]{:S(2)}) async-start(bf16[32,8,384]{2,1,0:T(8,128)(2,1)} %pad_maximum_fusion), calls=%async_computation | async-start | bytes 393216 | tf_op jit(solution)/shard_map/tokens_to_heads/all_to_all | solution.py:129
  11.7 1.7 %pick_stale.1.refs_3_ = bf16[256,256]{1,0:T(8,128)(2,1)} custom-call(s32[4]{0:T(128)} %lengths.3, s32[4]{0:T(128)} %steps.1, bf16[2,256,128]{2,1,0:T(8,128)(2,1)} %keys.1, bf16[2,256,128]{2,1,0:T(8,128)(2,1)} %values.1), custom_call_target="tpu_custom_call" | custom-call | tf_op jit(solution)/shard_map/stale/pick_stale/pallas_call | solution.py:133
  13.4 3.1 %collective-permute-start.2 = (bf16[256,256]{1,0:T(8,128)(2,1)}, bf16[256,256]{1,0:T(8,128)(2,1)S(1)}, u32[]{:S(2)}, u32[]{:S(2)}) collective-permute-start(bf16[256,256]{1,0:T(8,128)(2,1)} %pick_stale.1.refs_3_), channel_id=1, source_target_pairs={{0,96},{32,64},{64,32},{96,0},{1,97},{33,65},{65,33},{97,1},{2,98}... | collective-permute-start | bytes 393224 | tf_op jit(solution)/shard_map/stale/ppermute | solution.py:121
  16.5 3.0 %collective-permute-start.1 = (bf16[256,256]{1,0:T(8,128)(2,1)}, bf16[256,256]{1,0:T(8,128)(2,1)S(1)}, u32[]{:S(2)}, u32[]{:S(2)}) collective-permute-start(bf16[256,256]{1,0:T(8,128)(2,1)} %pick_stale.1.refs_3_), channel_id=1, source_target_pairs={{0,64},{64,0},{1,65},{65,1},{2,66},{66,2},{3,67},{67,3},{4,68},{68... | collective-permute-start | bytes 393224 | tf_op jit(solution)/shard_map/stale/ppermute | solution.py:120
  19.6 2.0 %collective-permute-start = (bf16[256,256]{1,0:T(8,128)(2,1)}, bf16[256,256]{1,0:T(8,128)(2,1)S(1)}, u32[]{:S(2)}, u32[]{:S(2)}) collective-permute-start(bf16[256,256]{1,0:T(8,128)(2,1)} %pick_stale.1.refs_3_), channel_id=1, source_target_pairs={{0,32},{32,0},{1,33},{33,1},{2,34},{34,2},{3,35},{35,3},{4,36},{36... | collective-permute-start | bytes 393224 | tf_op jit(solution)/shard_map/stale/ppermute | solution.py:119
  21.6 0.0 collective-permute-done.2.refs_6_
  21.6 3.1 %collective-permute-done.1.refs_5_ = bf16[256,256]{1,0:T(8,128)(2,1)S(1)} collective-permute-done((bf16[256,256]{1,0:T(8,128)(2,1)}, bf16[256,256]{1,0:T(8,128)(2,1)S(1)}, u32[]{:S(2)}, u32[]{:S(2)}) %collective-permute-start.1) | collective-permute-done | bytes 131104 | tf_op jit(solution)/shard_map/stale/ppermute | solution.py:120
  24.8 0.0 collective-permute-done.refs_4_
  24.8 0.0 all-to-all-done
  24.8 0.7 broadcast_in_dim.2
  25.5 9.4 %all-to-all-start.1 = ((bf16[4,256,128]{2,1,0:T(8,128)(2,1)}), bf16[4,256,128]{2,1,0:T(8,128)(2,1)S(1)}, u32[]{:S(2)}, u32[]{:S(2)}) async-start(bf16[4,256,128]{2,1,0:T(8,128)(2,1)} %broadcast_in_dim.2), calls=%async_computation.1 | async-start | bytes 524288 | tf_op jit(solution)/shard_map/gather_queries/all_to_all | solution.py:146
  34.9 0.0 copy-start.1
  34.9 2.3 %collective-permute-start.5 = (bf16[256,256]{1,0:T(8,128)(2,1)S(1)}, bf16[256,256]{1,0:T(8,128)(2,1)S(1)}, u32[]{:S(2)}, u32[]{:S(2)}) collective-permute-start(bf16[256,256]{1,0:T(8,128)(2,1)S(1)} %slice.7), channel_id=1, source_target_pairs={{0,96},{32,64},{64,32},{96,0},{1,97},{33,65},{65,33},{97,1},{2,98}... | collective-permute-start | bytes 393224 | tf_op jit(solution)/shard_map/neighbour_keys/ppermute | solution.py:121
  37.3 3.1 %collective-permute-start.4 = (bf16[256,256]{1,0:T(8,128)(2,1)S(1)}, bf16[256,256]{1,0:T(8,128)(2,1)S(1)}, u32[]{:S(2)}, u32[]{:S(2)}) collective-permute-start(bf16[256,256]{1,0:T(8,128)(2,1)S(1)} %slice.7), channel_id=1, source_target_pairs={{0,64},{64,0},{1,65},{65,1},{2,66},{66,2},{3,67},{67,3},{4,68},{68... | collective-permute-start | bytes 393224 | tf_op jit(solution)/shard_map/neighbour_keys/ppermute | solution.py:120
  40.4 2.3 %collective-permute-start.3 = (bf16[256,256]{1,0:T(8,128)(2,1)S(1)}, bf16[256,256]{1,0:T(8,128)(2,1)S(1)}, u32[]{:S(2)}, u32[]{:S(2)}) collective-permute-start(bf16[256,256]{1,0:T(8,128)(2,1)S(1)} %slice.7), channel_id=1, source_target_pairs={{0,32},{32,0},{1,33},{33,1},{2,34},{34,2},{3,35},{35,3},{4,36},{36... | collective-permute-start | bytes 393224 | tf_op jit(solution)/shard_map/neighbour_keys/ppermute | solution.py:119
  42.7 2.2 %collective-permute-done.5.refs_2_ = bf16[256,256]{1,0:T(8,128)(2,1)S(1)} collective-permute-done((bf16[256,256]{1,0:T(8,128)(2,1)S(1)}, bf16[256,256]{1,0:T(8,128)(2,1)S(1)}, u32[]{:S(2)}, u32[]{:S(2)}) %collective-permute-start.5) | collective-permute-done | bytes 131104 | tf_op jit(solution)/shard_map/neighbour_keys/ppermute | solution.py:121
  44.9 3.0 %collective-permute-done.4.refs_1_ = bf16[256,256]{1,0:T(8,128)(2,1)S(1)} collective-permute-done((bf16[256,256]{1,0:T(8,128)(2,1)S(1)}, bf16[256,256]{1,0:T(8,128)(2,1)S(1)}, u32[]{:S(2)}, u32[]{:S(2)}) %collective-permute-start.4) | collective-permute-done | bytes 131104 | tf_op jit(solution)/shard_map/neighbour_keys/ppermute | solution.py:120
  47.9 0.0 collective-permute-done.3.refs_0_
  47.9 0.0 all-to-all-done.1
  47.9 0.0 copy-done
  48.0 4.1 %attend.1 = bf16[1024,256]{1,0:T(8,128)(2,1)S(1)} custom-call(s32[4]{0:T(128)S(1)} %copy-done.1, bf16[1024,128]{1,0:T(8,128)(2,1)S(1)} %bitcast.17, bf16[256,384]{1,0:T(8,128)(2,1)S(1)} %bitcast.15, bf16[256,256]{1,0:T(8,128)(2,1)S(1)} %collective-permute-done.3.refs_0_, bf16[256,256]{1,0:T(8,128)(2,1)S(1)} %collective-permute-done.4.refs_1_, ...), custom_call_target="tpu_custom_call" | custom-call | flops 1073741824 | bytes 4194304 | tf_op jit(solution)/shard_map/attend/attend/pallas_call | solution.py:153
  52.1 37.3 %all_to_all.15 = bf16[128,8,256]{2,1,0:T(8,128)(2,1)} all-to-all(bf16[128,8,256]{2,1,0:T(8,128)(2,1)S(1)} %bitcast.16), channel_id=1, replica_groups=mesh['za'=4,'zb'=2,'core'=2,'y'=8,'x'=4] {'za','y','x'}, dimensions={0} | all-to-all | bytes 1048576 | tf_op jit(solution)/shard_map/heads_to_tokens/all_to_all | solution.py:164
  89.4 2.2 %combine.1 = bf16[8,4096]{1,0:T(8,128)(2,1)} custom-call(bf16[1024,256]{1,0:T(8,128)(2,1)} %bitcast.18), custom_call_target="tpu_custom_call" | custom-call | tf_op jit(solution)/shard_map/heads_to_tokens/combine/pallas_call | solution.py:165
  (4 shorter events, 0.0 us)
Async XLA Ops:
  1.6 23.2 %all-to-all-start = ((bf16[32,8,384]{2,1,0:T(8,128)(2,1)}), bf16[32,8,384]{2,1,0:T(8,128)(2,1)S(1)}, u32[]{:S(2)}, u32[]{:S(2)}) async-start(bf16[32,8,384]{2,1,0:T(8,128)(2,1)} %pad_maximum_fusion), calls=%async_computation | async-start | bytes 393216 | tf_op jit(solution)/shard_map/tokens_to_heads/all_to_all | solution.py:129
  13.4 8.2 %collective-permute-start.2 = (bf16[256,256]{1,0:T(8,128)(2,1)}, bf16[256,256]{1,0:T(8,128)(2,1)S(1)}, u32[]{:S(2)}, u32[]{:S(2)}) collective-permute-start(bf16[256,256]{1,0:T(8,128)(2,1)} %pick_stale.1.refs_3_), channel_id=1, source_target_pairs={{0,96},{32,64},{64,32},{96,0},{1,97},{33,65},{65,33},{97,1},{2,98}... | collective-permute-start | bytes 393224 | tf_op jit(solution)/shard_map/stale/ppermute | solution.py:121
  16.5 8.2 %collective-permute-start.1 = (bf16[256,256]{1,0:T(8,128)(2,1)}, bf16[256,256]{1,0:T(8,128)(2,1)S(1)}, u32[]{:S(2)}, u32[]{:S(2)}) collective-permute-start(bf16[256,256]{1,0:T(8,128)(2,1)} %pick_stale.1.refs_3_), channel_id=1, source_target_pairs={{0,64},{64,0},{1,65},{65,1},{2,66},{66,2},{3,67},{67,3},{4,68},{68... | collective-permute-start | bytes 393224 | tf_op jit(solution)/shard_map/stale/ppermute | solution.py:120
  19.6 5.2 %collective-permute-start = (bf16[256,256]{1,0:T(8,128)(2,1)}, bf16[256,256]{1,0:T(8,128)(2,1)S(1)}, u32[]{:S(2)}, u32[]{:S(2)}) collective-permute-start(bf16[256,256]{1,0:T(8,128)(2,1)} %pick_stale.1.refs_3_), channel_id=1, source_target_pairs={{0,32},{32,0},{1,33},{33,1},{2,34},{34,2},{3,35},{35,3},{4,36},{36... | collective-permute-start | bytes 393224 | tf_op jit(solution)/shard_map/stale/ppermute | solution.py:119
  25.5 22.4 %all-to-all-start.1 = ((bf16[4,256,128]{2,1,0:T(8,128)(2,1)}), bf16[4,256,128]{2,1,0:T(8,128)(2,1)S(1)}, u32[]{:S(2)}, u32[]{:S(2)}) async-start(bf16[4,256,128]{2,1,0:T(8,128)(2,1)} %broadcast_in_dim.2), calls=%async_computation.1 | async-start | bytes 524288 | tf_op jit(solution)/shard_map/gather_queries/all_to_all | solution.py:146
  34.9 13.0 %copy-start = (bf16[256,256]{1,0:T(8,128)(2,1)S(1)}, bf16[256,256]{1,0:T(8,128)(2,1)}, u32[]{:S(2)}) copy-start(bf16[256,256]{1,0:T(8,128)(2,1)} %pick_stale.1.refs_3_) | copy-start | bytes 393220
  34.9 13.0 %copy-start.1 = (s32[4]{0:T(128)S(1)}, s32[4]{0:T(128)}, u32[]{:S(2)}) copy-start(s32[4]{0:T(128)} %lengths.3) | copy-start | bytes 52
  34.9 10.0 %collective-permute-start.5 = (bf16[256,256]{1,0:T(8,128)(2,1)S(1)}, bf16[256,256]{1,0:T(8,128)(2,1)S(1)}, u32[]{:S(2)}, u32[]{:S(2)}) collective-permute-start(bf16[256,256]{1,0:T(8,128)(2,1)S(1)} %slice.7), channel_id=1, source_target_pairs={{0,96},{32,64},{64,32},{96,0},{1,97},{33,65},{65,33},{97,1},{2,98}... | collective-permute-start | bytes 393224 | tf_op jit(solution)/shard_map/neighbour_keys/ppermute | solution.py:121
  37.3 10.7 %collective-permute-start.4 = (bf16[256,256]{1,0:T(8,128)(2,1)S(1)}, bf16[256,256]{1,0:T(8,128)(2,1)S(1)}, u32[]{:S(2)}, u32[]{:S(2)}) collective-permute-start(bf16[256,256]{1,0:T(8,128)(2,1)S(1)} %slice.7), channel_id=1, source_target_pairs={{0,64},{64,0},{1,65},{65,1},{2,66},{66,2},{3,67},{67,3},{4,68},{68... | collective-permute-start | bytes 393224 | tf_op jit(solution)/shard_map/neighbour_keys/ppermute | solution.py:120
  40.4 7.6 %collective-permute-start.3 = (bf16[256,256]{1,0:T(8,128)(2,1)S(1)}, bf16[256,256]{1,0:T(8,128)(2,1)S(1)}, u32[]{:S(2)}, u32[]{:S(2)}) collective-permute-start(bf16[256,256]{1,0:T(8,128)(2,1)S(1)} %slice.7), channel_id=1, source_target_pairs={{0,32},{32,0},{1,33},{33,1},{2,34},{34,2},{3,35},{35,3},{4,36},{36... | collective-permute-start | bytes 393224 | tf_op jit(solution)/shard_map/neighbour_keys/ppermute | solution.py:119

commit v5 on v4

--- a/solution.py
+++ b/solution.py
@@ -18,6 +18,7 @@
 everywhere = pipe + head
 
 whole_vmem = pl.BlockSpec(memory_space=pltpu.VMEM)
+small_kernel = pltpu.CompilerParams(vmem_limit_bytes=8 << 20)
 whole_smem = pl.BlockSpec(memory_space=pltpu.SMEM)
 
 
@@ -41,8 +42,7 @@
         out[:, at * width : (at + 1) * width] = jnp.where(older, older_rows, newer_rows).astype(jnp.bfloat16)
 
 
-def attend(lengths, queries, own, *refs, place):
-    fresh_refs, stale_refs, out = refs[:3], refs[3:7], refs[7]
+def attend(lengths, queries, fresh, stale, out, *, place):
     za, zb, c = place()
     ends = patch_ends(lengths)
     lane = lax.broadcasted_iota(jnp.int32, (span, width), 1)
@@ -50,13 +50,9 @@
     row_offset = lax.broadcasted_iota(jnp.int32, (span, 1), 0)
 
     blocks = []
-    for at, (pair_at, core_at) in enumerate(((zb, c), (zb, 1 - c), (1 - zb, c), (1 - zb, 1 - c))):
-        if at == 0:
-            keys, values = own[:, width : 2 * width], own[:, 2 * width :]
-        else:
-            keys, values = fresh_refs[at - 1][:, :width], fresh_refs[at - 1][:, width:]
-        stale_keys, stale_values = stale_refs[at][:, :width], stale_refs[at][:, width:]
-        blocks.append((keys, values, stale_keys, stale_values, za * 1024 + pair_at * 512 + core_at * span))
+    for at in range(4):
+        rows = pl.ds(at * span, span)
+        blocks.append((fresh[rows, :width], fresh[rows, width:], stale[rows, :width], stale[rows, width:], za * 1024 + at * span))
 
     for at in range(4):
         rows = pl.ds(at * span, span)
@@ -115,11 +111,7 @@
     swap = [(0, 1), (1, 0)]
 
     def from_neighbours(x):
-        return (
-            lax.ppermute(x, core, swap),
-            lax.ppermute(x, pair, swap),
-            lax.ppermute(x, (pair, core), [(i, 3 - i) for i in range(4)]),
-        )
+        return lax.all_gather(x, (pair, core), axis=0, tiled=True)
 
     def by_head(x):
         return jnp.transpose(x.reshape(8, 32, width), (1, 0, 2))
@@ -135,11 +127,12 @@
             out_shape=jax.ShapeDtypeStruct((span, 2 * width), jnp.bfloat16),
             in_specs=[whole_smem] * 2 + [whole_vmem] * 2,
             out_specs=whole_vmem,
+            compiler_params=small_kernel,
             name="pick_stale",
         )(patch_lengths, stale_step, stale_key, stale_value)
         stale = from_neighbours(stale_own)
 
-    mine, *stale = lax.optimization_barrier((mine, *stale))
+    mine, stale = lax.optimization_barrier((mine, stale))
 
     with jax.named_scope("gather_queries"):
         queries = jnp.broadcast_to(mine[None, :, :width], (4, span, width))
@@ -153,12 +146,12 @@
         parts = pl.pallas_call(
             functools.partial(attend, place=place),
             out_shape=jax.ShapeDtypeStruct((4 * span, 2 * width), jnp.bfloat16),
-            in_specs=[whole_smem] + [whole_vmem] * 9,
+            in_specs=[whole_smem] + [whole_vmem] * 3,
             out_specs=whole_vmem,
-            compiler_params=pltpu.CompilerParams(vmem_limit_bytes=40 * 1024 * 1024),
+            compiler_params=pltpu.CompilerParams(vmem_limit_bytes=24 << 20),
             cost_estimate=pl.CostEstimate(flops=2 * 2 * 512 * 4096 * 128, bytes_accessed=4 << 20, transcendentals=1 << 20),
             name="attend",
-        )(patch_lengths, queries, mine, *fresh, stale_own, *stale)
+        )(patch_lengths, queries, fresh, stale)
 
     with jax.named_scope("heads_to_tokens"):
         parts = lax.all_to_all(parts.reshape(128, 8, 2 * width), (quad,) + head, split_axis=0, concat_axis=0, tiled=True)
@@ -167,6 +160,7 @@
             out_shape=jax.ShapeDtypeStruct((8, 32 * width), jnp.bfloat16),
             in_specs=[whole_vmem],
             out_specs=whole_vmem,
+            compiler_params=small_kernel,
             name="combine",
         )(parts.reshape(1024, 2 * width))
 

time: 92.1 us -> 85.2 us (0.925)
  blocking collectives: 37.3 us -> 53.4 us
  starting transfers between devices: 35.4 us -> 20.5 us
  waiting for transfers between devices: 8.39 us -> 2.71 us
  Pallas kernels: 8.02 us -> 5.83 us
    all_gather x0 -> x2, blocking collectives: none -> 18.4 us  [from_neighbours(): return lax.all_gather(x, (pair, core), axis=0, tiled=True)]
    ppermute x6 -> x0, starting transfers between devices: 15.9 us -> none  [the longest x2 6.12 us: from_neighbours(): lax.ppermute(x, pair, swap)]
    ppermute x6 -> x0, waiting for transfers between devices: 8.38 us -> none  [the longest x2 6.13 us: from_neighbours(): lax.ppermute(x, pair, swap)]
    all_to_all x1, blocking collectives: 37.3 us -> 35 us  [on_device(): lax.all_to_all(parts.reshape(128, 8, 2 * width), (quad,) + head, split_ax...]
    all_to_all x1, waiting for transfers between devices: 0.01 us -> 1.43 us  [on_device(): lax.all_to_all(queries, quad, split_axis=0, concat_axis=0, tiled=True)]
    all_to_all x1, waiting for transfers between devices: 0.01 us -> 1.28 us  [on_device(): mine = lax.all_to_all(mine, head, split_axis=0, concat_axis=0, tiled=True)]
    pallas_call x1, Pallas kernels: 1.72 us -> 0.64 us  [on_device(): pl.pallas_call(select, out_shape=jax.ShapeDtypeStruct((span, 2 * width),...]
    pallas_call x1, Pallas kernels: 2.18 us -> 1.14 us  [on_device(): pl.pallas_call(combine, out_shape=jax.ShapeDtypeStruct((8, 32 * width), j...]
  transfers between devices with their start and end apart: 8 -> 2, of which waited for: 3 -> 2; matrix products, arithmetic and copies ran while one was open for 0% -> 0% of each run, Pallas kernels for 2% -> 1%
where the time goes in v5:
time: 85.2 us; the launch traced here: 84.9 us
  blocking collectives  53.4 us (63%)
  starting transfers between devices  20.5 us (24%)
  Pallas kernels  5.83 us (7%)
  waiting for transfers between devices  2.71 us (3%)
  other arithmetic  1.6 us (2%)
    all_to_all x1, blocking collectives, on_device(): lax.all_to_all(parts.reshape(128, 8, 2 * width), (quad,) + head, split_ax...  35 us
    all_gather x2, blocking collectives, from_neighbours(): return lax.all_gather(x, (pair, core), axis=0, tiled=True)  18.4 us
    all_to_all x1, starting transfers between devices, on_device(): lax.all_to_all(queries, quad, split_axis=0, concat_axis=0, tiled=True)  10.3 us
    all_to_all x1, starting transfers between devices, on_device(): mine = lax.all_to_all(mine, head, split_axis=0, concat_axis=0, tiled=True)  10.2 us
    pallas_call x1, Pallas kernels, on_device(): pl.pallas_call(functools.partial(attend, place=place), out_shape=jax.Shap...  4.06 us
  transfers between devices with their start and end apart: 2, of which 2 were waited for; matrix products, arithmetic and copies ran while one was open for 0% of the time, Pallas kernels for 1%

profile of v5, /device:TPU:16, one launch (start us, length us, event | category | flops | bytes accessed | tf_op | source)
XLA Modules:
  0.0 84.9 jit_solution(17206022041255976682)
XLA Ops:
  0.0 1.6 %pad_maximum_fusion = bf16[32,8,384]{2,1,0:T(8,128)(2,1)} fusion(bf16[32,8,128]{2,1,0:T(8,128)(2,1)} %bitcast.18, bf16[32,8,128]{2,1,0:T(8,128)(2,1)} %bitcast.19, bf16[32,8,128]{2,1,0:T(8,128)(2,1)} %bitcast.20), kind=kLoop, calls=%fused_computation | loop fusion | flops 589824 | bytes 393216 | tf_op jit(solution)/shard_map/tokens_to_heads/concatenate | solution.py:120
  1.6 0.0 copy-start
  1.6 0.0 copy-start.1
  1.6 0.0 copy-start.2
  1.6 0.0 copy-start.3
  1.6 10.2 %all-to-all-start = ((bf16[32,8,384]{2,1,0:T(8,128)(2,1)}), bf16[32,8,384]{2,1,0:T(8,128)(2,1)S(1)}, u32[]{:S(2)}, u32[]{:S(2)}) async-start(bf16[32,8,384]{2,1,0:T(8,128)(2,1)} %pad_maximum_fusion), calls=%async_computation | async-start | bytes 393216 | tf_op jit(solution)/shard_map/tokens_to_heads/all_to_all | solution.py:121
  11.8 0.0 copy-done
  11.8 0.0 copy-done.1
  11.8 0.0 copy-done.2
  11.8 0.0 copy-done.3
  11.9 0.6 pick_stale.1
  12.5 8.1 %all_gather.6.stale = bf16[1024,256]{1,0:T(8,128)(2,1)S(1)} all-gather(bf16[256,256]{1,0:T(8,128)(2,1)S(1)} %pick_stale.1), channel_id=1, replica_groups=mesh['za'=4,'zb'=2,'core'=2,'y'=8,'x'=4] {'zb','core'}, dimensions={0}, use_global_device_ids=true | all-gather | bytes 655360 | tf_op jit(solution)/shard_map/stale/all_gather | solution.py:114
  20.6 1.3 %all-to-all-done = bf16[32,8,384]{2,1,0:T(8,128)(2,1)S(1)} async-done(((bf16[32,8,384]{2,1,0:T(8,128)(2,1)}), bf16[32,8,384]{2,1,0:T(8,128)(2,1)S(1)}, u32[]{:S(2)}, u32[]{:S(2)}) %all-to-all-start) | async-done | bytes 196640 | tf_op jit(solution)/shard_map/tokens_to_heads/all_to_all | solution.py:121
  21.8 0.7 broadcast_in_dim.2
  22.6 10.3 %all-to-all-start.1 = ((bf16[4,256,128]{2,1,0:T(8,128)(2,1)}), bf16[4,256,128]{2,1,0:T(8,128)(2,1)S(1)}, u32[]{:S(2)}, u32[]{:S(2)}) async-start(bf16[4,256,128]{2,1,0:T(8,128)(2,1)} %broadcast_in_dim.2), calls=%async_computation.1 | async-start | bytes 524288 | tf_op jit(solution)/shard_map/gather_queries/all_to_all | solution.py:139
  32.9 10.4 %all_gather.7.fresh = bf16[1024,256]{1,0:T(8,128)(2,1)S(1)} all-gather(bf16[256,256]{1,0:T(8,128)(2,1)S(1)} %slice.7), channel_id=1, replica_groups=mesh['za'=4,'zb'=2,'core'=2,'y'=8,'x'=4] {'zb','core'}, dimensions={0}, use_global_device_ids=true | all-gather | bytes 655360 | tf_op jit(solution)/shard_map/neighbour_keys/all_gather | solution.py:114
  43.3 1.4 %all-to-all-done.1 = bf16[4,256,128]{2,1,0:T(8,128)(2,1)S(1)} async-done(((bf16[4,256,128]{2,1,0:T(8,128)(2,1)}), bf16[4,256,128]{2,1,0:T(8,128)(2,1)S(1)}, u32[]{:S(2)}, u32[]{:S(2)}) %all-to-all-start.1) | async-done | bytes 262176 | tf_op jit(solution)/shard_map/gather_queries/all_to_all | solution.py:139
  44.7 4.1 %attend.1 = bf16[1024,256]{1,0:T(8,128)(2,1)S(1)} custom-call(s32[4]{0:T(128)S(1)} %copy-done.3, bf16[1024,128]{1,0:T(8,128)(2,1)S(1)} %bitcast.15, bf16[1024,256]{1,0:T(8,128)(2,1)S(1)} %all_gather.7.fresh, bf16[1024,256]{1,0:T(8,128)(2,1)S(1)} %all_gather.6.stale), custom_call_target="tpu_custom_call" | custom-call | flops 1073741824 | bytes 4194304 | tf_op jit(solution)/shard_map/attend/attend/pallas_call | solution.py:146
  48.8 35.0 %all_to_all.15 = bf16[128,8,256]{2,1,0:T(8,128)(2,1)S(1)} all-to-all(bf16[128,8,256]{2,1,0:T(8,128)(2,1)S(1)} %bitcast.14), channel_id=1, replica_groups=mesh['za'=4,'zb'=2,'core'=2,'y'=8,'x'=4] {'za','y','x'}, dimensions={0} | all-to-all | bytes 1048576 | tf_op jit(solution)/shard_map/heads_to_tokens/all_to_all | solution.py:157
  83.8 1.1 %combine.1 = bf16[8,4096]{1,0:T(8,128)(2,1)} custom-call(bf16[1024,256]{1,0:T(8,128)(2,1)S(1)} %bitcast.13), custom_call_target="tpu_custom_call" | custom-call | tf_op jit(solution)/shard_map/heads_to_tokens/combine/pallas_call | solution.py:158
  (2 shorter events, 0.0 us)
Async XLA Ops:
  1.6 10.2 %copy-start = (bf16[2,256,128]{2,1,0:T(8,128)(2,1)S(1)}, bf16[2,256,128]{2,1,0:T(8,128)(2,1)}, u32[]{:S(2)}) copy-start(bf16[2,256,128]{2,1,0:T(8,128)(2,1)} %keys.1) | copy-start | bytes 393220
  1.6 10.2 %copy-start.1 = (bf16[2,256,128]{2,1,0:T(8,128)(2,1)S(1)}, bf16[2,256,128]{2,1,0:T(8,128)(2,1)}, u32[]{:S(2)}) copy-start(bf16[2,256,128]{2,1,0:T(8,128)(2,1)} %values.1) | copy-start | bytes 393220
  1.6 10.2 %copy-start.2 = (s32[4]{0:T(128)S(1)}, s32[4]{0:T(128)}, u32[]{:S(2)}) copy-start(s32[4]{0:T(128)} %steps.1) | copy-start | bytes 52
  1.6 10.2 %copy-start.3 = (s32[4]{0:T(128)S(1)}, s32[4]{0:T(128)}, u32[]{:S(2)}) copy-start(s32[4]{0:T(128)} %lengths.3) | copy-start | bytes 52
  1.6 20.2 %all-to-all-start = ((bf16[32,8,384]{2,1,0:T(8,128)(2,1)}), bf16[32,8,384]{2,1,0:T(8,128)(2,1)S(1)}, u32[]{:S(2)}, u32[]{:S(2)}) async-start(bf16[32,8,384]{2,1,0:T(8,128)(2,1)} %pad_maximum_fusion), calls=%async_computation | async-start | bytes 393216 | tf_op jit(solution)/shard_map/tokens_to_heads/all_to_all | solution.py:121
  22.6 22.1 %all-to-all-start.1 = ((bf16[4,256,128]{2,1,0:T(8,128)(2,1)}), bf16[4,256,128]{2,1,0:T(8,128)(2,1)S(1)}, u32[]{:S(2)}, u32[]{:S(2)}) async-start(bf16[4,256,128]{2,1,0:T(8,128)(2,1)} %broadcast_in_dim.2), calls=%async_computation.1 | async-start | bytes 524288 | tf_op jit(solution)/shard_map/gather_queries/all_to_all | solution.py:139

commit v6 on v5

--- a/solution.py
+++ b/solution.py
@@ -88,16 +88,14 @@
 
 
 def combine(parts, out):
-    heads = out.shape[1] // width
-    blocks = parts[...].astype(jnp.float32).reshape(4, heads, 8, 2 * width)
-    outputs = blocks[..., :width]
-    peaks = blocks[..., width : width + 1]
-    totals = blocks[..., width + 1 : width + 2] + blocks[..., width + 2 : width + 3]
-    shares = totals * jnp.exp2(peaks - jnp.max(peaks, axis=0, keepdims=True))
-    shares = shares / jnp.sum(shares, axis=0, keepdims=True)
-    joined = jnp.sum(outputs * shares, axis=0)
-    for h in range(heads):
-        out[:, h * width : (h + 1) * width] = joined[h].astype(jnp.bfloat16)
+    blocks = [parts[pl.ds(s * span, span), :].astype(jnp.float32) for s in range(4)]
+    peaks = [b[:, width : width + 1] for b in blocks]
+    totals = [b[:, width + 1 : width + 2] + b[:, width + 2 : width + 3] for b in blocks]
+    top = functools.reduce(jnp.maximum, peaks)
+    shares = [t * jnp.exp2(p - top) for t, p in zip(totals, peaks)]
+    whole = functools.reduce(jnp.add, shares)
+    joined = functools.reduce(jnp.add, [b[:, :width] * s for b, s in zip(blocks, shares)])
+    out[...] = (joined / whole).astype(jnp.bfloat16)
 
 
 def on_device(query, key, value, stale_key, stale_value, patch_lengths, stale_step):
@@ -153,16 +151,20 @@
             name="attend",
         )(patch_lengths, queries, fresh, stale)
 
-    with jax.named_scope("heads_to_tokens"):
-        parts = lax.all_to_all(parts.reshape(128, 8, 2 * width), (quad,) + head, split_axis=0, concat_axis=0, tiled=True)
-        return pl.pallas_call(
+    with jax.named_scope("join_partials"):
+        parts = lax.all_to_all(parts.reshape(4, span, 2 * width), quad, split_axis=0, concat_axis=0, tiled=True)
+        joined = pl.pallas_call(
             combine,
-            out_shape=jax.ShapeDtypeStruct((8, 32 * width), jnp.bfloat16),
+            out_shape=jax.ShapeDtypeStruct((span, width), jnp.bfloat16),
             in_specs=[whole_vmem],
             out_specs=whole_vmem,
             compiler_params=small_kernel,
             name="combine",
-        )(parts.reshape(1024, 2 * width))
+        )(parts.reshape(4 * span, 2 * width))
+
+    with jax.named_scope("heads_to_tokens"):
+        joined = lax.all_to_all(joined.reshape(32, 8, width), head, split_axis=0, concat_axis=0, tiled=True)
+        return jnp.transpose(joined, (1, 0, 2)).reshape(8, 32 * width)
 
 
 def solution(mesh):

time: 85.2 us -> 89.7 us (1.053)
  the two profiles are of different devices: /device:TPU:16 before, /device:TPU:8 now
where the time goes in v6:
time: 89.7 us; the launch traced here: 89.3 us
  blocking collectives  56.2 us (63%)
  starting transfers between devices  20.6 us (23%)
  Pallas kernels  5.16 us (6%)
  waiting for transfers between devices  4.32 us (5%)
  other arithmetic  1.6 us (2%)
  local copies, waits for them, and re-layouts  1.39 us (2%)
    all_to_all x1, blocking collectives, on_device(): lax.all_to_all(parts.reshape(4, span, 2 * width), quad, split_axis=0, con...  21.6 us
    all_gather x2, blocking collectives, from_neighbours(): return lax.all_gather(x, (pair, core), axis=0, tiled=True)  17.6 us
    all_to_all x1, blocking collectives, on_device(): lax.all_to_all(joined.reshape(32, 8, width), head, split_axis=0, concat_a...  16.9 us
    all_to_all x1, starting transfers between devices, on_device(): mine = lax.all_to_all(mine, head, split_axis=0, concat_axis=0, tiled=True)  10.3 us
    all_to_all x1, starting transfers between devices, on_device(): lax.all_to_all(queries, quad, split_axis=0, concat_axis=0, tiled=True)  10.3 us
    pallas_call x1, Pallas kernels, on_device(): pl.pallas_call(functools.partial(attend, place=place), out_shape=jax.Shap...  4.06 us
    all_to_all x1, waiting for transfers between devices, on_device(): lax.all_to_all(queries, quad, split_axis=0, concat_axis=0, tiled=True)  2.19 us
    all_to_all x1, waiting for transfers between devices, on_device(): mine = lax.all_to_all(mine, head, split_axis=0, concat_axis=0, tiled=True)  2.13 us
  transfers between devices with their start and end apart: 2, of which 2 were waited for; matrix products, arithmetic and copies ran while one was open for 0% of the time, Pallas kernels for 1%

profile of v6, /device:TPU:8, one launch (start us, length us, event | category | flops | bytes accessed | tf_op | source)
XLA Modules:
  0.0 89.3 jit_solution(5575406521112063544)
XLA Ops:
  0.0 1.6 %pad_maximum_fusion = bf16[32,8,384]{2,1,0:T(8,128)(2,1)} fusion(bf16[32,8,128]{2,1,0:T(8,128)(2,1)} %bitcast.24, bf16[32,8,128]{2,1,0:T(8,128)(2,1)} %bitcast.25, bf16[32,8,128]{2,1,0:T(8,128)(2,1)} %bitcast.26), kind=kLoop, calls=%fused_computation | loop fusion | flops 589824 | bytes 393216 | tf_op jit(solution)/shard_map/tokens_to_heads/concatenate | solution.py:118
  1.6 0.0 copy-start
  1.6 0.0 copy-start.1
  1.6 0.0 copy-start.2
  1.6 0.0 copy-start.3
  1.6 10.3 %all-to-all-start = ((bf16[32,8,384]{2,1,0:T(8,128)(2,1)}), bf16[32,8,384]{2,1,0:T(8,128)(2,1)S(1)}, u32[]{:S(2)}, u32[]{:S(2)}) async-start(bf16[32,8,384]{2,1,0:T(8,128)(2,1)} %pad_maximum_fusion), calls=%async_computation | async-start | bytes 393216 | tf_op jit(solution)/shard_map/tokens_to_heads/all_to_all | solution.py:119
  11.9 0.0 copy-done
  11.9 0.0 copy-done.1
  12.0 0.0 copy-done.2
  12.0 0.0 copy-done.3
  12.0 0.6 pick_stale.1
  12.6 8.1 %all_gather.6.stale = bf16[1024,256]{1,0:T(8,128)(2,1)S(1)} all-gather(bf16[256,256]{1,0:T(8,128)(2,1)S(1)} %pick_stale.1), channel_id=1, replica_groups=mesh['za'=4,'zb'=2,'core'=2,'y'=8,'x'=4] {'zb','core'}, dimensions={0}, use_global_device_ids=true | all-gather | bytes 655360 | tf_op jit(solution)/shard_map/stale/all_gather | solution.py:112
  20.7 2.1 %all-to-all-done = bf16[32,8,384]{2,1,0:T(8,128)(2,1)S(1)} async-done(((bf16[32,8,384]{2,1,0:T(8,128)(2,1)}), bf16[32,8,384]{2,1,0:T(8,128)(2,1)S(1)}, u32[]{:S(2)}, u32[]{:S(2)}) %all-to-all-start) | async-done | bytes 196640 | tf_op jit(solution)/shard_map/tokens_to_heads/all_to_all | solution.py:119
  22.8 0.7 broadcast_in_dim.2
  23.5 10.3 %all-to-all-start.1 = ((bf16[4,256,128]{2,1,0:T(8,128)(2,1)}), bf16[4,256,128]{2,1,0:T(8,128)(2,1)S(1)}, u32[]{:S(2)}, u32[]{:S(2)}) async-start(bf16[4,256,128]{2,1,0:T(8,128)(2,1)} %broadcast_in_dim.2), calls=%async_computation.1 | async-start | bytes 524288 | tf_op jit(solution)/shard_map/gather_queries/all_to_all | solution.py:137
  33.8 9.6 %all_gather.7.fresh = bf16[1024,256]{1,0:T(8,128)(2,1)S(1)} all-gather(bf16[256,256]{1,0:T(8,128)(2,1)S(1)} %slice.7), channel_id=1, replica_groups=mesh['za'=4,'zb'=2,'core'=2,'y'=8,'x'=4] {'zb','core'}, dimensions={0}, use_global_device_ids=true | all-gather | bytes 655360 | tf_op jit(solution)/shard_map/neighbour_keys/all_gather | solution.py:112
  43.4 2.2 %all-to-all-done.1 = bf16[4,256,128]{2,1,0:T(8,128)(2,1)S(1)} async-done(((bf16[4,256,128]{2,1,0:T(8,128)(2,1)}), bf16[4,256,128]{2,1,0:T(8,128)(2,1)S(1)}, u32[]{:S(2)}, u32[]{:S(2)}) %all-to-all-start.1) | async-done | bytes 262176 | tf_op jit(solution)/shard_map/gather_queries/all_to_all | solution.py:137
  45.6 4.1 %attend.1 = bf16[1024,256]{1,0:T(8,128)(2,1)S(1)} custom-call(s32[4]{0:T(128)S(1)} %copy-done.3, bf16[1024,128]{1,0:T(8,128)(2,1)S(1)} %bitcast.20, bf16[1024,256]{1,0:T(8,128)(2,1)S(1)} %all_gather.7.fresh, bf16[1024,256]{1,0:T(8,128)(2,1)S(1)} %all_gather.6.stale), custom_call_target="tpu_custom_call" | custom-call | flops 1073741824 | bytes 4194304 | tf_op jit(solution)/shard_map/attend/attend/pallas_call | solution.py:144
  49.7 21.6 %all_to_all.20 = bf16[4,256,256]{2,1,0:T(8,128)(2,1)S(1)} all-to-all(bf16[4,256,256]{2,1,0:T(8,128)(2,1)S(1)} %bitcast.18), channel_id=1, replica_groups=mesh['za'=4,'zb'=2,'core'=2,'y'=8,'x'=4] {'za'}, dimensions={0} | all-to-all | bytes 1048576 | tf_op jit(solution)/shard_map/join_partials/all_to_all | solution.py:155
  71.3 0.5 combine.1
  71.8 16.9 %all_to_all.21 = bf16[32,8,128]{2,1,0:T(8,128)(2,1)S(1)} all-to-all(bf16[32,8,128]{2,1,0:T(8,128)(2,1)S(1)} %bitcast.19), channel_id=1, replica_groups=mesh['za'=4,'zb'=2,'core'=2,'y'=8,'x'=4] {'y','x'}, dimensions={0} | all-to-all | bytes 131072 | tf_op jit(solution)/shard_map/heads_to_tokens/all_to_all | solution.py:166
  88.7 0.6 copy.9
  (2 shorter events, 0.0 us)
Async XLA Ops:
  1.6 10.3 %copy-start = (bf16[2,256,128]{2,1,0:T(8,128)(2,1)S(1)}, bf16[2,256,128]{2,1,0:T(8,128)(2,1)}, u32[]{:S(2)}) copy-start(bf16[2,256,128]{2,1,0:T(8,128)(2,1)} %keys.1) | copy-start | bytes 393220
  1.6 10.3 %copy-start.1 = (bf16[2,256,128]{2,1,0:T(8,128)(2,1)S(1)}, bf16[2,256,128]{2,1,0:T(8,128)(2,1)}, u32[]{:S(2)}) copy-start(bf16[2,256,128]{2,1,0:T(8,128)(2,1)} %values.1) | copy-start | bytes 393220
  1.6 10.3 %copy-start.2 = (s32[4]{0:T(128)S(1)}, s32[4]{0:T(128)}, u32[]{:S(2)}) copy-start(s32[4]{0:T(128)} %steps.1) | copy-start | bytes 52
  1.6 10.4 %copy-start.3 = (s32[4]{0:T(128)S(1)}, s32[4]{0:T(128)}, u32[]{:S(2)}) copy-start(s32[4]{0:T(128)} %lengths.3) | copy-start | bytes 52
  1.6 21.2 %all-to-all-start = ((bf16[32,8,384]{2,1,0:T(8,128)(2,1)}), bf16[32,8,384]{2,1,0:T(8,128)(2,1)S(1)}, u32[]{:S(2)}, u32[]{:S(2)}) async-start(bf16[32,8,384]{2,1,0:T(8,128)(2,1)} %pad_maximum_fusion), calls=%async_computation | async-start | bytes 393216 | tf_op jit(solution)/shard_map/tokens_to_heads/all_to_all | solution.py:119
  23.5 22.1 %all-to-all-start.1 = ((bf16[4,256,128]{2,1,0:T(8,128)(2,1)}), bf16[4,256,128]{2,1,0:T(8,128)(2,1)S(1)}, u32[]{:S(2)}, u32[]{:S(2)}) async-start(bf16[4,256,128]{2,1,0:T(8,128)(2,1)} %broadcast_in_dim.2), calls=%async_computation.1 | async-start | bytes 524288 | tf_op jit(solution)/shard_map/gather_queries/all_to_all | solution.py:137

commit v7 on v5

--- a/solution.py
+++ b/solution.py
@@ -42,7 +42,7 @@
         out[:, at * width : (at + 1) * width] = jnp.where(older, older_rows, newer_rows).astype(jnp.bfloat16)
 
 
-def attend(lengths, queries, fresh, stale, out, *, place):
+def attend(lengths, own, away, fresh_same, fresh_other, stale_same, stale_other, out, *, place):
     za, zb, c = place()
     ends = patch_ends(lengths)
     lane = lax.broadcasted_iota(jnp.int32, (span, width), 1)
@@ -52,12 +52,13 @@
     blocks = []
     for at in range(4):
         rows = pl.ds(at * span, span)
-        blocks.append((fresh[rows, :width], fresh[rows, width:], stale[rows, :width], stale[rows, width:], za * 1024 + at * span))
+        for fresh, stale, core_at in ((fresh_same, stale_same, c), (fresh_other, stale_other, 1 - c)):
+            first = at * 1024 + zb * 512 + core_at * span
+            blocks.append((fresh[rows, :width], fresh[rows, width:], stale[rows, :width], stale[rows, width:], first))
 
-    for at in range(4):
-        rows = pl.ds(at * span, span)
-        q = queries[rows, :]
-        position = at * 1024 + zb * 512 + c * span + row_offset
+    for queries, pair_at in ((own, zb), (away, 1 - zb)):
+        q = queries[:, :width]
+        position = za * 1024 + pair_at * 512 + c * span + row_offset
         reach = jnp.full((span, 1), ends[patches - 1], jnp.int32)
         for m in range(patches - 2, -1, -1):
             reach = jnp.where(position < ends[m], ends[m], reach)
@@ -83,13 +84,14 @@
             )
         high = total.astype(jnp.bfloat16).astype(jnp.float32)
         stats = jnp.where(lane == 0, peak, jnp.where(lane == 1, high, total - high))
+        rows = pl.ds(pl.multiple_of(pair_at * span, span), span)
         out[rows, :width] = (summed / total).astype(jnp.bfloat16)
         out[rows, width:] = stats.astype(jnp.bfloat16)
 
 
 def combine(parts, out):
     heads = out.shape[1] // width
-    blocks = parts[...].astype(jnp.float32).reshape(4, heads, 8, 2 * width)
+    blocks = parts[...].astype(jnp.float32).reshape(2, heads, 8, 2 * width)
     outputs = blocks[..., :width]
     peaks = blocks[..., width : width + 1]
     totals = blocks[..., width + 1 : width + 2] + blocks[..., width + 2 : width + 3]
@@ -110,9 +112,6 @@
 
     swap = [(0, 1), (1, 0)]
 
-    def from_neighbours(x):
-        return lax.all_gather(x, (pair, core), axis=0, tiled=True)
-
     def by_head(x):
         return jnp.transpose(x.reshape(8, 32, width), (1, 0, 2))
 
@@ -130,31 +129,36 @@
             compiler_params=small_kernel,
             name="pick_stale",
         )(patch_lengths, stale_step, stale_key, stale_value)
-        stale = from_neighbours(stale_own)
+        stale_same = lax.all_gather(stale_own, quad, axis=0, tiled=True)
 
-    mine, stale = lax.optimization_barrier((mine, stale))
+    mine, stale_same = lax.optimization_barrier((mine, stale_same))
 
-    with jax.named_scope("gather_queries"):
-        queries = jnp.broadcast_to(mine[None, :, :width], (4, span, width))
-        queries = lax.all_to_all(queries, quad, split_axis=0, concat_axis=0, tiled=True)
-        queries = queries.reshape(4 * span, width)
+    with jax.named_scope("other_core_stale"):
+        stale_other = lax.ppermute(stale_same, core, swap)
 
-    with jax.named_scope("neighbour_keys"):
-        fresh = from_neighbours(mine[:, width:])
+    with jax.named_scope("swap_queries"):
+        away_q = lax.ppermute(mine[:, :width], pair, swap)
+
+    with jax.named_scope("gather_keys"):
+        fresh_same = jnp.broadcast_to(mine[None, :, width:], (4, span, 2 * width))
+        fresh_same = lax.all_to_all(fresh_same, quad, split_axis=0, concat_axis=0, tiled=True)
+        fresh_same, stale_other, away_q = lax.optimization_barrier((fresh_same, stale_other, away_q))
+        fresh_same = fresh_same.reshape(4 * span, 2 * width)
+        fresh_other = lax.ppermute(fresh_same, core, swap)
 
     with jax.named_scope("attend"):
         parts = pl.pallas_call(
             functools.partial(attend, place=place),
-            out_shape=jax.ShapeDtypeStruct((4 * span, 2 * width), jnp.bfloat16),
-            in_specs=[whole_smem] + [whole_vmem] * 3,
+            out_shape=jax.ShapeDtypeStruct((2 * span, 2 * width), jnp.bfloat16),
+            in_specs=[whole_smem] + [whole_vmem] * 6,
             out_specs=whole_vmem,
             compiler_params=pltpu.CompilerParams(vmem_limit_bytes=24 << 20),
             cost_estimate=pl.CostEstimate(flops=2 * 2 * 512 * 4096 * 128, bytes_accessed=4 << 20, transcendentals=1 << 20),
             name="attend",
-        )(patch_lengths, queries, fresh, stale)
+        )(patch_lengths, mine, away_q, fresh_same, fresh_other, stale_same, stale_other)
 
     with jax.named_scope("heads_to_tokens"):
-        parts = lax.all_to_all(parts.reshape(128, 8, 2 * width), (quad,) + head, split_axis=0, concat_axis=0, tiled=True)
+        parts = lax.all_to_all(parts.reshape(64, 8, 2 * width), (pair,) + head, split_axis=0, concat_axis=0, tiled=True)
         return pl.pallas_call(
             combine,
             out_shape=jax.ShapeDtypeStruct((8, 32 * width), jnp.bfloat16),
@@ -162,7 +166,7 @@
             out_specs=whole_vmem,
             compiler_params=small_kernel,
             name="combine",
-        )(parts.reshape(1024, 2 * width))
+        )(parts.reshape(512, 2 * width))
 
 
 def solution(mesh):

time: 85.2 us -> 87.9 us (1.032)
  the two profiles are of different devices: /device:TPU:16 before, /device:TPU:8 now
where the time goes in v7:
time: 87.9 us; the launch traced here: 87.5 us
  blocking collectives  44.8 us (51%)
  starting transfers between devices  22.8 us (26%)
  waiting for transfers between devices  11.9 us (14%)
  Pallas kernels  5.42 us (6%)
  other arithmetic  1.6 us (2%)
    all_to_all x1, blocking collectives, on_device(): lax.all_to_all(parts.reshape(64, 8, 2 * width), (pair,) + head, split_axi...  23.1 us
    all_gather x1, blocking collectives, on_device(): stale_same = lax.all_gather(stale_own, quad, axis=0, tiled=True)  21.7 us
    all_to_all x1, starting transfers between devices, on_device(): mine = lax.all_to_all(mine, head, split_axis=0, concat_axis=0, tiled=True)  10.3 us
    ppermute x1, waiting for transfers between devices, on_device(): away_q = lax.ppermute(mine[:, :width], pair, swap)  7.36 us
    all_to_all x1, starting transfers between devices, on_device(): lax.all_to_all(fresh_same, quad, split_axis=0, concat_axis=0, tiled=True)  5.85 us
    pallas_call x1, Pallas kernels, on_device(): pl.pallas_call(functools.partial(attend, place=place), out_shape=jax.Shap...  3.86 us
    ppermute x1, starting transfers between devices, on_device(): away_q = lax.ppermute(mine[:, :width], pair, swap)  2.85 us
    all_to_all x1, waiting for transfers between devices, on_device(): lax.all_to_all(fresh_same, quad, split_axis=0, concat_axis=0, tiled=True)  2.66 us
  transfers between devices with their start and end apart: 5, of which 3 were waited for; matrix products, arithmetic and copies ran while one was open for 0% of the time, Pallas kernels for 1%

profile of v7, /device:TPU:8, one launch (start us, length us, event | category | flops | bytes accessed | tf_op | source)
XLA Modules:
  0.0 87.5 jit_solution(106446478505912364)
XLA Ops:
  0.0 1.6 %pad_maximum_fusion = bf16[32,8,384]{2,1,0:T(8,128)(2,1)} fusion(bf16[32,8,128]{2,1,0:T(8,128)(2,1)} %bitcast.20, bf16[32,8,128]{2,1,0:T(8,128)(2,1)} %bitcast.21, bf16[32,8,128]{2,1,0:T(8,128)(2,1)} %bitcast.22), kind=kLoop, calls=%fused_computation | loop fusion | flops 589824 | bytes 393216 | tf_op jit(solution)/shard_map/tokens_to_heads/concatenate | solution.py:119
  1.6 0.0 copy-start
  1.6 0.0 copy-start.1
  1.6 0.0 copy-start.2
  1.6 10.3 %all-to-all-start = ((bf16[32,8,384]{2,1,0:T(8,128)(2,1)}), bf16[32,8,384]{2,1,0:T(8,128)(2,1)S(1)}, u32[]{:S(2)}, u32[]{:S(2)}) async-start(bf16[32,8,384]{2,1,0:T(8,128)(2,1)} %pad_maximum_fusion), calls=%async_computation | async-start | bytes 393216 | tf_op jit(solution)/shard_map/tokens_to_heads/all_to_all | solution.py:120
  11.9 0.0 copy-done
  11.9 0.0 copy-done.1
  12.0 0.0 copy-done.2
  12.0 0.0 copy-done.3
  12.0 0.6 pick_stale.1
  12.6 21.7 %all_gather.3.stale_same = bf16[1024,256]{1,0:T(8,128)(2,1)S(1)} all-gather(bf16[256,256]{1,0:T(8,128)(2,1)S(1)} %pick_stale.1), channel_id=1, replica_groups=mesh['za'=4,'zb'=2,'core'=2,'y'=8,'x'=4] {'za'}, dimensions={0}, use_global_device_ids=true | all-gather | bytes 655360 | tf_op jit(solution)/shard_map/stale/all_gather | solution.py:132
  34.3 0.0 all-to-all-done
  34.4 0.8 broadcast_in_dim.2
  35.2 5.8 %all-to-all-start.1 = ((bf16[4,256,256]{2,1,0:T(8,128)(2,1)}), bf16[4,256,256]{2,1,0:T(8,128)(2,1)S(1)}, u32[]{:S(2)}, u32[]{:S(2)}) async-start(bf16[4,256,256]{2,1,0:T(8,128)(2,1)} %broadcast_in_dim.2), calls=%async_computation.1 | async-start | bytes 1048576 | tf_op jit(solution)/shard_map/gather_keys/all_to_all | solution.py:144
  41.0 1.9 %collective-permute-start = (bf16[1024,256]{1,0:T(8,128)(2,1)S(1)}, bf16[1024,256]{1,0:T(8,128)(2,1)S(1)}, u32[]{:S(2)}, u32[]{:S(2)}) collective-permute-start(bf16[1024,256]{1,0:T(8,128)(2,1)S(1)} %all_gather.3.stale_same), channel_id=1, source_target_pairs={{0,32},{32,0},{1,33},{33,1},{2,34},{34,2},{3,35},{35,3},{4,36},{36... | collective-permute-start | bytes 1572872 | tf_op jit(solution)/shard_map/other_core_stale/ppermute | solution.py:137
  43.0 2.9 %collective-permute-start.1 = (bf16[256,128]{1,0:T(8,128)(2,1)S(1)}, bf16[256,128]{1,0:T(8,128)(2,1)S(1)}, u32[]{:S(2)}, u32[]{:S(2)}) collective-permute-start(bf16[256,128]{1,0:T(8,128)(2,1)S(1)} %slice.7), channel_id=1, source_target_pairs={{0,64},{64,0},{1,65},{65,1},{2,66},{66,2},{3,67},{67,3},{4,68},{68... | collective-permute-start | bytes 196616 | tf_op jit(solution)/shard_map/swap_queries/ppermute | solution.py:140
  45.8 7.4 %collective-permute-done.1.away = bf16[256,128]{1,0:T(8,128)(2,1)S(1)} collective-permute-done((bf16[256,128]{1,0:T(8,128)(2,1)S(1)}, bf16[256,128]{1,0:T(8,128)(2,1)S(1)}, u32[]{:S(2)}, u32[]{:S(2)}) %collective-permute-start.1) | collective-permute-done | bytes 65568 | tf_op jit(solution)/shard_map/swap_queries/ppermute | solution.py:140
  53.2 0.0 collective-permute-done.stale_other
  53.2 2.7 %all-to-all-done.1 = bf16[4,256,256]{2,1,0:T(8,128)(2,1)S(1)} async-done(((bf16[4,256,256]{2,1,0:T(8,128)(2,1)}), bf16[4,256,256]{2,1,0:T(8,128)(2,1)S(1)}, u32[]{:S(2)}, u32[]{:S(2)}) %all-to-all-start.1) | async-done | bytes 524320 | tf_op jit(solution)/shard_map/gather_keys/all_to_all | solution.py:144
  55.9 1.9 %collective-permute-start.2 = (bf16[1024,256]{1,0:T(8,128)(2,1)S(1)}, bf16[1024,256]{1,0:T(8,128)(2,1)S(1)}, u32[]{:S(2)}, u32[]{:S(2)}) collective-permute-start(bf16[1024,256]{1,0:T(8,128)(2,1)S(1)} %bitcast.17), channel_id=1, source_target_pairs={{0,32},{32,0},{1,33},{33,1},{2,34},{34,2},{3,35},{35,3},{4,36},{36... | collective-permute-start | bytes 1572872 | tf_op jit(solution)/shard_map/gather_keys/ppermute | solution.py:147
  57.8 1.9 %collective-permute-done.2.fresh_other = bf16[1024,256]{1,0:T(8,128)(2,1)S(1)} collective-permute-done((bf16[1024,256]{1,0:T(8,128)(2,1)S(1)}, bf16[1024,256]{1,0:T(8,128)(2,1)S(1)}, u32[]{:S(2)}, u32[]{:S(2)}) %collective-permute-start.2) | collective-permute-done | bytes 524320 | tf_op jit(solution)/shard_map/gather_keys/ppermute | solution.py:147
  59.7 3.9 %attend.1 = bf16[512,256]{1,0:T(8,128)(2,1)S(1)} custom-call(s32[4]{0:T(128)S(1)} %copy-done.3, bf16[256,384]{1,0:T(8,128)(2,1)S(1)} %bitcast.16, bf16[256,128]{1,0:T(8,128)(2,1)S(1)} %collective-permute-done.1.away, bf16[1024,256]{1,0:T(8,128)(2,1)S(1)} %bitcast.18, bf16[1024,256]{1,0:T(8,128)(2,1)S(1)} %collective-permute-done.2.fresh_other, ...), custom_call_target="tpu_custom_call" | custom-call | flops 1073741824 | bytes 4194304 | tf_op jit(solution)/shard_map/attend/attend/pallas_call | solution.py:150
  63.5 23.1 %all_to_all.15 = bf16[64,8,256]{2,1,0:T(8,128)(2,1)S(1)} all-to-all(bf16[64,8,256]{2,1,0:T(8,128)(2,1)S(1)} %bitcast.19), channel_id=1, replica_groups=mesh['za'=4,'zb'=2,'core'=2,'y'=8,'x'=4] {'zb','y','x'}, dimensions={0} | all-to-all | bytes 524288 | tf_op jit(solution)/shard_map/heads_to_tokens/all_to_all | solution.py:161
  86.6 0.9 %combine.1 = bf16[8,4096]{1,0:T(8,128)(2,1)} custom-call(bf16[512,256]{1,0:T(8,128)(2,1)S(1)} %bitcast.13), custom_call_target="tpu_custom_call" | custom-call | tf_op jit(solution)/shard_map/heads_to_tokens/combine/pallas_call | solution.py:162
  (3 shorter events, 0.0 us)
Async XLA Ops:
  1.6 10.3 %copy-start = (bf16[2,256,128]{2,1,0:T(8,128)(2,1)S(1)}, bf16[2,256,128]{2,1,0:T(8,128)(2,1)}, u32[]{:S(2)}) copy-start(bf16[2,256,128]{2,1,0:T(8,128)(2,1)} %keys.1) | copy-start | bytes 393220
  1.6 10.3 %copy-start.1 = (bf16[2,256,128]{2,1,0:T(8,128)(2,1)S(1)}, bf16[2,256,128]{2,1,0:T(8,128)(2,1)}, u32[]{:S(2)}) copy-start(bf16[2,256,128]{2,1,0:T(8,128)(2,1)} %values.1) | copy-start | bytes 393220
  1.6 10.3 %copy-start.2 = (s32[4]{0:T(128)S(1)}, s32[4]{0:T(128)}, u32[]{:S(2)}) copy-start(s32[4]{0:T(128)} %steps.1) | copy-start | bytes 52
  1.6 10.4 %copy-start.3 = (s32[4]{0:T(128)S(1)}, s32[4]{0:T(128)}, u32[]{:S(2)}) copy-start(s32[4]{0:T(128)} %lengths.3) | copy-start | bytes 52
  1.6 32.7 %all-to-all-start = ((bf16[32,8,384]{2,1,0:T(8,128)(2,1)}), bf16[32,8,384]{2,1,0:T(8,128)(2,1)S(1)}, u32[]{:S(2)}, u32[]{:S(2)}) async-start(bf16[32,8,384]{2,1,0:T(8,128)(2,1)} %pad_maximum_fusion), calls=%async_computation | async-start | bytes 393216 | tf_op jit(solution)/shard_map/tokens_to_heads/all_to_all | solution.py:120
  35.2 20.7 %all-to-all-start.1 = ((bf16[4,256,256]{2,1,0:T(8,128)(2,1)}), bf16[4,256,256]{2,1,0:T(8,128)(2,1)S(1)}, u32[]{:S(2)}, u32[]{:S(2)}) async-start(bf16[4,256,256]{2,1,0:T(8,128)(2,1)} %broadcast_in_dim.2), calls=%async_computation.1 | async-start | bytes 1048576 | tf_op jit(solution)/shard_map/gather_keys/all_to_all | solution.py:144
  41.0 12.2 %collective-permute-start = (bf16[1024,256]{1,0:T(8,128)(2,1)S(1)}, bf16[1024,256]{1,0:T(8,128)(2,1)S(1)}, u32[]{:S(2)}, u32[]{:S(2)}) collective-permute-start(bf16[1024,256]{1,0:T(8,128)(2,1)S(1)} %all_gather.3.stale_same), channel_id=1, source_target_pairs={{0,32},{32,0},{1,33},{33,1},{2,34},{34,2},{3,35},{35,3},{4,36},{36... | collective-permute-start | bytes 1572872 | tf_op jit(solution)/shard_map/other_core_stale/ppermute | solution.py:137
  43.0 10.2 %collective-permute-start.1 = (bf16[256,128]{1,0:T(8,128)(2,1)S(1)}, bf16[256,128]{1,0:T(8,128)(2,1)S(1)}, u32[]{:S(2)}, u32[]{:S(2)}) collective-permute-start(bf16[256,128]{1,0:T(8,128)(2,1)S(1)} %slice.7), channel_id=1, source_target_pairs={{0,64},{64,0},{1,65},{65,1},{2,66},{66,2},{3,67},{67,3},{4,68},{68... | collective-permute-start | bytes 196616 | tf_op jit(solution)/shard_map/swap_queries/ppermute | solution.py:140
  55.9 3.8 %collective-permute-start.2 = (bf16[1024,256]{1,0:T(8,128)(2,1)S(1)}, bf16[1024,256]{1,0:T(8,128)(2,1)S(1)}, u32[]{:S(2)}, u32[]{:S(2)}) collective-permute-start(bf16[1024,256]{1,0:T(8,128)(2,1)S(1)} %bitcast.17), channel_id=1, source_target_pairs={{0,32},{32,0},{1,33},{33,1},{2,34},{34,2},{3,35},{35,3},{4,36},{36... | collective-permute-start | bytes 1572872 | tf_op jit(solution)/shard_map/gather_keys/ppermute | solution.py:147

commit v8 on v5

--- a/solution.py
+++ b/solution.py
@@ -42,10 +42,22 @@
         out[:, at * width : (at + 1) * width] = jnp.where(older, older_rows, newer_rows).astype(jnp.bfloat16)
 
 
+def pack(out, first, outputs, *stats):
+    outputs = outputs.reshape(32, 8, width)
+    spread = [jnp.broadcast_to(x, (span, width)).reshape(32, 8, width) for x in stats]
+    lane = lax.broadcasted_iota(jnp.int32, (32, 2, width), 2)
+    packed = jnp.zeros((32, 2, width), jnp.float32)
+    for row in range(4):
+        two = slice(2 * row, 2 * row + 2)
+        out[pl.ds(first, 32), row] = outputs[:, two, :].astype(jnp.bfloat16)
+        for i, x in enumerate(spread):
+            packed = jnp.where(lane == 3 * row + i, x[:, two, :], packed)
+    out[pl.ds(first, 32), 4] = packed.astype(jnp.bfloat16)
+
+
 def attend(lengths, queries, fresh, stale, out, *, place):
     za, zb, c = place()
     ends = patch_ends(lengths)
-    lane = lax.broadcasted_iota(jnp.int32, (span, width), 1)
     key_offset = lax.broadcasted_iota(jnp.int32, (span, span), 1)
     row_offset = lax.broadcasted_iota(jnp.int32, (span, 1), 0)
 
@@ -82,21 +94,24 @@
                 jnp.where(is_fresh, 0.0, w).astype(jnp.bfloat16), stale_values, preferred_element_type=jnp.float32
             )
         high = total.astype(jnp.bfloat16).astype(jnp.float32)
-        stats = jnp.where(lane == 0, peak, jnp.where(lane == 1, high, total - high))
-        out[rows, :width] = (summed / total).astype(jnp.bfloat16)
-        out[rows, width:] = stats.astype(jnp.bfloat16)
+        pack(out, at * 32, summed / total, peak, high, total - high)
 
 
 def combine(parts, out):
-    heads = out.shape[1] // width
-    blocks = parts[...].astype(jnp.float32).reshape(4, heads, 8, 2 * width)
-    outputs = blocks[..., :width]
-    peaks = blocks[..., width : width + 1]
-    totals = blocks[..., width + 1 : width + 2] + blocks[..., width + 2 : width + 3]
-    shares = totals * jnp.exp2(peaks - jnp.max(peaks, axis=0, keepdims=True))
-    shares = shares / jnp.sum(shares, axis=0, keepdims=True)
-    joined = jnp.sum(outputs * shares, axis=0)
-    for h in range(heads):
+    stats = [parts[pl.ds(s * 32, 32), 4].astype(jnp.float32) for s in range(4)]
+    joined = []
+    for row in range(4):
+        peaks, totals = [], []
+        for x in stats:
+            peaks.append(x[:, :, 3 * row : 3 * row + 1])
+            totals.append(x[:, :, 3 * row + 1 : 3 * row + 2] + x[:, :, 3 * row + 2 : 3 * row + 3])
+        top = functools.reduce(jnp.maximum, peaks)
+        shares = [t * jnp.exp2(p - top) for t, p in zip(totals, peaks)]
+        whole = functools.reduce(jnp.add, shares)
+        outputs = [parts[pl.ds(s * 32, 32), row].astype(jnp.float32) for s in range(4)]
+        joined.append(functools.reduce(jnp.add, [o * (s / whole) for o, s in zip(outputs, shares)]))
+    joined = jnp.concatenate(joined, axis=1)
+    for h in range(32):
         out[:, h * width : (h + 1) * width] = joined[h].astype(jnp.bfloat16)
 
 
@@ -145,7 +160,7 @@
     with jax.named_scope("attend"):
         parts = pl.pallas_call(
             functools.partial(attend, place=place),
-            out_shape=jax.ShapeDtypeStruct((4 * span, 2 * width), jnp.bfloat16),
+            out_shape=jax.ShapeDtypeStruct((128, 5, 2, width), jnp.bfloat16),
             in_specs=[whole_smem] + [whole_vmem] * 3,
             out_specs=whole_vmem,
             compiler_params=pltpu.CompilerParams(vmem_limit_bytes=24 << 20),
@@ -154,7 +169,7 @@
         )(patch_lengths, queries, fresh, stale)
 
     with jax.named_scope("heads_to_tokens"):
-        parts = lax.all_to_all(parts.reshape(128, 8, 2 * width), (quad,) + head, split_axis=0, concat_axis=0, tiled=True)
+        parts = lax.all_to_all(parts, (quad,) + head, split_axis=0, concat_axis=0, tiled=True)
         return pl.pallas_call(
             combine,
             out_shape=jax.ShapeDtypeStruct((8, 32 * width), jnp.bfloat16),
@@ -162,7 +177,7 @@
             out_specs=whole_vmem,
             compiler_params=small_kernel,
             name="combine",
-        )(parts.reshape(1024, 2 * width))
+        )(parts)
 
 
 def solution(mesh):

time: 85.2 us -> 82.1 us (0.964)
  blocking collectives: 53.4 us -> 49.3 us
  Pallas kernels: 5.83 us -> 6.78 us
    all_to_all x1, blocking collectives: 35 us -> 30.9 us  [on_device(): lax.all_to_all(parts, (quad,) + head, split_axis=0, concat_axis=0, tiled=...]
where the time goes in v8:
time: 82.1 us; the launch traced here: 81.7 us
  blocking collectives  49.3 us (60%)
  starting transfers between devices  20.5 us (25%)
  Pallas kernels  6.78 us (8%)
  waiting for transfers between devices  2.71 us (3%)
  other arithmetic  1.6 us (2%)
    all_to_all x1, blocking collectives, on_device(): lax.all_to_all(parts, (quad,) + head, split_axis=0, concat_axis=0, tiled=...  30.9 us
    all_gather x2, blocking collectives, from_neighbours(): return lax.all_gather(x, (pair, core), axis=0, tiled=True)  18.4 us
    all_to_all x1, starting transfers between devices, on_device(): lax.all_to_all(queries, quad, split_axis=0, concat_axis=0, tiled=True)  10.3 us
    all_to_all x1, starting transfers between devices, on_device(): mine = lax.all_to_all(mine, head, split_axis=0, concat_axis=0, tiled=True)  10.2 us
    pallas_call x1, Pallas kernels, on_device(): pl.pallas_call(functools.partial(attend, place=place), out_shape=jax.Shap...  4.52 us
  transfers between devices with their start and end apart: 2, of which 2 were waited for; matrix products, arithmetic and copies ran while one was open for 0% of the time, Pallas kernels for 1%

profile of v8, /device:TPU:16, one launch (start us, length us, event | category | flops | bytes accessed | tf_op | source)
XLA Modules:
  0.0 81.7 jit_solution(12626916174559173456)
XLA Ops:
  0.0 1.6 %pad_maximum_fusion = bf16[32,8,384]{2,1,0:T(8,128)(2,1)} fusion(bf16[32,8,128]{2,1,0:T(8,128)(2,1)} %bitcast.14, bf16[32,8,128]{2,1,0:T(8,128)(2,1)} %bitcast.15, bf16[32,8,128]{2,1,0:T(8,128)(2,1)} %bitcast.16), kind=kLoop, calls=%fused_computation | loop fusion | flops 589824 | bytes 393216 | tf_op jit(solution)/shard_map/tokens_to_heads/concatenate | solution.py:135
  1.6 0.0 copy-start
  1.6 0.0 copy-start.1
  1.6 0.0 copy-start.2
  1.6 0.0 copy-start.3
  1.6 10.2 %all-to-all-start = ((bf16[32,8,384]{2,1,0:T(8,128)(2,1)}), bf16[32,8,384]{2,1,0:T(8,128)(2,1)S(1)}, u32[]{:S(2)}, u32[]{:S(2)}) async-start(bf16[32,8,384]{2,1,0:T(8,128)(2,1)} %pad_maximum_fusion), calls=%async_computation | async-start | bytes 393216 | tf_op jit(solution)/shard_map/tokens_to_heads/all_to_all | solution.py:136
  11.8 0.0 copy-done
  11.8 0.0 copy-done.1
  11.8 0.0 copy-done.2
  11.8 0.0 copy-done.3
  11.9 0.6 pick_stale.1
  12.5 8.1 %all_gather.6.stale = bf16[1024,256]{1,0:T(8,128)(2,1)S(1)} all-gather(bf16[256,256]{1,0:T(8,128)(2,1)S(1)} %pick_stale.1), channel_id=1, replica_groups=mesh['za'=4,'zb'=2,'core'=2,'y'=8,'x'=4] {'zb','core'}, dimensions={0}, use_global_device_ids=true | all-gather | bytes 655360 | tf_op jit(solution)/shard_map/stale/all_gather | solution.py:129
  20.6 1.3 %all-to-all-done = bf16[32,8,384]{2,1,0:T(8,128)(2,1)S(1)} async-done(((bf16[32,8,384]{2,1,0:T(8,128)(2,1)}), bf16[32,8,384]{2,1,0:T(8,128)(2,1)S(1)}, u32[]{:S(2)}, u32[]{:S(2)}) %all-to-all-start) | async-done | bytes 196640 | tf_op jit(solution)/shard_map/tokens_to_heads/all_to_all | solution.py:136
  21.8 0.7 broadcast_in_dim.2
  22.6 10.3 %all-to-all-start.1 = ((bf16[4,256,128]{2,1,0:T(8,128)(2,1)}), bf16[4,256,128]{2,1,0:T(8,128)(2,1)S(1)}, u32[]{:S(2)}, u32[]{:S(2)}) async-start(bf16[4,256,128]{2,1,0:T(8,128)(2,1)} %broadcast_in_dim.2), calls=%async_computation.1 | async-start | bytes 524288 | tf_op jit(solution)/shard_map/gather_queries/all_to_all | solution.py:154
  32.9 10.4 %all_gather.7.fresh = bf16[1024,256]{1,0:T(8,128)(2,1)S(1)} all-gather(bf16[256,256]{1,0:T(8,128)(2,1)S(1)} %slice.7), channel_id=1, replica_groups=mesh['za'=4,'zb'=2,'core'=2,'y'=8,'x'=4] {'zb','core'}, dimensions={0}, use_global_device_ids=true | all-gather | bytes 655360 | tf_op jit(solution)/shard_map/neighbour_keys/all_gather | solution.py:129
  43.3 1.4 %all-to-all-done.1 = bf16[4,256,128]{2,1,0:T(8,128)(2,1)S(1)} async-done(((bf16[4,256,128]{2,1,0:T(8,128)(2,1)}), bf16[4,256,128]{2,1,0:T(8,128)(2,1)S(1)}, u32[]{:S(2)}, u32[]{:S(2)}) %all-to-all-start.1) | async-done | bytes 262176 | tf_op jit(solution)/shard_map/gather_queries/all_to_all | solution.py:154
  44.7 4.5 %attend.1 = bf16[128,5,2,128]{3,2,1,0:T(2,128)(2,1)S(1)} custom-call(s32[4]{0:T(128)S(1)} %copy-done.3, bf16[1024,128]{1,0:T(8,128)(2,1)S(1)} %bitcast.11, bf16[1024,256]{1,0:T(8,128)(2,1)S(1)} %all_gather.7.fresh, bf16[1024,256]{1,0:T(8,128)(2,1)S(1)} %all_gather.6.stale), custom_call_target="tpu_custom_call" | custom-call | flops 1073741824 | bytes 4194304 | tf_op jit(solution)/shard_map/attend/attend/pallas_call | solution.py:161
  49.2 30.9 %all_to_all.15.parts = bf16[128,5,2,128]{3,2,1,0:T(2,128)(2,1)S(1)} all-to-all(bf16[128,5,2,128]{3,2,1,0:T(2,128)(2,1)S(1)} %attend.1), channel_id=1, replica_groups=mesh['za'=4,'zb'=2,'core'=2,'y'=8,'x'=4] {'za','y','x'}, dimensions={0} | all-to-all | bytes 655360 | tf_op jit(solution)/shard_map/heads_to_tokens/all_to_all | solution.py:172
  80.1 1.6 %combine.1 = bf16[8,4096]{1,0:T(8,128)(2,1)} custom-call(bf16[128,5,2,128]{3,2,1,0:T(2,128)(2,1)S(1)} %all_to_all.15.parts), custom_call_target="tpu_custom_call" | custom-call | tf_op jit(solution)/shard_map/heads_to_tokens/combine/pallas_call | solution.py:173
  (2 shorter events, 0.0 us)
Async XLA Ops:
  1.6 10.2 %copy-start = (bf16[2,256,128]{2,1,0:T(8,128)(2,1)S(1)}, bf16[2,256,128]{2,1,0:T(8,128)(2,1)}, u32[]{:S(2)}) copy-start(bf16[2,256,128]{2,1,0:T(8,128)(2,1)} %keys.1) | copy-start | bytes 393220
  1.6 10.2 %copy-start.1 = (bf16[2,256,128]{2,1,0:T(8,128)(2,1)S(1)}, bf16[2,256,128]{2,1,0:T(8,128)(2,1)}, u32[]{:S(2)}) copy-start(bf16[2,256,128]{2,1,0:T(8,128)(2,1)} %values.1) | copy-start | bytes 393220
  1.6 10.2 %copy-start.2 = (s32[4]{0:T(128)S(1)}, s32[4]{0:T(128)}, u32[]{:S(2)}) copy-start(s32[4]{0:T(128)} %steps.1) | copy-start | bytes 52
  1.6 10.2 %copy-start.3 = (s32[4]{0:T(128)S(1)}, s32[4]{0:T(128)}, u32[]{:S(2)}) copy-start(s32[4]{0:T(128)} %lengths.3) | copy-start | bytes 52
  1.6 20.2 %all-to-all-start = ((bf16[32,8,384]{2,1,0:T(8,128)(2,1)}), bf16[32,8,384]{2,1,0:T(8,128)(2,1)S(1)}, u32[]{:S(2)}, u32[]{:S(2)}) async-start(bf16[32,8,384]{2,1,0:T(8,128)(2,1)} %pad_maximum_fusion), calls=%async_computation | async-start | bytes 393216 | tf_op jit(solution)/shard_map/tokens_to_heads/all_to_all | solution.py:136
  22.6 22.1 %all-to-all-start.1 = ((bf16[4,256,128]{2,1,0:T(8,128)(2,1)}), bf16[4,256,128]{2,1,0:T(8,128)(2,1)S(1)}, u32[]{:S(2)}, u32[]{:S(2)}) async-start(bf16[4,256,128]{2,1,0:T(8,128)(2,1)} %broadcast_in_dim.2), calls=%async_computation.1 | async-start | bytes 524288 | tf_op jit(solution)/shard_map/gather_queries/all_to_all | solution.py:154

commit v9 on v8

--- a/solution.py
+++ b/solution.py
@@ -44,72 +44,97 @@
 
 def pack(out, first, outputs, *stats):
     outputs = outputs.reshape(32, 8, width)
-    spread = [jnp.broadcast_to(x, (span, width)).reshape(32, 8, width) for x in stats]
-    lane = lax.broadcasted_iota(jnp.int32, (32, 2, width), 2)
-    packed = jnp.zeros((32, 2, width), jnp.float32)
+    shape = (32, 8, width)
+    lane = lax.broadcasted_iota(jnp.int32, shape, 2) - 3 * (lax.broadcasted_iota(jnp.int32, shape, 1) // 2)
+    spread = jnp.zeros(shape, jnp.float32)
+    for i, x in enumerate(stats):
+        spread = jnp.where(lane == i, jnp.broadcast_to(x, (span, width)).reshape(shape), spread)
+    packed = spread[:, 0:2] + spread[:, 2:4] + spread[:, 4:6] + spread[:, 6:8]
+    rows = pl.ds(first, 32)
     for row in range(4):
-        two = slice(2 * row, 2 * row + 2)
-        out[pl.ds(first, 32), row] = outputs[:, two, :].astype(jnp.bfloat16)
-        for i, x in enumerate(spread):
-            packed = jnp.where(lane == 3 * row + i, x[:, two, :], packed)
-    out[pl.ds(first, 32), 4] = packed.astype(jnp.bfloat16)
+        out[rows, row] = outputs[:, 2 * row : 2 * row + 2].astype(jnp.bfloat16)
+    out[rows, 4] = packed.astype(jnp.bfloat16)
+
+
+def row_peak(scores):
+    peak = jnp.max(functools.reduce(jnp.maximum, scores), axis=1, keepdims=True) * log2_scale
+    return peak.astype(jnp.bfloat16).astype(jnp.float32)
+
+
+def products(q, keys):
+    return lax.dot_general(q, keys, (((1,), (1,)), ((), ())), preferred_element_type=jnp.float32)
 
 
 def attend(lengths, queries, fresh, stale, out, *, place):
     za, zb, c = place()
     ends = patch_ends(lengths)
-    key_offset = lax.broadcasted_iota(jnp.int32, (span, span), 1)
-    row_offset = lax.broadcasted_iota(jnp.int32, (span, 1), 0)
-
-    blocks = []
-    for at in range(4):
-        rows = pl.ds(at * span, span)
-        blocks.append((fresh[rows, :width], fresh[rows, width:], stale[rows, :width], stale[rows, width:], za * 1024 + at * span))
-
-    for at in range(4):
-        rows = pl.ds(at * span, span)
-        q = queries[rows, :]
-        position = at * 1024 + zb * 512 + c * span + row_offset
-        reach = jnp.full((span, 1), ends[patches - 1], jnp.int32)
+    key_first = za * 1024
+    parts = [pl.ds(at * span, span) for at in range(4)]
+
+    def reach_of(position):
+        reach = ends[patches - 1]
         for m in range(patches - 2, -1, -1):
             reach = jnp.where(position < ends[m], ends[m], reach)
-        scores, fresh_at = [], []
-        for keys, _, stale_keys, _, first in blocks:
-            fresh_scores = lax.dot_general(q, keys, (((1,), (1,)), ((), ())), preferred_element_type=jnp.float32)
-            stale_scores = lax.dot_general(q, stale_keys, (((1,), (1,)), ((), ())), preferred_element_type=jnp.float32)
-            is_fresh = key_offset < reach - first
-            fresh_at.append(is_fresh)
-            scores.append(jnp.where(is_fresh, fresh_scores, stale_scores))
-        peak = functools.reduce(jnp.maximum, scores)
-        peak = jnp.max(peak, axis=1, keepdims=True) * log2_scale
-        peak = peak.astype(jnp.bfloat16).astype(jnp.float32)
+        return reach
+
+    def finish(at, summed, peak, total):
+        high = total.astype(jnp.bfloat16).astype(jnp.float32)
+        pack(out, at * 32, summed / total, peak, high, total - high)
+
+    def one_version(at, rows):
+        q = queries[parts[at], :]
+        scores = [products(q, rows[part, :width]) for part in parts]
+        peak = row_peak(scores)
         weights = [jnp.exp2(s * log2_scale - peak) for s in scores]
         total = jnp.sum(functools.reduce(jnp.add, weights), axis=1, keepdims=True)
         summed = jnp.zeros((span, width), jnp.float32)
-        for w, is_fresh, (_, values, _, stale_values, _) in zip(weights, fresh_at, blocks):
-            summed += jnp.dot(
-                jnp.where(is_fresh, w, 0.0).astype(jnp.bfloat16), values, preferred_element_type=jnp.float32
-            )
-            summed += jnp.dot(
-                jnp.where(is_fresh, 0.0, w).astype(jnp.bfloat16), stale_values, preferred_element_type=jnp.float32
-            )
-        high = total.astype(jnp.bfloat16).astype(jnp.float32)
-        pack(out, at * 32, summed / total, peak, high, total - high)
+        for w, part in zip(weights, parts):
+            summed += jnp.dot(w.astype(jnp.bfloat16), rows[part, width:], preferred_element_type=jnp.float32)
+        finish(at, summed, peak, total)
+
+    def both_versions(at, query_first):
+        q = queries[parts[at], :]
+        reach = reach_of(query_first + lax.broadcasted_iota(jnp.int32, (span, 1), 0))
+        offset = lax.broadcasted_iota(jnp.int32, (span, span), 1)
+        scores, fresh_at = [], []
+        for index, part in enumerate(parts):
+            is_fresh = offset < reach - (key_first + index * span)
+            fresh_at.append(is_fresh)
+            scores.append(jnp.where(is_fresh, products(q, fresh[part, :width]), products(q, stale[part, :width])))
+        peak = row_peak(scores)
+        weights = [jnp.exp2(s * log2_scale - peak) for s in scores]
+        total = jnp.sum(functools.reduce(jnp.add, weights), axis=1, keepdims=True)
+        summed = jnp.zeros((span, width), jnp.float32)
+        for w, is_fresh, part in zip(weights, fresh_at, parts):
+            for version, kept in ((fresh, jnp.where(is_fresh, w, 0.0)), (stale, jnp.where(is_fresh, 0.0, w))):
+                summed += jnp.dot(kept.astype(jnp.bfloat16), version[part, width:], preferred_element_type=jnp.float32)
+        finish(at, summed, peak, total)
+
+    for at in range(4):
+        query_first = at * 1024 + zb * 512 + c * span
+        all_fresh = reach_of(query_first) >= key_first + 1024
+        all_stale = reach_of(query_first + span - 1) <= key_first
+        pl.when(all_fresh)(functools.partial(one_version, at, fresh))
+        pl.when(all_stale)(functools.partial(one_version, at, stale))
+        pl.when(jnp.logical_not(jnp.logical_or(all_fresh, all_stale)))(functools.partial(both_versions, at, query_first))
 
 
 def combine(parts, out):
-    stats = [parts[pl.ds(s * 32, 32), 4].astype(jnp.float32) for s in range(4)]
+    peaks, totals = [], []
+    for s in range(4):
+        stats = parts[pl.ds(s * 32, 32), 4].astype(jnp.float32)
+        peaks.append(stats)
+        totals.append(pltpu.roll(stats, width - 1, 2) + pltpu.roll(stats, width - 2, 2))
+    top = functools.reduce(jnp.maximum, peaks)
+    shares = [t * jnp.exp2(p - top) for t, p in zip(totals, peaks)]
+    scale = 1.0 / functools.reduce(jnp.add, shares)
+    shares = [s * scale for s in shares]
     joined = []
     for row in range(4):
-        peaks, totals = [], []
-        for x in stats:
-            peaks.append(x[:, :, 3 * row : 3 * row + 1])
-            totals.append(x[:, :, 3 * row + 1 : 3 * row + 2] + x[:, :, 3 * row + 2 : 3 * row + 3])
-        top = functools.reduce(jnp.maximum, peaks)
-        shares = [t * jnp.exp2(p - top) for t, p in zip(totals, peaks)]
-        whole = functools.reduce(jnp.add, shares)
-        outputs = [parts[pl.ds(s * 32, 32), row].astype(jnp.float32) for s in range(4)]
-        joined.append(functools.reduce(jnp.add, [o * (s / whole) for o, s in zip(outputs, shares)]))
+        terms = [
+            parts[pl.ds(s * 32, 32), row].astype(jnp.float32) * shares[s][:, :, 3 * row : 3 * row + 1] for s in range(4)
+        ]
+        joined.append(functools.reduce(jnp.add, terms))
     joined = jnp.concatenate(joined, axis=1)
     for h in range(32):
         out[:, h * width : (h + 1) * width] = joined[h].astype(jnp.bfloat16)

time: 82.1 us -> 80.9 us (0.985)
  Pallas kernels: 6.78 us -> 5.58 us
    pallas_call x1, Pallas kernels: 4.52 us -> 3.38 us  [on_device(): pl.pallas_call(functools.partial(attend, place=place), out_shape=jax.Shap...]
where the time goes in v9:
time: 80.9 us; the launch traced here: 80.5 us
  blocking collectives  49.3 us (61%)
  starting transfers between devices  20.5 us (25%)
  Pallas kernels  5.58 us (7%)
  waiting for transfers between devices  2.71 us (3%)
  other arithmetic  1.6 us (2%)
    all_to_all x1, blocking collectives, on_device(): lax.all_to_all(parts, (quad,) + head, split_axis=0, concat_axis=0, tiled=...  30.8 us
    all_gather x2, blocking collectives, from_neighbours(): return lax.all_gather(x, (pair, core), axis=0, tiled=True)  18.4 us
    all_to_all x1, starting transfers between devices, on_device(): lax.all_to_all(queries, quad, split_axis=0, concat_axis=0, tiled=True)  10.3 us
    all_to_all x1, starting transfers between devices, on_device(): mine = lax.all_to_all(mine, head, split_axis=0, concat_axis=0, tiled=True)  10.2 us
    pallas_call x1, Pallas kernels, on_device(): pl.pallas_call(functools.partial(attend, place=place), out_shape=jax.Shap...  3.38 us
  transfers between devices with their start and end apart: 2, of which 2 were waited for; matrix products, arithmetic and copies ran while one was open for 0% of the time, Pallas kernels for 1%

profile of v9, /device:TPU:16, one launch (start us, length us, event | category | flops | bytes accessed | tf_op | source)
XLA Modules:
  0.0 80.5 jit_solution(11639577103949897326)
XLA Ops:
  0.0 1.6 %pad_maximum_fusion = bf16[32,8,384]{2,1,0:T(8,128)(2,1)} fusion(bf16[32,8,128]{2,1,0:T(8,128)(2,1)} %bitcast.14, bf16[32,8,128]{2,1,0:T(8,128)(2,1)} %bitcast.15, bf16[32,8,128]{2,1,0:T(8,128)(2,1)} %bitcast.16), kind=kLoop, calls=%fused_computation | loop fusion | flops 589824 | bytes 393216 | tf_op jit(solution)/shard_map/tokens_to_heads/concatenate | solution.py:160
  1.6 0.0 copy-start
  1.6 0.0 copy-start.1
  1.6 0.0 copy-start.2
  1.6 0.0 copy-start.3
  1.6 10.2 %all-to-all-start = ((bf16[32,8,384]{2,1,0:T(8,128)(2,1)}), bf16[32,8,384]{2,1,0:T(8,128)(2,1)S(1)}, u32[]{:S(2)}, u32[]{:S(2)}) async-start(bf16[32,8,384]{2,1,0:T(8,128)(2,1)} %pad_maximum_fusion), calls=%async_computation | async-start | bytes 393216 | tf_op jit(solution)/shard_map/tokens_to_heads/all_to_all | solution.py:161
  11.8 0.0 copy-done
  11.8 0.0 copy-done.1
  11.8 0.0 copy-done.2
  11.8 0.0 copy-done.3
  11.9 0.6 pick_stale.1
  12.5 8.1 %all_gather.6.stale = bf16[1024,256]{1,0:T(8,128)(2,1)S(1)} all-gather(bf16[256,256]{1,0:T(8,128)(2,1)S(1)} %pick_stale.1), channel_id=1, replica_groups=mesh['za'=4,'zb'=2,'core'=2,'y'=8,'x'=4] {'zb','core'}, dimensions={0}, use_global_device_ids=true | all-gather | bytes 655360 | tf_op jit(solution)/shard_map/stale/all_gather | solution.py:154
  20.6 1.3 %all-to-all-done = bf16[32,8,384]{2,1,0:T(8,128)(2,1)S(1)} async-done(((bf16[32,8,384]{2,1,0:T(8,128)(2,1)}), bf16[32,8,384]{2,1,0:T(8,128)(2,1)S(1)}, u32[]{:S(2)}, u32[]{:S(2)}) %all-to-all-start) | async-done | bytes 196640 | tf_op jit(solution)/shard_map/tokens_to_heads/all_to_all | solution.py:161
  21.8 0.7 broadcast_in_dim.2
  22.6 10.3 %all-to-all-start.1 = ((bf16[4,256,128]{2,1,0:T(8,128)(2,1)}), bf16[4,256,128]{2,1,0:T(8,128)(2,1)S(1)}, u32[]{:S(2)}, u32[]{:S(2)}) async-start(bf16[4,256,128]{2,1,0:T(8,128)(2,1)} %broadcast_in_dim.2), calls=%async_computation.1 | async-start | bytes 524288 | tf_op jit(solution)/shard_map/gather_queries/all_to_all | solution.py:179
  32.9 10.4 %all_gather.7.fresh = bf16[1024,256]{1,0:T(8,128)(2,1)S(1)} all-gather(bf16[256,256]{1,0:T(8,128)(2,1)S(1)} %slice.7), channel_id=1, replica_groups=mesh['za'=4,'zb'=2,'core'=2,'y'=8,'x'=4] {'zb','core'}, dimensions={0}, use_global_device_ids=true | all-gather | bytes 655360 | tf_op jit(solution)/shard_map/neighbour_keys/all_gather | solution.py:154
  43.3 1.4 %all-to-all-done.1 = bf16[4,256,128]{2,1,0:T(8,128)(2,1)S(1)} async-done(((bf16[4,256,128]{2,1,0:T(8,128)(2,1)}), bf16[4,256,128]{2,1,0:T(8,128)(2,1)S(1)}, u32[]{:S(2)}, u32[]{:S(2)}) %all-to-all-start.1) | async-done | bytes 262176 | tf_op jit(solution)/shard_map/gather_queries/all_to_all | solution.py:179
  44.7 3.4 %attend.1 = bf16[128,5,2,128]{3,2,1,0:T(2,128)(2,1)S(1)} custom-call(s32[4]{0:T(128)S(1)} %copy-done.3, bf16[1024,128]{1,0:T(8,128)(2,1)S(1)} %bitcast.11, bf16[1024,256]{1,0:T(8,128)(2,1)S(1)} %all_gather.7.fresh, bf16[1024,256]{1,0:T(8,128)(2,1)S(1)} %all_gather.6.stale), custom_call_target="tpu_custom_call" | custom-call | flops 1073741824 | bytes 4194304 | tf_op jit(solution)/shard_map/attend/attend/pallas_call | solution.py:186
  48.1 30.8 %all_to_all.15.parts = bf16[128,5,2,128]{3,2,1,0:T(2,128)(2,1)S(1)} all-to-all(bf16[128,5,2,128]{3,2,1,0:T(2,128)(2,1)S(1)} %attend.1), channel_id=1, replica_groups=mesh['za'=4,'zb'=2,'core'=2,'y'=8,'x'=4] {'za','y','x'}, dimensions={0} | all-to-all | bytes 655360 | tf_op jit(solution)/shard_map/heads_to_tokens/all_to_all | solution.py:197
  78.9 1.6 %combine.1 = bf16[8,4096]{1,0:T(8,128)(2,1)} custom-call(bf16[128,5,2,128]{3,2,1,0:T(2,128)(2,1)S(1)} %all_to_all.15.parts), custom_call_target="tpu_custom_call" | custom-call | tf_op jit(solution)/shard_map/heads_to_tokens/combine/pallas_call | solution.py:198
  (2 shorter events, 0.0 us)
Async XLA Ops:
  1.6 10.2 %copy-start = (bf16[2,256,128]{2,1,0:T(8,128)(2,1)S(1)}, bf16[2,256,128]{2,1,0:T(8,128)(2,1)}, u32[]{:S(2)}) copy-start(bf16[2,256,128]{2,1,0:T(8,128)(2,1)} %keys.1) | copy-start | bytes 393220
  1.6 10.2 %copy-start.1 = (bf16[2,256,128]{2,1,0:T(8,128)(2,1)S(1)}, bf16[2,256,128]{2,1,0:T(8,128)(2,1)}, u32[]{:S(2)}) copy-start(bf16[2,256,128]{2,1,0:T(8,128)(2,1)} %values.1) | copy-start | bytes 393220
  1.6 10.2 %copy-start.2 = (s32[4]{0:T(128)S(1)}, s32[4]{0:T(128)}, u32[]{:S(2)}) copy-start(s32[4]{0:T(128)} %steps.1) | copy-start | bytes 52
  1.6 10.2 %copy-start.3 = (s32[4]{0:T(128)S(1)}, s32[4]{0:T(128)}, u32[]{:S(2)}) copy-start(s32[4]{0:T(128)} %lengths.3) | copy-start | bytes 52
  1.6 20.2 %all-to-all-start = ((bf16[32,8,384]{2,1,0:T(8,128)(2,1)}), bf16[32,8,384]{2,1,0:T(8,128)(2,1)S(1)}, u32[]{:S(2)}, u32[]{:S(2)}) async-start(bf16[32,8,384]{2,1,0:T(8,128)(2,1)} %pad_maximum_fusion), calls=%async_computation | async-start | bytes 393216 | tf_op jit(solution)/shard_map/tokens_to_heads/all_to_all | solution.py:161
  22.6 22.1 %all-to-all-start.1 = ((bf16[4,256,128]{2,1,0:T(8,128)(2,1)}), bf16[4,256,128]{2,1,0:T(8,128)(2,1)S(1)}, u32[]{:S(2)}, u32[]{:S(2)}) async-start(bf16[4,256,128]{2,1,0:T(8,128)(2,1)} %broadcast_in_dim.2), calls=%async_computation.1 | async-start | bytes 524288 | tf_op jit(solution)/shard_map/gather_queries/all_to_all | solution.py:179

commit v10 on v9

--- a/solution.py
+++ b/solution.py
@@ -65,11 +65,19 @@
     return lax.dot_general(q, keys, (((1,), (1,)), ((), ())), preferred_element_type=jnp.float32)
 
 
-def attend(lengths, queries, fresh, stale, out, *, place):
+def attend(lengths, queries, fresh, stale, *outs, place, aheads):
+    for ahead, out in zip(aheads, outs):
+        attend_block(lengths, queries, fresh, stale, out, place=place, ahead=ahead)
+
+
+def attend_block(lengths, queries, fresh, stale, out, *, place, ahead):
     za, zb, c = place()
     ends = patch_ends(lengths)
     key_first = za * 1024
     parts = [pl.ds(at * span, span) for at in range(4)]
+    owner = lax.rem(za + ahead, 4)
+    query_first = owner * 1024 + zb * 512 + c * span
+    query_rows = pl.ds(pl.multiple_of(owner * span, span), span)
 
     def reach_of(position):
         reach = ends[patches - 1]
@@ -77,12 +85,12 @@
             reach = jnp.where(position < ends[m], ends[m], reach)
         return reach
 
-    def finish(at, summed, peak, total):
+    def finish(summed, peak, total):
         high = total.astype(jnp.bfloat16).astype(jnp.float32)
-        pack(out, at * 32, summed / total, peak, high, total - high)
-
-    def one_version(at, rows):
-        q = queries[parts[at], :]
+        pack(out, 0, summed / total, peak, high, total - high)
+
+    def one_version(rows):
+        q = queries[query_rows, :]
         scores = [products(q, rows[part, :width]) for part in parts]
         peak = row_peak(scores)
         weights = [jnp.exp2(s * log2_scale - peak) for s in scores]
@@ -90,10 +98,10 @@
         summed = jnp.zeros((span, width), jnp.float32)
         for w, part in zip(weights, parts):
             summed += jnp.dot(w.astype(jnp.bfloat16), rows[part, width:], preferred_element_type=jnp.float32)
-        finish(at, summed, peak, total)
-
-    def both_versions(at, query_first):
-        q = queries[parts[at], :]
+        finish(summed, peak, total)
+
+    def both_versions():
+        q = queries[query_rows, :]
         reach = reach_of(query_first + lax.broadcasted_iota(jnp.int32, (span, 1), 0))
         offset = lax.broadcasted_iota(jnp.int32, (span, span), 1)
         scores, fresh_at = [], []
@@ -108,21 +116,20 @@
         for w, is_fresh, part in zip(weights, fresh_at, parts):
             for version, kept in ((fresh, jnp.where(is_fresh, w, 0.0)), (stale, jnp.where(is_fresh, 0.0, w))):
                 summed += jnp.dot(kept.astype(jnp.bfloat16), version[part, width:], preferred_element_type=jnp.float32)
-        finish(at, summed, peak, total)
-
-    for at in range(4):
-        query_first = at * 1024 + zb * 512 + c * span
-        all_fresh = reach_of(query_first) >= key_first + 1024
-        all_stale = reach_of(query_first + span - 1) <= key_first
-        pl.when(all_fresh)(functools.partial(one_version, at, fresh))
-        pl.when(all_stale)(functools.partial(one_version, at, stale))
-        pl.when(jnp.logical_not(jnp.logical_or(all_fresh, all_stale)))(functools.partial(both_versions, at, query_first))
-
-
-def combine(parts, out):
+        finish(summed, peak, total)
+
+    all_fresh = reach_of(query_first) >= key_first + 1024
+    all_stale = reach_of(query_first + span - 1) <= key_first
+    pl.when(all_fresh)(functools.partial(one_version, fresh))
+    pl.when(all_stale)(functools.partial(one_version, stale))
+    pl.when(jnp.logical_not(jnp.logical_or(all_fresh, all_stale)))(both_versions)
+
+
+def combine(*refs):
+    parts, out = refs[:4], refs[4]
     peaks, totals = [], []
-    for s in range(4):
-        stats = parts[pl.ds(s * 32, 32), 4].astype(jnp.float32)
+    for part in parts:
+        stats = part[:, 4].astype(jnp.float32)
         peaks.append(stats)
         totals.append(pltpu.roll(stats, width - 1, 2) + pltpu.roll(stats, width - 2, 2))
     top = functools.reduce(jnp.maximum, peaks)
@@ -131,13 +138,9 @@
     shares = [s * scale for s in shares]
     joined = []
     for row in range(4):
-        terms = [
-            parts[pl.ds(s * 32, 32), row].astype(jnp.float32) * shares[s][:, :, 3 * row : 3 * row + 1] for s in range(4)
-        ]
+        terms = [part[:, row].astype(jnp.float32) * s[:, :, 3 * row : 3 * row + 1] for part, s in zip(parts, shares)]
         joined.append(functools.reduce(jnp.add, terms))
-    joined = jnp.concatenate(joined, axis=1)
-    for h in range(32):
-        out[:, h * width : (h + 1) * width] = joined[h].astype(jnp.bfloat16)
+    out[...] = jnp.concatenate(joined, axis=1).astype(jnp.bfloat16)
 
 
 def on_device(query, key, value, stale_key, stale_value, patch_lengths, stale_step):
@@ -182,27 +185,40 @@
     with jax.named_scope("neighbour_keys"):
         fresh = from_neighbours(mine[:, width:])
 
-    with jax.named_scope("attend"):
-        parts = pl.pallas_call(
-            functools.partial(attend, place=place),
-            out_shape=jax.ShapeDtypeStruct((128, 5, 2, width), jnp.bfloat16),
+    def attend_for(*aheads):
+        return pl.pallas_call(
+            functools.partial(attend, place=place, aheads=aheads),
+            out_shape=[jax.ShapeDtypeStruct((32, 5, 2, width), jnp.bfloat16)] * len(aheads),
             in_specs=[whole_smem] + [whole_vmem] * 3,
-            out_specs=whole_vmem,
-            compiler_params=pltpu.CompilerParams(vmem_limit_bytes=24 << 20),
-            cost_estimate=pl.CostEstimate(flops=2 * 2 * 512 * 4096 * 128, bytes_accessed=4 << 20, transcendentals=1 << 20),
+            out_specs=[whole_vmem] * len(aheads),
+            compiler_params=pltpu.CompilerParams(vmem_limit_bytes=16 << 20),
+            cost_estimate=pl.CostEstimate(
+                flops=len(aheads) * 2 * 2 * 256 * 2048 * 128, bytes_accessed=2 << 20, transcendentals=len(aheads) << 18
+            ),
             name="attend",
         )(patch_lengths, queries, fresh, stale)
 
-    with jax.named_scope("heads_to_tokens"):
-        parts = lax.all_to_all(parts, (quad,) + head, split_axis=0, concat_axis=0, tiled=True)
-        return pl.pallas_call(
+    with jax.named_scope("attend_and_send"):
+        away = (2, 1, 3)
+        parts = [
+            lax.ppermute(block, quad, [(i, (i + ahead) % 4) for i in range(4)])
+            for ahead, block in zip(away, attend_for(*away))
+        ]
+        parts += attend_for(0)
+
+    with jax.named_scope("join_partials"):
+        joined = pl.pallas_call(
             combine,
-            out_shape=jax.ShapeDtypeStruct((8, 32 * width), jnp.bfloat16),
-            in_specs=[whole_vmem],
+            out_shape=jax.ShapeDtypeStruct((32, 8, width), jnp.bfloat16),
+            in_specs=[whole_vmem] * 4,
             out_specs=whole_vmem,
             compiler_params=small_kernel,
             name="combine",
-        )(parts)
+        )(*parts)
+
+    with jax.named_scope("heads_to_tokens"):
+        joined = lax.all_to_all(joined, head, split_axis=0, concat_axis=0, tiled=True)
+        return jnp.transpose(joined, (1, 0, 2)).reshape(8, 32 * width)
 
 
 def solution(mesh):

time: 80.9 us -> 84.5 us (1.044)
  the two profiles are of different devices: /device:TPU:16 before, /device:TPU:8 now
where the time goes in v10:
time: 84.5 us; the launch traced here: 84.1 us
  blocking collectives  34.7 us (41%)
  starting transfers between devices  33.6 us (40%)
  waiting for transfers between devices  7.03 us (8%)
  Pallas kernels  5.6 us (7%)
  other arithmetic  1.61 us (2%)
  local copies, waits for them, and re-layouts  1.4 us (2%)
    all_gather x2, blocking collectives, from_neighbours(): return lax.all_gather(x, (pair, core), axis=0, tiled=True)  17.6 us
    all_to_all x1, blocking collectives, on_device(): lax.all_to_all(joined, head, split_axis=0, concat_axis=0, tiled=True)  17.1 us
    ppermute x3, starting transfers between devices, on_device(): lax.ppermute(block, quad, [(i, (i + ahead) % 4) for i in range(4)])  13 us
    all_to_all x1, starting transfers between devices, on_device(): mine = lax.all_to_all(mine, head, split_axis=0, concat_axis=0, tiled=True)  10.3 us
    all_to_all x1, starting transfers between devices, on_device(): lax.all_to_all(queries, quad, split_axis=0, concat_axis=0, tiled=True)  10.3 us
    pallas_call x2, Pallas kernels, attend_for(): pl.pallas_call(functools.partial(attend, place=place, aheads=aheads), out...  3.95 us
    ppermute x3, waiting for transfers between devices, on_device(): lax.ppermute(block, quad, [(i, (i + ahead) % 4) for i in range(4)])  2.71 us
    all_to_all x1, waiting for transfers between devices, on_device(): lax.all_to_all(queries, quad, split_axis=0, concat_axis=0, tiled=True)  2.19 us
  transfers between devices with their start and end apart: 5, of which 3 were waited for; matrix products, arithmetic and copies ran while one was open for 0% of the time, Pallas kernels for 2%

profile of v10, /device:TPU:8, one launch (start us, length us, event | category | flops | bytes accessed | tf_op | source)
XLA Modules:
  0.0 84.1 jit_solution(4002982902486881104)
XLA Ops:
  0.0 1.6 %pad_maximum_fusion = bf16[32,8,384]{2,1,0:T(8,128)(2,1)} fusion(bf16[32,8,128]{2,1,0:T(8,128)(2,1)} %bitcast.19, bf16[32,8,128]{2,1,0:T(8,128)(2,1)} %bitcast.20, bf16[32,8,128]{2,1,0:T(8,128)(2,1)} %bitcast.21), kind=kLoop, calls=%fused_computation | loop fusion | flops 589824 | bytes 393216 | tf_op jit(solution)/shard_map/tokens_to_heads/concatenate | solution.py:163
  1.6 10.3 %all-to-all-start = ((bf16[32,8,384]{2,1,0:T(8,128)(2,1)}), bf16[32,8,384]{2,1,0:T(8,128)(2,1)S(1)}, u32[]{:S(2)}, u32[]{:S(2)}) async-start(bf16[32,8,384]{2,1,0:T(8,128)(2,1)} %pad_maximum_fusion), calls=%async_computation | async-start | bytes 393216 | tf_op jit(solution)/shard_map/tokens_to_heads/all_to_all | solution.py:164
  11.9 0.0 copy-done
  11.9 0.0 copy-done.1
  12.0 0.0 copy-done.2
  12.0 0.0 copy-done.3
  12.0 0.6 pick_stale.1
  12.6 8.1 %all_gather.6.stale = bf16[1024,256]{1,0:T(8,128)(2,1)S(1)} all-gather(bf16[256,256]{1,0:T(8,128)(2,1)S(1)} %pick_stale.1), channel_id=1, replica_groups=mesh['za'=4,'zb'=2,'core'=2,'y'=8,'x'=4] {'zb','core'}, dimensions={0}, use_global_device_ids=true | all-gather | bytes 655360 | tf_op jit(solution)/shard_map/stale/all_gather | solution.py:157
  20.7 2.1 %all-to-all-done = bf16[32,8,384]{2,1,0:T(8,128)(2,1)S(1)} async-done(((bf16[32,8,384]{2,1,0:T(8,128)(2,1)}), bf16[32,8,384]{2,1,0:T(8,128)(2,1)S(1)}, u32[]{:S(2)}, u32[]{:S(2)}) %all-to-all-start) | async-done | bytes 196640 | tf_op jit(solution)/shard_map/tokens_to_heads/all_to_all | solution.py:164
  22.8 0.7 broadcast_in_dim.2
  23.6 10.3 %all-to-all-start.1 = ((bf16[4,256,128]{2,1,0:T(8,128)(2,1)}), bf16[4,256,128]{2,1,0:T(8,128)(2,1)S(1)}, u32[]{:S(2)}, u32[]{:S(2)}) async-start(bf16[4,256,128]{2,1,0:T(8,128)(2,1)} %broadcast_in_dim.2), calls=%async_computation.1 | async-start | bytes 524288 | tf_op jit(solution)/shard_map/gather_queries/all_to_all | solution.py:182
  33.9 9.6 %all_gather.7.fresh = bf16[1024,256]{1,0:T(8,128)(2,1)S(1)} all-gather(bf16[256,256]{1,0:T(8,128)(2,1)S(1)} %slice.7), channel_id=1, replica_groups=mesh['za'=4,'zb'=2,'core'=2,'y'=8,'x'=4] {'zb','core'}, dimensions={0}, use_global_device_ids=true | all-gather | bytes 655360 | tf_op jit(solution)/shard_map/neighbour_keys/all_gather | solution.py:157
  43.4 2.2 %all-to-all-done.1 = bf16[4,256,128]{2,1,0:T(8,128)(2,1)S(1)} async-done(((bf16[4,256,128]{2,1,0:T(8,128)(2,1)}), bf16[4,256,128]{2,1,0:T(8,128)(2,1)S(1)}, u32[]{:S(2)}, u32[]{:S(2)}) %all-to-all-start.1) | async-done | bytes 262176 | tf_op jit(solution)/shard_map/gather_queries/all_to_all | solution.py:182
  45.6 2.7 %attend.2 = (bf16[32,5,2,128]{3,2,1,0:T(2,128)(2,1)S(1)}, bf16[32,5,2,128]{3,2,1,0:T(2,128)(2,1)S(1)}, bf16[32,5,2,128]{3,2,1,0:T(2,128)(2,1)S(1)}) custom-call(s32[4]{0:T(128)S(1)} %copy-done.2, bf16[1024,128]{1,0:T(8,128)(2,1)S(1)} %bitcast.14, bf16[1024,256]{1,0:T(8,128)(2,1)S(1)} %all_gather.7.fresh, bf16[1024,256]{1,0:T(8,128)(2,1)S(1)} %all_gather.6.stale), custom_call_target="tpu_custom_call" | custom-call | flops 805306368 | bytes 2097152 | tf_op jit(solution)/shard_map/attend_and_send/attend/pallas_call | solution.py:189
  48.3 5.1 %collective-permute-start = (bf16[32,5,2,128]{3,2,1,0:T(2,128)(2,1)S(1)}, bf16[32,5,2,128]{3,2,1,0:T(2,128)(2,1)S(1)}, u32[]{:S(2)}, u32[]{:S(2)}) collective-permute-start(bf16[32,5,2,128]{3,2,1,0:T(2,128)(2,1)S(1)} %get-tuple-element.12), channel_id=1, source_target_pairs={{0,256},{128,384},{256,0},{384,128},{1,257},{129,385},{257,1},{385... | collective-permute-start | bytes 245768 | tf_op jit(solution)/shard_map/attend_and_send/ppermute | solution.py:204
  53.4 2.9 %collective-permute-start.1 = (bf16[32,5,2,128]{3,2,1,0:T(2,128)(2,1)S(1)}, bf16[32,5,2,128]{3,2,1,0:T(2,128)(2,1)S(1)}, u32[]{:S(2)}, u32[]{:S(2)}) collective-permute-start(bf16[32,5,2,128]{3,2,1,0:T(2,128)(2,1)S(1)} %get-tuple-element.13), channel_id=1, source_target_pairs={{0,128},{128,256},{256,384},{384,0},{1,129},{129,257},{257,385},{3... | collective-permute-start | bytes 245768 | tf_op jit(solution)/shard_map/attend_and_send/ppermute | solution.py:204
  56.3 5.1 %collective-permute-start.2 = (bf16[32,5,2,128]{3,2,1,0:T(2,128)(2,1)S(1)}, bf16[32,5,2,128]{3,2,1,0:T(2,128)(2,1)S(1)}, u32[]{:S(2)}, u32[]{:S(2)}) collective-permute-start(bf16[32,5,2,128]{3,2,1,0:T(2,128)(2,1)S(1)} %get-tuple-element.14), channel_id=1, source_target_pairs={{0,384},{128,0},{256,128},{384,256},{1,385},{129,1},{257,129},{385... | collective-permute-start | bytes 245768 | tf_op jit(solution)/shard_map/attend_and_send/ppermute | solution.py:204
  61.4 1.3 %attend.3.refs_3_ = bf16[32,5,2,128]{3,2,1,0:T(2,128)(2,1)S(1)} custom-call(s32[4]{0:T(128)S(1)} %copy-done.2, bf16[1024,128]{1,0:T(8,128)(2,1)S(1)} %bitcast.15, bf16[1024,256]{1,0:T(8,128)(2,1)S(1)} %all_gather.7.fresh, bf16[1024,256]{1,0:T(8,128)(2,1)S(1)} %all_gather.6.stale), custom_call_target="tpu_custom_call" | custom-call | flops 268435456 | bytes 2097152 | tf_op jit(solution)/shard_map/attend_and_send/attend/pallas_call | solution.py:189
  62.6 0.0 collective-permute-done.refs_0_
  62.6 0.0 collective-permute-done.1.refs_1_
  62.7 2.7 %collective-permute-done.2.refs_2_ = bf16[32,5,2,128]{3,2,1,0:T(2,128)(2,1)S(1)} collective-permute-done((bf16[32,5,2,128]{3,2,1,0:T(2,128)(2,1)S(1)}, bf16[32,5,2,128]{3,2,1,0:T(2,128)(2,1)S(1)}, u32[]{:S(2)}, u32[]{:S(2)}) %collective-permute-start.2) | collective-permute-done | bytes 81952 | tf_op jit(solution)/shard_map/attend_and_send/ppermute | solution.py:204
  65.4 1.0 %combine.1 = bf16[32,8,128]{2,1,0:T(8,128)(2,1)S(1)} custom-call(bf16[32,5,2,128]{3,2,1,0:T(2,128)(2,1)S(1)} %collective-permute-done.refs_0_, bf16[32,5,2,128]{3,2,1,0:T(2,128)(2,1)S(1)} %collective-permute-done.1.refs_1_, bf16[32,5,2,128]{3,2,1,0:T(2,128)(2,1)S(1)} %collective-permute-done.2.refs_2_, bf16[32,5,2,128]{3,2,1,0:T(2,128)(2,1)S(1)} %attend.3.refs_3_), custom_call_target="tpu_custom_call" | custom-call | tf_op jit(solution)/shard_map/join_partials/combine/pallas_call | solution.py:210
  66.4 17.1 %all_to_all.15 = bf16[32,8,128]{2,1,0:T(8,128)(2,1)S(1)} all-to-all(bf16[32,8,128]{2,1,0:T(8,128)(2,1)S(1)} %combine.1), channel_id=1, replica_groups=mesh['za'=4,'zb'=2,'core'=2,'y'=8,'x'=4] {'y','x'}, dimensions={0} | all-to-all | bytes 131072 | tf_op jit(solution)/shard_map/heads_to_tokens/all_to_all | solution.py:220
  83.5 0.6 copy.9
  (6 shorter events, 0.0 us)
Async XLA Ops:
  1.6 10.3 %copy-start = (bf16[2,256,128]{2,1,0:T(8,128)(2,1)S(1)}, bf16[2,256,128]{2,1,0:T(8,128)(2,1)}, u32[]{:S(2)}) copy-start(bf16[2,256,128]{2,1,0:T(8,128)(2,1)} %keys.1) | copy-start | bytes 393220
  1.6 10.3 %copy-start.1 = (bf16[2,256,128]{2,1,0:T(8,128)(2,1)S(1)}, bf16[2,256,128]{2,1,0:T(8,128)(2,1)}, u32[]{:S(2)}) copy-start(bf16[2,256,128]{2,1,0:T(8,128)(2,1)} %values.1) | copy-start | bytes 393220
  1.6 10.3 %copy-start.2 = (s32[4]{0:T(128)S(1)}, s32[4]{0:T(128)}, u32[]{:S(2)}) copy-start(s32[4]{0:T(128)} %lengths.5) | copy-start | bytes 52
  1.6 10.4 %copy-start.3 = (s32[4]{0:T(128)S(1)}, s32[4]{0:T(128)}, u32[]{:S(2)}) copy-start(s32[4]{0:T(128)} %steps.1) | copy-start | bytes 52
  1.6 21.2 %all-to-all-start = ((bf16[32,8,384]{2,1,0:T(8,128)(2,1)}), bf16[32,8,384]{2,1,0:T(8,128)(2,1)S(1)}, u32[]{:S(2)}, u32[]{:S(2)}) async-start(bf16[32,8,384]{2,1,0:T(8,128)(2,1)} %pad_maximum_fusion), calls=%async_computation | async-start | bytes 393216 | tf_op jit(solution)/shard_map/tokens_to_heads/all_to_all | solution.py:164
  23.6 22.1 %all-to-all-start.1 = ((bf16[4,256,128]{2,1,0:T(8,128)(2,1)}), bf16[4,256,128]{2,1,0:T(8,128)(2,1)S(1)}, u32[]{:S(2)}, u32[]{:S(2)}) async-start(bf16[4,256,128]{2,1,0:T(8,128)(2,1)} %broadcast_in_dim.2), calls=%async_computation.1 | async-start | bytes 524288 | tf_op jit(solution)/shard_map/gather_queries/all_to_all | solution.py:182
  48.3 14.3 %collective-permute-start = (bf16[32,5,2,128]{3,2,1,0:T(2,128)(2,1)S(1)}, bf16[32,5,2,128]{3,2,1,0:T(2,128)(2,1)S(1)}, u32[]{:S(2)}, u32[]{:S(2)}) collective-permute-start(bf16[32,5,2,128]{3,2,1,0:T(2,128)(2,1)S(1)} %get-tuple-element.12), channel_id=1, source_target_pairs={{0,256},{128,384},{256,0},{384,128},{1,257},{129,385},{257,1},{385... | collective-permute-start | bytes 245768 | tf_op jit(solution)/shard_map/attend_and_send/ppermute | solution.py:204
  53.4 9.3 %collective-permute-start.1 = (bf16[32,5,2,128]{3,2,1,0:T(2,128)(2,1)S(1)}, bf16[32,5,2,128]{3,2,1,0:T(2,128)(2,1)S(1)}, u32[]{:S(2)}, u32[]{:S(2)}) collective-permute-start(bf16[32,5,2,128]{3,2,1,0:T(2,128)(2,1)S(1)} %get-tuple-element.13), channel_id=1, source_target_pairs={{0,128},{128,256},{256,384},{384,0},{1,129},{129,257},{257,385},{3... | collective-permute-start | bytes 245768 | tf_op jit(solution)/shard_map/attend_and_send/ppermute | solution.py:204
  56.3 9.1 %collective-permute-start.2 = (bf16[32,5,2,128]{3,2,1,0:T(2,128)(2,1)S(1)}, bf16[32,5,2,128]{3,2,1,0:T(2,128)(2,1)S(1)}, u32[]{:S(2)}, u32[]{:S(2)}) collective-permute-start(bf16[32,5,2,128]{3,2,1,0:T(2,128)(2,1)S(1)} %get-tuple-element.14), channel_id=1, source_target_pairs={{0,384},{128,0},{256,128},{384,256},{1,385},{129,1},{257,129},{385... | collective-permute-start | bytes 245768 | tf_op jit(solution)/shard_map/attend_and_send/ppermute | solution.py:204

commit v11 on v9

--- a/solution.py
+++ b/solution.py
@@ -120,24 +120,24 @@
 
 
 def combine(parts, out):
-    peaks, totals = [], []
-    for s in range(4):
-        stats = parts[pl.ds(s * 32, 32), 4].astype(jnp.float32)
-        peaks.append(stats)
-        totals.append(pltpu.roll(stats, width - 1, 2) + pltpu.roll(stats, width - 2, 2))
-    top = functools.reduce(jnp.maximum, peaks)
-    shares = [t * jnp.exp2(p - top) for t, p in zip(totals, peaks)]
-    scale = 1.0 / functools.reduce(jnp.add, shares)
-    shares = [s * scale for s in shares]
-    joined = []
-    for row in range(4):
-        terms = [
-            parts[pl.ds(s * 32, 32), row].astype(jnp.float32) * shares[s][:, :, 3 * row : 3 * row + 1] for s in range(4)
-        ]
-        joined.append(functools.reduce(jnp.add, terms))
-    joined = jnp.concatenate(joined, axis=1)
-    for h in range(32):
-        out[:, h * width : (h + 1) * width] = joined[h].astype(jnp.bfloat16)
+    lane = lax.broadcasted_iota(jnp.int32, (8, 8, width), 2) - 3 * (lax.broadcasted_iota(jnp.int32, (8, 8, width), 1) // 2)
+    blocks = [parts[pl.ds(s * 320, 320), :].astype(jnp.float32).reshape(8, 40, width) for s in range(4)]
+    for j in range(4):
+        stats = [x[:, 10 * j + 8 : 10 * j + 10] for x in blocks]
+        totals = [pltpu.roll(x, width - 1, 2) + pltpu.roll(x, width - 2, 2) for x in stats]
+        top = functools.reduce(jnp.maximum, stats)
+        shares = [t * jnp.exp2(p - top) for t, p in zip(totals, stats)]
+        scale = 1.0 / functools.reduce(jnp.add, shares)
+        joined = jnp.zeros((8, 8, width), jnp.float32)
+        for x, share in zip(blocks, shares):
+            share = share * scale
+            share = jnp.concatenate([share] * 4, axis=1)
+            share = jnp.sum(jnp.where(lane == 0, share, 0.0), axis=2, keepdims=True)
+            joined += x[:, 10 * j : 10 * j + 8] * share
+        joined = joined.astype(jnp.bfloat16)
+        for g in range(8):
+            h = 4 * g + j
+            out[:, h * width : (h + 1) * width] = joined[g]
 
 
 def on_device(query, key, value, stale_key, stale_value, patch_lengths, stale_step):
@@ -202,7 +202,7 @@
             out_specs=whole_vmem,
             compiler_params=small_kernel,
             name="combine",
-        )(parts)
+        )(parts.reshape(1280, width))
 
 
 def solution(mesh):

time: 80.9 us -> 81.3 us (level)
  no operation moved by 1% of the time
where the time goes in v11:
time: 81.3 us; the launch traced here: 80.9 us
  blocking collectives  49.6 us (61%)
  starting transfers between devices  20.5 us (25%)
  Pallas kernels  5.67 us (7%)
  waiting for transfers between devices  2.71 us (3%)
  other arithmetic  1.6 us (2%)
    all_to_all x1, blocking collectives, on_device(): lax.all_to_all(parts, (quad,) + head, split_axis=0, concat_axis=0, tiled=...  31.2 us
    all_gather x2, blocking collectives, from_neighbours(): return lax.all_gather(x, (pair, core), axis=0, tiled=True)  18.4 us
    all_to_all x1, starting transfers between devices, on_device(): lax.all_to_all(queries, quad, split_axis=0, concat_axis=0, tiled=True)  10.3 us
    all_to_all x1, starting transfers between devices, on_device(): mine = lax.all_to_all(mine, head, split_axis=0, concat_axis=0, tiled=True)  10.2 us
    pallas_call x1, Pallas kernels, on_device(): pl.pallas_call(functools.partial(attend, place=place), out_shape=jax.Shap...  3.71 us
  transfers between devices with their start and end apart: 2, of which 2 were waited for; matrix products, arithmetic and copies ran while one was open for 0% of the time, Pallas kernels for 1%

profile of v11, /device:TPU:16, one launch (start us, length us, event | category | flops | bytes accessed | tf_op | source)
XLA Modules:
  0.0 80.9 jit_solution(3299610397546179950)
XLA Ops:
  0.0 1.6 %pad_maximum_fusion = bf16[32,8,384]{2,1,0:T(8,128)(2,1)} fusion(bf16[32,8,128]{2,1,0:T(8,128)(2,1)} %bitcast.16, bf16[32,8,128]{2,1,0:T(8,128)(2,1)} %bitcast.17, bf16[32,8,128]{2,1,0:T(8,128)(2,1)} %bitcast.18), kind=kLoop, calls=%fused_computation | loop fusion | flops 589824 | bytes 393216 | tf_op jit(solution)/shard_map/tokens_to_heads/concatenate | solution.py:160
  1.6 0.0 copy-start
  1.6 0.0 copy-start.1
  1.6 0.0 copy-start.2
  1.6 0.0 copy-start.3
  1.6 10.2 %all-to-all-start = ((bf16[32,8,384]{2,1,0:T(8,128)(2,1)}), bf16[32,8,384]{2,1,0:T(8,128)(2,1)S(1)}, u32[]{:S(2)}, u32[]{:S(2)}) async-start(bf16[32,8,384]{2,1,0:T(8,128)(2,1)} %pad_maximum_fusion), calls=%async_computation | async-start | bytes 393216 | tf_op jit(solution)/shard_map/tokens_to_heads/all_to_all | solution.py:161
  11.8 0.0 copy-done
  11.8 0.0 copy-done.1
  11.8 0.0 copy-done.2
  11.8 0.0 copy-done.3
  11.9 0.6 pick_stale.1
  12.5 8.1 %all_gather.6.stale = bf16[1024,256]{1,0:T(8,128)(2,1)S(1)} all-gather(bf16[256,256]{1,0:T(8,128)(2,1)S(1)} %pick_stale.1), channel_id=1, replica_groups=mesh['za'=4,'zb'=2,'core'=2,'y'=8,'x'=4] {'zb','core'}, dimensions={0}, use_global_device_ids=true | all-gather | bytes 655360 | tf_op jit(solution)/shard_map/stale/all_gather | solution.py:154
  20.6 1.3 %all-to-all-done = bf16[32,8,384]{2,1,0:T(8,128)(2,1)S(1)} async-done(((bf16[32,8,384]{2,1,0:T(8,128)(2,1)}), bf16[32,8,384]{2,1,0:T(8,128)(2,1)S(1)}, u32[]{:S(2)}, u32[]{:S(2)}) %all-to-all-start) | async-done | bytes 196640 | tf_op jit(solution)/shard_map/tokens_to_heads/all_to_all | solution.py:161
  21.8 0.7 broadcast_in_dim.2
  22.6 10.3 %all-to-all-start.1 = ((bf16[4,256,128]{2,1,0:T(8,128)(2,1)}), bf16[4,256,128]{2,1,0:T(8,128)(2,1)S(1)}, u32[]{:S(2)}, u32[]{:S(2)}) async-start(bf16[4,256,128]{2,1,0:T(8,128)(2,1)} %broadcast_in_dim.2), calls=%async_computation.1 | async-start | bytes 524288 | tf_op jit(solution)/shard_map/gather_queries/all_to_all | solution.py:179
  32.9 10.4 %all_gather.7.fresh = bf16[1024,256]{1,0:T(8,128)(2,1)S(1)} all-gather(bf16[256,256]{1,0:T(8,128)(2,1)S(1)} %slice.7), channel_id=1, replica_groups=mesh['za'=4,'zb'=2,'core'=2,'y'=8,'x'=4] {'zb','core'}, dimensions={0}, use_global_device_ids=true | all-gather | bytes 655360 | tf_op jit(solution)/shard_map/neighbour_keys/all_gather | solution.py:154
  43.3 1.4 %all-to-all-done.1 = bf16[4,256,128]{2,1,0:T(8,128)(2,1)S(1)} async-done(((bf16[4,256,128]{2,1,0:T(8,128)(2,1)}), bf16[4,256,128]{2,1,0:T(8,128)(2,1)S(1)}, u32[]{:S(2)}, u32[]{:S(2)}) %all-to-all-start.1) | async-done | bytes 262176 | tf_op jit(solution)/shard_map/gather_queries/all_to_all | solution.py:179
  44.7 3.7 %attend.1 = bf16[128,5,2,128]{3,2,1,0:T(2,128)(2,1)S(1)} custom-call(s32[4]{0:T(128)S(1)} %copy-done.3, bf16[1024,128]{1,0:T(8,128)(2,1)S(1)} %bitcast.13, bf16[1024,256]{1,0:T(8,128)(2,1)S(1)} %all_gather.7.fresh, bf16[1024,256]{1,0:T(8,128)(2,1)S(1)} %all_gather.6.stale), custom_call_target="tpu_custom_call" | custom-call | flops 1073741824 | bytes 4194304 | tf_op jit(solution)/shard_map/attend/attend/pallas_call | solution.py:186
  48.4 31.2 %all_to_all.15 = bf16[128,5,2,128]{3,2,1,0:T(2,128)(2,1)S(1)} all-to-all(bf16[128,5,2,128]{3,2,1,0:T(2,128)(2,1)S(1)} %attend.1), channel_id=1, replica_groups=mesh['za'=4,'zb'=2,'core'=2,'y'=8,'x'=4] {'za','y','x'}, dimensions={0} | all-to-all | bytes 655360 | tf_op jit(solution)/shard_map/heads_to_tokens/all_to_all | solution.py:197
  79.6 1.3 %combine.1 = bf16[8,4096]{1,0:T(8,128)(2,1)} custom-call(bf16[1280,128]{1,0:T(8,128)(2,1)S(1)} %bitcast.12), custom_call_target="tpu_custom_call" | custom-call | tf_op jit(solution)/shard_map/heads_to_tokens/combine/pallas_call | solution.py:198
  (2 shorter events, 0.0 us)
Async XLA Ops:
  1.6 10.2 %copy-start = (bf16[2,256,128]{2,1,0:T(8,128)(2,1)S(1)}, bf16[2,256,128]{2,1,0:T(8,128)(2,1)}, u32[]{:S(2)}) copy-start(bf16[2,256,128]{2,1,0:T(8,128)(2,1)} %keys.1) | copy-start | bytes 393220
  1.6 10.2 %copy-start.1 = (bf16[2,256,128]{2,1,0:T(8,128)(2,1)S(1)}, bf16[2,256,128]{2,1,0:T(8,128)(2,1)}, u32[]{:S(2)}) copy-start(bf16[2,256,128]{2,1,0:T(8,128)(2,1)} %values.1) | copy-start | bytes 393220
  1.6 10.2 %copy-start.2 = (s32[4]{0:T(128)S(1)}, s32[4]{0:T(128)}, u32[]{:S(2)}) copy-start(s32[4]{0:T(128)} %steps.1) | copy-start | bytes 52
  1.6 10.2 %copy-start.3 = (s32[4]{0:T(128)S(1)}, s32[4]{0:T(128)}, u32[]{:S(2)}) copy-start(s32[4]{0:T(128)} %lengths.3) | copy-start | bytes 52
  1.6 20.2 %all-to-all-start = ((bf16[32,8,384]{2,1,0:T(8,128)(2,1)}), bf16[32,8,384]{2,1,0:T(8,128)(2,1)S(1)}, u32[]{:S(2)}, u32[]{:S(2)}) async-start(bf16[32,8,384]{2,1,0:T(8,128)(2,1)} %pad_maximum_fusion), calls=%async_computation | async-start | bytes 393216 | tf_op jit(solution)/shard_map/tokens_to_heads/all_to_all | solution.py:161
  22.6 22.1 %all-to-all-start.1 = ((bf16[4,256,128]{2,1,0:T(8,128)(2,1)}), bf16[4,256,128]{2,1,0:T(8,128)(2,1)S(1)}, u32[]{:S(2)}, u32[]{:S(2)}) async-start(bf16[4,256,128]{2,1,0:T(8,128)(2,1)} %broadcast_in_dim.2), calls=%async_computation.1 | async-start | bytes 524288 | tf_op jit(solution)/shard_map/gather_queries/all_to_all | solution.py:179

commit v12 on v11

--- a/solution.py
+++ b/solution.py
@@ -65,7 +65,7 @@
     return lax.dot_general(q, keys, (((1,), (1,)), ((), ())), preferred_element_type=jnp.float32)
 
 
-def attend(lengths, queries, fresh, stale, out, *, place):
+def attend(lengths, queries, fresh, stale, out, merged, *, place):
     za, zb, c = place()
     ends = patch_ends(lengths)
     key_first = za * 1024
@@ -82,7 +82,7 @@
         pack(out, at * 32, summed / total, peak, high, total - high)
 
     def one_version(at, rows):
-        q = queries[parts[at], :]
+        q = queries[pl.ds(pl.multiple_of(at * span, span), span), :]
         scores = [products(q, rows[part, :width]) for part in parts]
         peak = row_peak(scores)
         weights = [jnp.exp2(s * log2_scale - peak) for s in scores]
@@ -93,7 +93,7 @@
         finish(at, summed, peak, total)
 
     def both_versions(at, query_first):
-        q = queries[parts[at], :]
+        q = queries[pl.ds(pl.multiple_of(at * span, span), span), :]
         reach = reach_of(query_first + lax.broadcasted_iota(jnp.int32, (span, 1), 0))
         offset = lax.broadcasted_iota(jnp.int32, (span, span), 1)
         scores, fresh_at = [], []
@@ -110,13 +110,37 @@
                 summed += jnp.dot(kept.astype(jnp.bfloat16), version[part, width:], preferred_element_type=jnp.float32)
         finish(at, summed, peak, total)
 
-    for at in range(4):
+    def merge(reach):
+        position = key_first + lax.broadcasted_iota(jnp.int32, (span, 2 * width), 0)
+        for index, part in enumerate(parts):
+            chosen = jnp.where(position + index * span < reach, fresh[part].astype(jnp.float32), stale[part].astype(jnp.float32))
+            merged[part] = chosen.astype(jnp.bfloat16)
+
+    @pl.loop(0, 4)
+    def one_block(at):
         query_first = at * 1024 + zb * 512 + c * span
-        all_fresh = reach_of(query_first) >= key_first + 1024
-        all_stale = reach_of(query_first + span - 1) <= key_first
-        pl.when(all_fresh)(functools.partial(one_version, at, fresh))
-        pl.when(all_stale)(functools.partial(one_version, at, stale))
-        pl.when(jnp.logical_not(jnp.logical_or(all_fresh, all_stale)))(functools.partial(both_versions, at, query_first))
+        least, most = reach_of(query_first), reach_of(query_first + span - 1)
+        all_fresh = least >= key_first + 1024
+        all_stale = most <= key_first
+        some = jnp.logical_not(jnp.logical_or(all_fresh, all_stale))
+        alike = least == most
+
+        @pl.when(all_fresh)
+        def fresh_only():
+            one_version(at, fresh)
+
+        @pl.when(all_stale)
+        def stale_only():
+            one_version(at, stale)
+
+        @pl.when(jnp.logical_and(some, alike))
+        def one_boundary():
+            merge(least)
+            one_version(at, merged)
+
+        @pl.when(jnp.logical_and(some, jnp.logical_not(alike)))
+        def several_boundaries():
+            both_versions(at, query_first)
 
 
 def combine(parts, out):
@@ -188,6 +212,7 @@
             out_shape=jax.ShapeDtypeStruct((128, 5, 2, width), jnp.bfloat16),
             in_specs=[whole_smem] + [whole_vmem] * 3,
             out_specs=whole_vmem,
+            scratch_shapes=[pltpu.VMEM((4 * span, 2 * width), jnp.bfloat16)],
             compiler_params=pltpu.CompilerParams(vmem_limit_bytes=24 << 20),
             cost_estimate=pl.CostEstimate(flops=2 * 2 * 512 * 4096 * 128, bytes_accessed=4 << 20, transcendentals=1 << 20),
             name="attend",

time: 81.3 us -> 80.8 us (level)
  no operation moved by 1% of the time
where the time goes in v12:
time: 80.8 us; the launch traced here: 80.4 us
  blocking collectives  49.3 us (61%)
  starting transfers between devices  20.5 us (25%)
  Pallas kernels  5.5 us (7%)
  waiting for transfers between devices  2.71 us (3%)
  other arithmetic  1.6 us (2%)
    all_to_all x1, blocking collectives, on_device(): lax.all_to_all(parts, (quad,) + head, split_axis=0, concat_axis=0, tiled=...  30.8 us
    all_gather x2, blocking collectives, from_neighbours(): return lax.all_gather(x, (pair, core), axis=0, tiled=True)  18.4 us
    all_to_all x1, starting transfers between devices, on_device(): lax.all_to_all(queries, quad, split_axis=0, concat_axis=0, tiled=True)  10.3 us
    all_to_all x1, starting transfers between devices, on_device(): mine = lax.all_to_all(mine, head, split_axis=0, concat_axis=0, tiled=True)  10.2 us
    pallas_call x1, Pallas kernels, on_device(): pl.pallas_call(functools.partial(attend, place=place), out_shape=jax.Shap...  3.54 us
  transfers between devices with their start and end apart: 2, of which 2 were waited for; matrix products, arithmetic and copies ran while one was open for 0% of the time, Pallas kernels for 1%

profile of v12, /device:TPU:16, one launch (start us, length us, event | category | flops | bytes accessed | tf_op | source)
XLA Modules:
  0.0 80.4 jit_solution(10823087658455920244)
XLA Ops:
  0.0 1.6 %pad_maximum_fusion = bf16[32,8,384]{2,1,0:T(8,128)(2,1)} fusion(bf16[32,8,128]{2,1,0:T(8,128)(2,1)} %bitcast.16, bf16[32,8,128]{2,1,0:T(8,128)(2,1)} %bitcast.17, bf16[32,8,128]{2,1,0:T(8,128)(2,1)} %bitcast.18), kind=kLoop, calls=%fused_computation | loop fusion | flops 589824 | bytes 393216 | tf_op jit(solution)/shard_map/tokens_to_heads/concatenate | solution.py:184
  1.6 0.0 copy-start
  1.6 0.0 copy-start.1
  1.6 0.0 copy-start.2
  1.6 0.0 copy-start.3
  1.6 10.2 %all-to-all-start = ((bf16[32,8,384]{2,1,0:T(8,128)(2,1)}), bf16[32,8,384]{2,1,0:T(8,128)(2,1)S(1)}, u32[]{:S(2)}, u32[]{:S(2)}) async-start(bf16[32,8,384]{2,1,0:T(8,128)(2,1)} %pad_maximum_fusion), calls=%async_computation | async-start | bytes 393216 | tf_op jit(solution)/shard_map/tokens_to_heads/all_to_all | solution.py:185
  11.8 0.0 copy-done
  11.8 0.0 copy-done.1
  11.8 0.0 copy-done.2
  11.8 0.0 copy-done.3
  11.9 0.6 pick_stale.1
  12.5 8.1 %all_gather.6.stale = bf16[1024,256]{1,0:T(8,128)(2,1)S(1)} all-gather(bf16[256,256]{1,0:T(8,128)(2,1)S(1)} %pick_stale.1), channel_id=1, replica_groups=mesh['za'=4,'zb'=2,'core'=2,'y'=8,'x'=4] {'zb','core'}, dimensions={0}, use_global_device_ids=true | all-gather | bytes 655360 | tf_op jit(solution)/shard_map/stale/all_gather | solution.py:178
  20.6 1.3 %all-to-all-done = bf16[32,8,384]{2,1,0:T(8,128)(2,1)S(1)} async-done(((bf16[32,8,384]{2,1,0:T(8,128)(2,1)}), bf16[32,8,384]{2,1,0:T(8,128)(2,1)S(1)}, u32[]{:S(2)}, u32[]{:S(2)}) %all-to-all-start) | async-done | bytes 196640 | tf_op jit(solution)/shard_map/tokens_to_heads/all_to_all | solution.py:185
  21.8 0.7 broadcast_in_dim.2
  22.6 10.3 %all-to-all-start.1 = ((bf16[4,256,128]{2,1,0:T(8,128)(2,1)}), bf16[4,256,128]{2,1,0:T(8,128)(2,1)S(1)}, u32[]{:S(2)}, u32[]{:S(2)}) async-start(bf16[4,256,128]{2,1,0:T(8,128)(2,1)} %broadcast_in_dim.2), calls=%async_computation.1 | async-start | bytes 524288 | tf_op jit(solution)/shard_map/gather_queries/all_to_all | solution.py:203
  32.9 10.4 %all_gather.7.fresh = bf16[1024,256]{1,0:T(8,128)(2,1)S(1)} all-gather(bf16[256,256]{1,0:T(8,128)(2,1)S(1)} %slice.7), channel_id=1, replica_groups=mesh['za'=4,'zb'=2,'core'=2,'y'=8,'x'=4] {'zb','core'}, dimensions={0}, use_global_device_ids=true | all-gather | bytes 655360 | tf_op jit(solution)/shard_map/neighbour_keys/all_gather | solution.py:178
  43.3 1.4 %all-to-all-done.1 = bf16[4,256,128]{2,1,0:T(8,128)(2,1)S(1)} async-done(((bf16[4,256,128]{2,1,0:T(8,128)(2,1)}), bf16[4,256,128]{2,1,0:T(8,128)(2,1)S(1)}, u32[]{:S(2)}, u32[]{:S(2)}) %all-to-all-start.1) | async-done | bytes 262176 | tf_op jit(solution)/shard_map/gather_queries/all_to_all | solution.py:203
  44.7 3.5 %attend.1 = bf16[128,5,2,128]{3,2,1,0:T(2,128)(2,1)S(1)} custom-call(s32[4]{0:T(128)S(1)} %copy-done.3, bf16[1024,128]{1,0:T(8,128)(2,1)S(1)} %bitcast.13, bf16[1024,256]{1,0:T(8,128)(2,1)S(1)} %all_gather.7.fresh, bf16[1024,256]{1,0:T(8,128)(2,1)S(1)} %all_gather.6.stale), custom_call_target="tpu_custom_call" | custom-call | flops 1073741824 | bytes 4194304 | tf_op jit(solution)/shard_map/attend/attend/pallas_call | solution.py:210
  48.3 30.8 %all_to_all.15 = bf16[128,5,2,128]{3,2,1,0:T(2,128)(2,1)S(1)} all-to-all(bf16[128,5,2,128]{3,2,1,0:T(2,128)(2,1)S(1)} %attend.1), channel_id=1, replica_groups=mesh['za'=4,'zb'=2,'core'=2,'y'=8,'x'=4] {'za','y','x'}, dimensions={0} | all-to-all | bytes 655360 | tf_op jit(solution)/shard_map/heads_to_tokens/all_to_all | solution.py:222
  79.1 1.3 %combine.1 = bf16[8,4096]{1,0:T(8,128)(2,1)} custom-call(bf16[1280,128]{1,0:T(8,128)(2,1)S(1)} %bitcast.12), custom_call_target="tpu_custom_call" | custom-call | tf_op jit(solution)/shard_map/heads_to_tokens/combine/pallas_call | solution.py:223
  (2 shorter events, 0.0 us)
Async XLA Ops:
  1.6 10.2 %copy-start = (bf16[2,256,128]{2,1,0:T(8,128)(2,1)S(1)}, bf16[2,256,128]{2,1,0:T(8,128)(2,1)}, u32[]{:S(2)}) copy-start(bf16[2,256,128]{2,1,0:T(8,128)(2,1)} %keys.1) | copy-start | bytes 393220
  1.6 10.2 %copy-start.1 = (bf16[2,256,128]{2,1,0:T(8,128)(2,1)S(1)}, bf16[2,256,128]{2,1,0:T(8,128)(2,1)}, u32[]{:S(2)}) copy-start(bf16[2,256,128]{2,1,0:T(8,128)(2,1)} %values.1) | copy-start | bytes 393220
  1.6 10.2 %copy-start.2 = (s32[4]{0:T(128)S(1)}, s32[4]{0:T(128)}, u32[]{:S(2)}) copy-start(s32[4]{0:T(128)} %steps.1) | copy-start | bytes 52
  1.6 10.2 %copy-start.3 = (s32[4]{0:T(128)S(1)}, s32[4]{0:T(128)}, u32[]{:S(2)}) copy-start(s32[4]{0:T(128)} %lengths.3) | copy-start | bytes 52
  1.6 20.2 %all-to-all-start = ((bf16[32,8,384]{2,1,0:T(8,128)(2,1)}), bf16[32,8,384]{2,1,0:T(8,128)(2,1)S(1)}, u32[]{:S(2)}, u32[]{:S(2)}) async-start(bf16[32,8,384]{2,1,0:T(8,128)(2,1)} %pad_maximum_fusion), calls=%async_computation | async-start | bytes 393216 | tf_op jit(solution)/shard_map/tokens_to_heads/all_to_all | solution.py:185
  22.6 22.1 %all-to-all-start.1 = ((bf16[4,256,128]{2,1,0:T(8,128)(2,1)}), bf16[4,256,128]{2,1,0:T(8,128)(2,1)S(1)}, u32[]{:S(2)}, u32[]{:S(2)}) async-start(bf16[4,256,128]{2,1,0:T(8,128)(2,1)} %broadcast_in_dim.2), calls=%async_computation.1 | async-start | bytes 524288 | tf_op jit(solution)/shard_map/gather_queries/all_to_all | solution.py:203

commit v13 on v12

--- a/solution.py
+++ b/solution.py
@@ -30,16 +30,21 @@
     return ends
 
 
-def pick_stale(lengths, steps, keys, values, out, *, first):
+def prepare(lengths, steps, query, key, value, stale_keys, stale_values, mine, stale, *, place):
+    for at, tokens in enumerate((query, key, value)):
+        for h in range(32):
+            mine[h, :, at * width : (at + 1) * width] = tokens[:, h * width : (h + 1) * width]
+
+    za, zb, c = place()
     ends = patch_ends(lengths)
-    position = first + lax.broadcasted_iota(jnp.int32, (span, width), 0)
+    position = za * 1024 + zb * 512 + c * span + lax.broadcasted_iota(jnp.int32, (span, width), 0)
     step = jnp.full((span, width), steps[0], jnp.int32)
     for m in range(1, patches):
         step = jnp.where(position >= ends[m - 1], steps[m], step)
     older = step == 1
-    for at, cache in enumerate((keys, values)):
-        older_rows, newer_rows = cache[1].astype(jnp.float32), cache[0].astype(jnp.float32)
-        out[:, at * width : (at + 1) * width] = jnp.where(older, older_rows, newer_rows).astype(jnp.bfloat16)
+    for at, cache in enumerate((stale_keys, stale_values)):
+        chosen = jnp.where(older, cache[1].astype(jnp.float32), cache[0].astype(jnp.float32))
+        stale[:, at * width : (at + 1) * width] = chosen.astype(jnp.bfloat16)
 
 
 def pack(out, first, outputs, *stats):
@@ -168,32 +173,26 @@
     def place():
         return lax.axis_index(quad), lax.axis_index(pair), lax.axis_index(core)
 
-    def select(lengths, steps, keys, values, out):
-        za, zb, c = place()
-        pick_stale(lengths, steps, keys, values, out, first=za * 1024 + zb * 512 + c * span)
-
-    swap = [(0, 1), (1, 0)]
-
     def from_neighbours(x):
         return lax.all_gather(x, (pair, core), axis=0, tiled=True)
 
-    def by_head(x):
-        return jnp.transpose(x.reshape(8, 32, width), (1, 0, 2))
+    with jax.named_scope("prepare"):
+        mine, stale_own = pl.pallas_call(
+            functools.partial(prepare, place=place),
+            out_shape=[
+                jax.ShapeDtypeStruct((32, 8, 3 * width), jnp.bfloat16),
+                jax.ShapeDtypeStruct((span, 2 * width), jnp.bfloat16),
+            ],
+            in_specs=[whole_smem] * 2 + [whole_vmem] * 5,
+            out_specs=[whole_vmem] * 2,
+            name="prepare",
+        )(patch_lengths, stale_step, query, key, value, stale_key, stale_value)
 
     with jax.named_scope("tokens_to_heads"):
-        mine = jnp.concatenate([by_head(query), by_head(key), by_head(value)], axis=2)
         mine = lax.all_to_all(mine, head, split_axis=0, concat_axis=0, tiled=True)
         mine = mine.reshape(span, 3 * width)
 
     with jax.named_scope("stale"):
-        stale_own = pl.pallas_call(
-            select,
-            out_shape=jax.ShapeDtypeStruct((span, 2 * width), jnp.bfloat16),
-            in_specs=[whole_smem] * 2 + [whole_vmem] * 2,
-            out_specs=whole_vmem,
-            compiler_params=small_kernel,
-            name="pick_stale",
-        )(patch_lengths, stale_step, stale_key, stale_value)
         stale = from_neighbours(stale_own)
 
     mine, stale = lax.optimization_barrier((mine, stale))

time: 80.8 us -> 81.1 us (level)
  other arithmetic: 1.6 us -> 0 us
  Pallas kernels: 5.5 us -> 6.74 us
    concatenate x1 -> x0, other arithmetic: 1.6 us -> none  [on_device(): jnp.concatenate([by_head(query), by_head(key), by_head(value)], axis=2)]
    pallas_call x1, Pallas kernels: 0.64 us -> 1.87 us  [on_device(): pl.pallas_call(functools.partial(prepare, place=place), out_shape=[jax.Sh...]
  transfers between devices with their start and end apart: 2 -> 2, of which waited for: 2 -> 2; matrix products, arithmetic and copies ran while one was open for 0% -> 0% of each run, Pallas kernels for 1% -> 0%
where the time goes in v13:
time: 81.1 us; the launch traced here: 80.8 us
  blocking collectives  49.4 us (61%)
  starting transfers between devices  20.5 us (25%)
  Pallas kernels  6.74 us (8%)
  waiting for transfers between devices  3.38 us (4%)
    all_to_all x1, blocking collectives, on_device(): lax.all_to_all(parts, (quad,) + head, split_axis=0, concat_axis=0, tiled=...  30.9 us
    all_gather x2, blocking collectives, from_neighbours(): return lax.all_gather(x, (pair, core), axis=0, tiled=True)  18.4 us
    all_to_all x1, starting transfers between devices, on_device(): lax.all_to_all(queries, quad, split_axis=0, concat_axis=0, tiled=True)  10.3 us
    all_to_all x1, starting transfers between devices, on_device(): mine = lax.all_to_all(mine, head, split_axis=0, concat_axis=0, tiled=True)  10.2 us
    pallas_call x1, Pallas kernels, on_device(): pl.pallas_call(functools.partial(attend, place=place), out_shape=jax.Shap...  3.54 us
    all_to_all x1, waiting for transfers between devices, on_device(): mine = lax.all_to_all(mine, head, split_axis=0, concat_axis=0, tiled=True)  1.95 us
    pallas_call x1, Pallas kernels, on_device(): pl.pallas_call(functools.partial(prepare, place=place), out_shape=[jax.Sh...  1.87 us
  transfers between devices with their start and end apart: 2, of which 2 were waited for; matrix products, arithmetic and copies ran while one was open for 0% of the time, Pallas kernels for 0%

profile of v13, /device:TPU:16, one launch (start us, length us, event | category | flops | bytes accessed | tf_op | source)
XLA Modules:
  0.0 80.8 jit_solution(12585926557042855848)
XLA Ops:
  0.0 1.9 %prepare.1 = (bf16[32,8,384]{2,1,0:T(8,128)(2,1)}, bf16[256,256]{1,0:T(8,128)(2,1)}) custom-call(s32[4]{0:T(128)} %lengths.3, s32[4]{0:T(128)} %steps.1, bf16[8,4096]{1,0:T(8,128)(2,1)} %query.1, bf16[8,4096]{1,0:T(8,128)(2,1)} %key.1, bf16[8,4096]{1,0:T(8,128)(2,1)} %value.1, bf16[2,256,128]{2,1,0:T(8,128)(2,1)} %stale_keys.1, bf16[2,256,128]{2,1,0:T(8,128)(2,1)} %stale_values.1), custom_call_target="tpu_custom_call" | custom-call | tf_op jit(solution)/shard_map/prepare/prepare/pallas_call | solution.py:180
  1.9 0.0 copy-start.1
  1.9 10.2 %all-to-all-start = ((bf16[32,8,384]{2,1,0:T(8,128)(2,1)}), bf16[32,8,384]{2,1,0:T(8,128)(2,1)S(1)}, u32[]{:S(2)}, u32[]{:S(2)}) async-start(bf16[32,8,384]{2,1,0:T(8,128)(2,1)} %get-tuple-element.9), calls=%async_computation | async-start | bytes 393216 | tf_op jit(solution)/shard_map/tokens_to_heads/all_to_all | solution.py:192
  12.1 0.0 copy-done.1
  12.1 8.1 %all_gather.6.stale = bf16[1024,256]{1,0:T(8,128)(2,1)S(1)} all-gather(bf16[256,256]{1,0:T(8,128)(2,1)S(1)} %copy-done.1), channel_id=1, replica_groups=mesh['za'=4,'zb'=2,'core'=2,'y'=8,'x'=4] {'zb','core'}, dimensions={0}, use_global_device_ids=true | all-gather | bytes 655360 | tf_op jit(solution)/shard_map/stale/all_gather | solution.py:177
  20.1 2.0 %all-to-all-done = bf16[32,8,384]{2,1,0:T(8,128)(2,1)S(1)} async-done(((bf16[32,8,384]{2,1,0:T(8,128)(2,1)}), bf16[32,8,384]{2,1,0:T(8,128)(2,1)S(1)}, u32[]{:S(2)}, u32[]{:S(2)}) %all-to-all-start) | async-done | bytes 196640 | tf_op jit(solution)/shard_map/tokens_to_heads/all_to_all | solution.py:192
  22.1 0.7 broadcast_in_dim.2
  22.8 10.3 %all-to-all-start.1 = ((bf16[4,256,128]{2,1,0:T(8,128)(2,1)}), bf16[4,256,128]{2,1,0:T(8,128)(2,1)S(1)}, u32[]{:S(2)}, u32[]{:S(2)}) async-start(bf16[4,256,128]{2,1,0:T(8,128)(2,1)} %broadcast_in_dim.2), calls=%async_computation.1 | async-start | bytes 524288 | tf_op jit(solution)/shard_map/gather_queries/all_to_all | solution.py:202
  33.1 10.4 %all_gather.7.fresh = bf16[1024,256]{1,0:T(8,128)(2,1)S(1)} all-gather(bf16[256,256]{1,0:T(8,128)(2,1)S(1)} %slice.7), channel_id=1, replica_groups=mesh['za'=4,'zb'=2,'core'=2,'y'=8,'x'=4] {'zb','core'}, dimensions={0}, use_global_device_ids=true | all-gather | bytes 655360 | tf_op jit(solution)/shard_map/neighbour_keys/all_gather | solution.py:177
  43.5 0.0 copy-start
  43.5 1.4 %all-to-all-done.1 = bf16[4,256,128]{2,1,0:T(8,128)(2,1)S(1)} async-done(((bf16[4,256,128]{2,1,0:T(8,128)(2,1)}), bf16[4,256,128]{2,1,0:T(8,128)(2,1)S(1)}, u32[]{:S(2)}, u32[]{:S(2)}) %all-to-all-start.1) | async-done | bytes 262176 | tf_op jit(solution)/shard_map/gather_queries/all_to_all | solution.py:202
  45.0 0.0 copy-done
  45.0 3.5 %attend.1 = bf16[128,5,2,128]{3,2,1,0:T(2,128)(2,1)S(1)} custom-call(s32[4]{0:T(128)S(1)} %copy-done, bf16[1024,128]{1,0:T(8,128)(2,1)S(1)} %bitcast.4, bf16[1024,256]{1,0:T(8,128)(2,1)S(1)} %all_gather.7.fresh, bf16[1024,256]{1,0:T(8,128)(2,1)S(1)} %all_gather.6.stale), custom_call_target="tpu_custom_call" | custom-call | flops 1073741824 | bytes 4194304 | tf_op jit(solution)/shard_map/attend/attend/pallas_call | solution.py:209
  48.5 30.9 %all_to_all.15 = bf16[128,5,2,128]{3,2,1,0:T(2,128)(2,1)S(1)} all-to-all(bf16[128,5,2,128]{3,2,1,0:T(2,128)(2,1)S(1)} %attend.1), channel_id=1, replica_groups=mesh['za'=4,'zb'=2,'core'=2,'y'=8,'x'=4] {'za','y','x'}, dimensions={0} | all-to-all | bytes 655360 | tf_op jit(solution)/shard_map/heads_to_tokens/all_to_all | solution.py:221
  79.4 1.3 %combine.1 = bf16[8,4096]{1,0:T(8,128)(2,1)} custom-call(bf16[1280,128]{1,0:T(8,128)(2,1)S(1)} %bitcast.3), custom_call_target="tpu_custom_call" | custom-call | tf_op jit(solution)/shard_map/heads_to_tokens/combine/pallas_call | solution.py:222
  (2 shorter events, 0.0 us)
Async XLA Ops:
  1.9 10.2 %copy-start.1 = (bf16[256,256]{1,0:T(8,128)(2,1)S(1)}, bf16[256,256]{1,0:T(8,128)(2,1)}, u32[]{:S(2)}) copy-start(bf16[256,256]{1,0:T(8,128)(2,1)} %get-tuple-element.10) | copy-start | bytes 393220
  1.9 20.2 %all-to-all-start = ((bf16[32,8,384]{2,1,0:T(8,128)(2,1)}), bf16[32,8,384]{2,1,0:T(8,128)(2,1)S(1)}, u32[]{:S(2)}, u32[]{:S(2)}) async-start(bf16[32,8,384]{2,1,0:T(8,128)(2,1)} %get-tuple-element.9), calls=%async_computation | async-start | bytes 393216 | tf_op jit(solution)/shard_map/tokens_to_heads/all_to_all | solution.py:192
  22.8 22.1 %all-to-all-start.1 = ((bf16[4,256,128]{2,1,0:T(8,128)(2,1)}), bf16[4,256,128]{2,1,0:T(8,128)(2,1)S(1)}, u32[]{:S(2)}, u32[]{:S(2)}) async-start(bf16[4,256,128]{2,1,0:T(8,128)(2,1)} %broadcast_in_dim.2), calls=%async_computation.1 | async-start | bytes 524288 | tf_op jit(solution)/shard_map/gather_queries/all_to_all | solution.py:202
  43.5 1.4 %copy-start = (s32[4]{0:T(128)S(1)}, s32[4]{0:T(128)}, u32[]{:S(2)}) copy-start(s32[4]{0:T(128)} %lengths.3) | copy-start | bytes 52

commit v14 on v12

--- a/solution.py
+++ b/solution.py
@@ -113,8 +113,7 @@
     def merge(reach):
         position = key_first + lax.broadcasted_iota(jnp.int32, (span, 2 * width), 0)
         for index, part in enumerate(parts):
-            chosen = jnp.where(position + index * span < reach, fresh[part].astype(jnp.float32), stale[part].astype(jnp.float32))
-            merged[part] = chosen.astype(jnp.bfloat16)
+            merged[part] = jnp.where(position + index * span < reach, fresh[part], stale[part])
 
     @pl.loop(0, 4)
     def one_block(at):

time: 80.8 us -> 81.1 us (level)
  no operation moved by 1% of the time
where the time goes in v14:
time: 81.1 us; the launch traced here: 80.7 us
  blocking collectives  49.6 us (61%)
  starting transfers between devices  20.5 us (25%)
  Pallas kernels  5.44 us (7%)
  waiting for transfers between devices  2.71 us (3%)
  other arithmetic  1.6 us (2%)
    all_to_all x1, blocking collectives, on_device(): lax.all_to_all(parts, (quad,) + head, split_axis=0, concat_axis=0, tiled=...  31.2 us
    all_gather x2, blocking collectives, from_neighbours(): return lax.all_gather(x, (pair, core), axis=0, tiled=True)  18.4 us
    all_to_all x1, starting transfers between devices, on_device(): lax.all_to_all(queries, quad, split_axis=0, concat_axis=0, tiled=True)  10.3 us
    all_to_all x1, starting transfers between devices, on_device(): mine = lax.all_to_all(mine, head, split_axis=0, concat_axis=0, tiled=True)  10.2 us
    pallas_call x1, Pallas kernels, on_device(): pl.pallas_call(functools.partial(attend, place=place), out_shape=jax.Shap...  3.48 us
  transfers between devices with their start and end apart: 2, of which 2 were waited for; matrix products, arithmetic and copies ran while one was open for 0% of the time, Pallas kernels for 1%

profile of v14, /device:TPU:16, one launch (start us, length us, event | category | flops | bytes accessed | tf_op | source)
XLA Modules:
  0.0 80.7 jit_solution(14744092685928398564)
XLA Ops:
  0.0 1.6 %pad_maximum_fusion = bf16[32,8,384]{2,1,0:T(8,128)(2,1)} fusion(bf16[32,8,128]{2,1,0:T(8,128)(2,1)} %bitcast.16, bf16[32,8,128]{2,1,0:T(8,128)(2,1)} %bitcast.17, bf16[32,8,128]{2,1,0:T(8,128)(2,1)} %bitcast.18), kind=kLoop, calls=%fused_computation | loop fusion | flops 589824 | bytes 393216 | tf_op jit(solution)/shard_map/tokens_to_heads/concatenate | solution.py:183
  1.6 0.0 copy-start
  1.6 0.0 copy-start.1
  1.6 0.0 copy-start.2
  1.6 0.0 copy-start.3
  1.6 10.2 %all-to-all-start = ((bf16[32,8,384]{2,1,0:T(8,128)(2,1)}), bf16[32,8,384]{2,1,0:T(8,128)(2,1)S(1)}, u32[]{:S(2)}, u32[]{:S(2)}) async-start(bf16[32,8,384]{2,1,0:T(8,128)(2,1)} %pad_maximum_fusion), calls=%async_computation | async-start | bytes 393216 | tf_op jit(solution)/shard_map/tokens_to_heads/all_to_all | solution.py:184
  11.8 0.0 copy-done
  11.8 0.0 copy-done.1
  11.8 0.0 copy-done.2
  11.8 0.0 copy-done.3
  11.9 0.6 pick_stale.1
  12.5 8.1 %all_gather.6.stale = bf16[1024,256]{1,0:T(8,128)(2,1)S(1)} all-gather(bf16[256,256]{1,0:T(8,128)(2,1)S(1)} %pick_stale.1), channel_id=1, replica_groups=mesh['za'=4,'zb'=2,'core'=2,'y'=8,'x'=4] {'zb','core'}, dimensions={0}, use_global_device_ids=true | all-gather | bytes 655360 | tf_op jit(solution)/shard_map/stale/all_gather | solution.py:177
  20.6 1.3 %all-to-all-done = bf16[32,8,384]{2,1,0:T(8,128)(2,1)S(1)} async-done(((bf16[32,8,384]{2,1,0:T(8,128)(2,1)}), bf16[32,8,384]{2,1,0:T(8,128)(2,1)S(1)}, u32[]{:S(2)}, u32[]{:S(2)}) %all-to-all-start) | async-done | bytes 196640 | tf_op jit(solution)/shard_map/tokens_to_heads/all_to_all | solution.py:184
  21.8 0.7 broadcast_in_dim.2
  22.6 10.3 %all-to-all-start.1 = ((bf16[4,256,128]{2,1,0:T(8,128)(2,1)}), bf16[4,256,128]{2,1,0:T(8,128)(2,1)S(1)}, u32[]{:S(2)}, u32[]{:S(2)}) async-start(bf16[4,256,128]{2,1,0:T(8,128)(2,1)} %broadcast_in_dim.2), calls=%async_computation.1 | async-start | bytes 524288 | tf_op jit(solution)/shard_map/gather_queries/all_to_all | solution.py:202
  32.9 10.4 %all_gather.7.fresh = bf16[1024,256]{1,0:T(8,128)(2,1)S(1)} all-gather(bf16[256,256]{1,0:T(8,128)(2,1)S(1)} %slice.7), channel_id=1, replica_groups=mesh['za'=4,'zb'=2,'core'=2,'y'=8,'x'=4] {'zb','core'}, dimensions={0}, use_global_device_ids=true | all-gather | bytes 655360 | tf_op jit(solution)/shard_map/neighbour_keys/all_gather | solution.py:177
  43.3 1.4 %all-to-all-done.1 = bf16[4,256,128]{2,1,0:T(8,128)(2,1)S(1)} async-done(((bf16[4,256,128]{2,1,0:T(8,128)(2,1)}), bf16[4,256,128]{2,1,0:T(8,128)(2,1)S(1)}, u32[]{:S(2)}, u32[]{:S(2)}) %all-to-all-start.1) | async-done | bytes 262176 | tf_op jit(solution)/shard_map/gather_queries/all_to_all | solution.py:202
  44.7 3.5 %attend.1 = bf16[128,5,2,128]{3,2,1,0:T(2,128)(2,1)S(1)} custom-call(s32[4]{0:T(128)S(1)} %copy-done.3, bf16[1024,128]{1,0:T(8,128)(2,1)S(1)} %bitcast.13, bf16[1024,256]{1,0:T(8,128)(2,1)S(1)} %all_gather.7.fresh, bf16[1024,256]{1,0:T(8,128)(2,1)S(1)} %all_gather.6.stale), custom_call_target="tpu_custom_call" | custom-call | flops 1073741824 | bytes 4194304 | tf_op jit(solution)/shard_map/attend/attend/pallas_call | solution.py:209
  48.2 31.2 %all_to_all.15 = bf16[128,5,2,128]{3,2,1,0:T(2,128)(2,1)S(1)} all-to-all(bf16[128,5,2,128]{3,2,1,0:T(2,128)(2,1)S(1)} %attend.1), channel_id=1, replica_groups=mesh['za'=4,'zb'=2,'core'=2,'y'=8,'x'=4] {'za','y','x'}, dimensions={0} | all-to-all | bytes 655360 | tf_op jit(solution)/shard_map/heads_to_tokens/all_to_all | solution.py:221
  79.4 1.3 %combine.1 = bf16[8,4096]{1,0:T(8,128)(2,1)} custom-call(bf16[1280,128]{1,0:T(8,128)(2,1)S(1)} %bitcast.12), custom_call_target="tpu_custom_call" | custom-call | tf_op jit(solution)/shard_map/heads_to_tokens/combine/pallas_call | solution.py:222
  (2 shorter events, 0.0 us)
Async XLA Ops:
  1.6 10.2 %copy-start = (bf16[2,256,128]{2,1,0:T(8,128)(2,1)S(1)}, bf16[2,256,128]{2,1,0:T(8,128)(2,1)}, u32[]{:S(2)}) copy-start(bf16[2,256,128]{2,1,0:T(8,128)(2,1)} %keys.1) | copy-start | bytes 393220
  1.6 10.2 %copy-start.1 = (bf16[2,256,128]{2,1,0:T(8,128)(2,1)S(1)}, bf16[2,256,128]{2,1,0:T(8,128)(2,1)}, u32[]{:S(2)}) copy-start(bf16[2,256,128]{2,1,0:T(8,128)(2,1)} %values.1) | copy-start | bytes 393220
  1.6 10.2 %copy-start.2 = (s32[4]{0:T(128)S(1)}, s32[4]{0:T(128)}, u32[]{:S(2)}) copy-start(s32[4]{0:T(128)} %steps.1) | copy-start | bytes 52
  1.6 10.2 %copy-start.3 = (s32[4]{0:T(128)S(1)}, s32[4]{0:T(128)}, u32[]{:S(2)}) copy-start(s32[4]{0:T(128)} %lengths.3) | copy-start | bytes 52
  1.6 20.2 %all-to-all-start = ((bf16[32,8,384]{2,1,0:T(8,128)(2,1)}), bf16[32,8,384]{2,1,0:T(8,128)(2,1)S(1)}, u32[]{:S(2)}, u32[]{:S(2)}) async-start(bf16[32,8,384]{2,1,0:T(8,128)(2,1)} %pad_maximum_fusion), calls=%async_computation | async-start | bytes 393216 | tf_op jit(solution)/shard_map/tokens_to_heads/all_to_all | solution.py:184
  22.6 22.1 %all-to-all-start.1 = ((bf16[4,256,128]{2,1,0:T(8,128)(2,1)}), bf16[4,256,128]{2,1,0:T(8,128)(2,1)S(1)}, u32[]{:S(2)}, u32[]{:S(2)}) async-start(bf16[4,256,128]{2,1,0:T(8,128)(2,1)} %broadcast_in_dim.2), calls=%async_computation.1 | async-start | bytes 524288 | tf_op jit(solution)/shard_map/gather_queries/all_to_all | solution.py:202
